TPU v7x, 32 devices: a whole 2x2x4 slice. The times are simulated.
32 devices in a mesh: blk: 4 (over y, x), img: 8 (over z, core).
Axes of the slice: x: 2, y: 2, z: 4, core: 2. Of those that a mesh axis runs over, the one named last changes fastest.
Arguments:
- patch_tokens: bfloat16 [32, 576, 768], P('img', 'blk'), may hold values from -6 to 6
- captions: bfloat16 [400, 768], P('img'), may hold values from -6 to 6
- pair_labels: int32 [32, 400], P('img'), may hold values from 0 to 1, as said below
- master_weights: float32 [768, 12288], P(('blk', 'img')), may hold values from -0.8660254 to 0.8660254
- first_moments: float32 [768, 12288], P(('blk', 'img')), may hold values from -0.00021809896 to 0.00021809896
- second_moments: float32 [768, 12288], P(('blk', 'img')), may hold values from 5.2981906e-11 to 8.477105e-10
- master_vectors: float32 [768, 7], P(('blk', 'img')), may hold values from -6 to 6, as said below
- vector_first: float32 [768, 7], P(('blk', 'img')), may hold values from -0.0017578125 to 0.0017578125
- vector_second: float32 [768, 7], P(('blk', 'img')), may hold values from 3.390842e-09 to 5.4253472e-08
- loss_scalars: float32 [2], replicated, may hold values from -7 to 2.5
- scalar_first: float32 [2], replicated, may hold values from -0.2 to 0.2
- scalar_second: float32 [2], replicated, may hold values from 4.5e-05 to 0.00072
Outputs:
- loss: float32 [], replicated
- grad_norm: float32 [], replicated
- patch_grad: float32 [32, 576, 768], P('img', 'blk')
- new_weights: float32 [768, 12288], P(('blk', 'img'))
- new_first: float32 [768, 12288], P(('blk', 'img'))
- new_second: float32 [768, 12288], P(('blk', 'img'))
- weight_copies: bfloat16 [768, 12288], P(('blk', 'img'))
- new_vectors: float32 [768, 7], P(('blk', 'img'))
- new_vector_first: float32 [768, 7], P(('blk', 'img'))
- new_vector_second: float32 [768, 7], P(('blk', 'img'))
- vector_copies: bfloat16 [768, 7], P(('blk', 'img'))
- new_scalars: float32 [2], replicated
- new_scalar_first: float32 [2], replicated
- new_scalar_second: float32 [2], replicated
Inputs may be any that keep to these rules, and one draw needn't show every extreme that they name: `pair_labels`: 1 marks a matching image and caption; images have uneven numbers of matches. `master_vectors`: gains are positive.
All inputs are finite; a program needn't handle non-finite values.
Results may differ from a plain program's by a relative error of at most 0.015.
Values may be sent and summed in bfloat16 or wider, within the bound.
A program may use at most 256 MiB of HBM per device.

v0:
```python
import jax
import jax.numpy as jnp
from jax import lax
from jax.sharding import PartitionSpec as P

D = 768
HEADS = 12
HEAD_DIM = 64
FF = 3072
STEP = 10


BETA_ONE = 0.9
BETA_TWO = 0.999
EPS_ADAM = 1e-08
CLIP_AT = 1.0


def joined(value, axis, combine):
    everything = jax.tree.map(lambda part: lax.all_gather(part, axis), value)
    leading = jax.tree.map(lambda part: part[0], everything)

    def step(k, so_far):
        return combine(so_far, jax.tree.map(lambda part: part[k], everything))

    return lax.fori_loop(1, lax.axis_size(axis), step, leading)


def layer_norm(values, gain_vec, bias_vec):
    row_mean = jnp.mean(values, axis=-1, keepdims=True)
    centered = values - row_mean
    row_var = jnp.mean(centered * centered, axis=-1, keepdims=True)
    return centered * lax.rsqrt(row_var + 1e-06) * gain_vec + bias_vec


def unit_rows(pooled):
    return pooled * lax.rsqrt(jnp.sum(pooled * pooled, axis=-1, keepdims=True) + 1e-06)


def merge_stats(earlier, later):
    row_max = jnp.maximum(earlier[0], later[0])
    return (
        row_max,
        earlier[1] * jnp.exp(earlier[0] - row_max) + later[1] * jnp.exp(later[0] - row_max),
    )


def attend(queries, keys_all, values_all):
    scale = HEAD_DIM ** (-0.5)
    scores = (
        jnp.einsum("iqhe,ikhe->ihqk", queries, keys_all, preferred_element_type=jnp.float32) * scale
    )
    row_max = jnp.max(scores, axis=-1, keepdims=True)
    expos = jnp.exp(scores - row_max)
    row_sum = jnp.sum(expos, axis=-1, keepdims=True)
    attn_probs = (expos / row_sum).astype(jnp.bfloat16)
    mixed_out = jnp.einsum(
        "ihqk,ikhe->iqhe", attn_probs, values_all, preferred_element_type=jnp.float32
    )
    return (mixed_out.astype(jnp.bfloat16), row_max + jnp.log(row_sum))


def attend_back(queries, keys_all, values_all, log_norm, grad_mixed):
    scale = HEAD_DIM ** (-0.5)
    scores = (
        jnp.einsum("iqhe,ikhe->ihqk", queries, keys_all, preferred_element_type=jnp.float32) * scale
    )
    attn_probs = jnp.exp(scores - log_norm)
    grad_values = jnp.einsum(
        "ihqk,iqhe->ikhe",
        attn_probs.astype(jnp.bfloat16),
        grad_mixed,
        preferred_element_type=jnp.float32,
    )
    grad_probs = jnp.einsum(
        "iqhe,ikhe->ihqk", grad_mixed, values_all, preferred_element_type=jnp.float32
    )
    centre = jnp.sum(attn_probs * grad_probs, axis=-1, keepdims=True)
    grad_scores = (attn_probs * (grad_probs - centre)).astype(jnp.bfloat16)
    grad_queries = (
        jnp.einsum("ihqk,ikhe->iqhe", grad_scores, keys_all, preferred_element_type=jnp.float32)
        * scale
    )
    grad_keys = (
        jnp.einsum("ihqk,iqhe->ikhe", grad_scores, queries, preferred_element_type=jnp.float32)
        * scale
    )
    return (grad_queries, grad_keys, grad_values)


def adamw(parameter, gradient, moment_one, moment_two, step_rate, decay_rate):
    moment_one = BETA_ONE * moment_one + (1.0 - BETA_ONE) * gradient
    moment_two = BETA_TWO * moment_two + (1.0 - BETA_TWO) * gradient * gradient
    first_hat = moment_one / (1.0 - BETA_ONE**STEP)
    second_hat = moment_two / (1.0 - BETA_TWO**STEP)
    updated = parameter - step_rate * (
        first_hat / (jnp.sqrt(second_hat) + EPS_ADAM) + decay_rate * parameter
    )
    return (updated, moment_one, moment_two)


def local(
    patch_tokens,
    captions,
    pair_labels,
    master_weights,
    first_moments,
    second_moments,
    master_vectors,
    vector_first,
    vector_second,
    loss_scalars,
    scalar_first,
    scalar_second,
):
    images = patch_tokens.shape[0]
    length = patch_tokens.shape[1]
    blocks = lax.axis_size("blk")
    all_images = images * lax.axis_size("img")
    scale = HEAD_DIM ** (-0.5)
    own_block = lax.axis_index("blk") == 0
    full_weights, full_vectors = (
        lax.all_gather(master_weights.astype(jnp.bfloat16), ("blk", "img"), axis=0, tiled=True),
        lax.all_gather(master_vectors.astype(jnp.bfloat16), ("blk", "img"), axis=0, tiled=True),
    )
    vectors = full_vectors.astype(jnp.float32)
    w_qkv = full_weights[:, : 3 * D]
    w_out = full_weights[:, 3 * D : 4 * D]
    w_up = full_weights[:, 4 * D : 4 * D + FF]
    w_down = full_weights[:, 4 * D + FF : 4 * D + 2 * FF]
    w_map_q = full_weights[:, 4 * D + 2 * FF : 5 * D + 2 * FF]
    w_map_kv = full_weights[:, 5 * D + 2 * FF : 7 * D + 2 * FF]
    w_map_out = full_weights[:, 7 * D + 2 * FF :]
    tokens = patch_tokens.astype(jnp.float32)
    normed, norm_one_pull = jax.vjp(layer_norm, tokens, vectors[:, 0], vectors[:, 1])
    normed_b = normed.astype(jnp.bfloat16)
    qkv_b = jnp.einsum("ipd,dc->ipc", normed_b, w_qkv, preferred_element_type=jnp.float32).astype(
        jnp.bfloat16
    )
    queries = qkv_b[:, :, :D].reshape(images, length, HEADS, HEAD_DIM)
    kv_full = lax.all_gather(qkv_b[:, :, D:], "blk", axis=1, tiled=True)
    keys_all = kv_full[:, :, :D].reshape(images, length * blocks, HEADS, HEAD_DIM)
    values_all = kv_full[:, :, D:].reshape(images, length * blocks, HEADS, HEAD_DIM)
    mixed_heads, log_norm = attend(queries, keys_all, values_all)
    mixed_b = mixed_heads.reshape(images, length, D)
    residual = tokens + jnp.einsum(
        "ipd,dc->ipc", mixed_b, w_out, preferred_element_type=jnp.float32
    )
    hidden, norm_two_pull = jax.vjp(layer_norm, residual, vectors[:, 2], vectors[:, 3])
    hidden_b = hidden.astype(jnp.bfloat16)
    pre_act = jnp.einsum("ipd,df->ipf", hidden_b, w_up, preferred_element_type=jnp.float32)
    activation, gelu_pull = jax.vjp(jax.nn.gelu, pre_act)
    activation_b = activation.astype(jnp.bfloat16)
    layer_out = residual + jnp.einsum(
        "ipf,df->ipd", activation_b, w_down, preferred_element_type=jnp.float32
    )
    final_norm, norm_three_pull = jax.vjp(layer_norm, layer_out, vectors[:, 4], vectors[:, 5])
    final_b = final_norm.astype(jnp.bfloat16)
    map_kv = jnp.einsum("ipd,dc->ipc", final_b, w_map_kv, preferred_element_type=jnp.float32)
    map_kv = map_kv.astype(jnp.bfloat16).reshape(images, length, 2, HEADS, HEAD_DIM)
    probe_query = jnp.dot(full_vectors[:, 6], w_map_q, preferred_element_type=jnp.float32)
    probe_query = probe_query.astype(jnp.bfloat16).reshape(HEADS, HEAD_DIM)
    pool_scores = (
        jnp.einsum("he,iphe->ihp", probe_query, map_kv[:, :, 0], preferred_element_type=jnp.float32)
        * scale
    )
    local_max = jnp.max(pool_scores, axis=-1)
    local_sum = jnp.sum(jnp.exp(pool_scores - local_max[..., None]), axis=-1)
    row_max, row_sum = joined((local_max, local_sum), "blk", merge_stats)
    pool_probs = jnp.exp(pool_scores - row_max[..., None]) / row_sum[..., None]
    map_values = map_kv[:, :, 1].astype(jnp.float32)
    pooled_part = jnp.einsum(
        "ihp,iphe->ihe", pool_probs, map_values, precision=lax.Precision.HIGHEST
    )
    pooled_heads = lax.psum(pooled_part.reshape(images, D), "blk")
    pooled_heads_b = pooled_heads.astype(jnp.bfloat16)
    pooled = jnp.dot(pooled_heads_b, w_map_out, preferred_element_type=jnp.float32)
    caption_all = lax.all_gather(captions, "img", axis=0, tiled=True).astype(jnp.float32)
    caption_unit = unit_rows(caption_all).astype(jnp.bfloat16)
    unit_image, unit_pull = jax.vjp(unit_rows, pooled)
    cosine = jnp.einsum(
        "id,cd->ic",
        unit_image.astype(jnp.bfloat16),
        caption_unit,
        preferred_element_type=jnp.float32,
    )
    signs = 2.0 * pair_labels.astype(jnp.float32) - 1.0

    def pair_loss(cosine_in, scalars_in):
        logits = jnp.exp(scalars_in[0]) * cosine_in + scalars_in[1]
        return jnp.sum(jax.nn.softplus(-signs * logits)) / all_images

    loss_local, loss_pull = jax.vjp(pair_loss, cosine, loss_scalars)
    grad_cosine, grad_scalars = loss_pull(jnp.ones((), jnp.float32))
    loss_total, scalar_total = lax.psum((loss_local, grad_scalars), "img")
    grad_unit = jnp.einsum(
        "ic,cd->id",
        grad_cosine.astype(jnp.bfloat16),
        caption_unit,
        preferred_element_type=jnp.float32,
    )
    (grad_pooled,) = unit_pull(grad_unit)
    grad_pooled_b = grad_pooled.astype(jnp.bfloat16)
    owned_grad = jnp.where(own_block, grad_pooled_b, jnp.zeros_like(grad_pooled_b))
    grad_w_map_out = jnp.einsum(
        "id,ic->dc", pooled_heads_b, owned_grad, preferred_element_type=jnp.float32
    )
    grad_heads_b = jnp.einsum(
        "ic,dc->id", grad_pooled_b, w_map_out, preferred_element_type=jnp.float32
    )
    grad_heads_b = grad_heads_b.astype(jnp.bfloat16).reshape(images, HEADS, HEAD_DIM)
    grad_heads = grad_heads_b.astype(jnp.float32)
    centre = jnp.sum(grad_heads * pooled_heads.reshape(images, HEADS, HEAD_DIM), axis=-1)
    grad_probs = jnp.einsum(
        "ihe,iphe->ihp", grad_heads_b, map_kv[:, :, 1], preferred_element_type=jnp.float32
    )
    grad_pool_scores = (pool_probs * (grad_probs - centre[..., None])).astype(jnp.bfloat16)
    grad_map_keys = (
        jnp.einsum(
            "ihp,he->iphe", grad_pool_scores, probe_query, preferred_element_type=jnp.float32
        )
        * scale
    )
    grad_map_values = jnp.einsum(
        "ihp,ihe->iphe", pool_probs, grad_heads, precision=lax.Precision.HIGHEST
    )
    grad_probe_query = (
        jnp.einsum(
            "ihp,iphe->he", grad_pool_scores, map_kv[:, :, 0], preferred_element_type=jnp.float32
        ).reshape(D)
        * scale
    )
    grad_map_kv = (
        jnp.stack([grad_map_keys, grad_map_values], axis=2)
        .astype(jnp.bfloat16)
        .reshape(images, length, 2 * D)
    )
    grad_w_map_kv = jnp.einsum(
        "ipd,ipc->dc", final_b, grad_map_kv, preferred_element_type=jnp.float32
    )
    grad_final = jnp.einsum(
        "ipc,dc->ipd", grad_map_kv, w_map_kv, preferred_element_type=jnp.float32
    )
    grad_layer_out, grad_gain_three, grad_bias_three = norm_three_pull(grad_final)
    grad_w_map_q = jnp.outer(vectors[:, 6], grad_probe_query)
    grad_probe = jnp.dot(
        w_map_q.astype(jnp.float32), grad_probe_query, precision=lax.Precision.HIGHEST
    )
    grad_branch_two = grad_layer_out.astype(jnp.bfloat16)
    grad_w_down = jnp.einsum(
        "ipd,ipf->df", grad_branch_two, activation_b, preferred_element_type=jnp.float32
    )
    grad_activation = jnp.einsum(
        "ipd,df->ipf", grad_branch_two, w_down, preferred_element_type=jnp.float32
    )
    (grad_pre,) = gelu_pull(grad_activation)
    grad_pre_b = grad_pre.astype(jnp.bfloat16)
    grad_w_up = jnp.einsum("ipd,ipf->df", hidden_b, grad_pre_b, preferred_element_type=jnp.float32)
    grad_hidden = jnp.einsum("ipf,df->ipd", grad_pre_b, w_up, preferred_element_type=jnp.float32)
    grad_res_part, grad_gain_two, grad_bias_two = norm_two_pull(grad_hidden)
    grad_residual = grad_layer_out + grad_res_part
    grad_tail = jnp.concatenate(
        [grad_w_up, grad_w_down, grad_w_map_q, grad_w_map_kv, grad_w_map_out], axis=1
    )
    grad_branch_one = grad_residual.astype(jnp.bfloat16)
    grad_w_out = jnp.einsum(
        "ipd,ipc->dc", mixed_b, grad_branch_one, preferred_element_type=jnp.float32
    )
    grad_mixed = jnp.einsum(
        "ipc,dc->ipd", grad_branch_one, w_out, preferred_element_type=jnp.float32
    )
    grad_mixed = grad_mixed.astype(jnp.bfloat16)
    grad_queries, grad_keys, grad_values = attend_back(
        queries, keys_all, values_all, log_norm, grad_mixed.reshape(images, length, HEADS, HEAD_DIM)
    )
    grad_keys_own, grad_values_own = (
        lax.psum_scatter(
            grad_keys.reshape(images, length * blocks, D).astype(jnp.bfloat16),
            "blk",
            scatter_dimension=1,
            tiled=True,
        ).astype(jnp.float32),
        lax.psum_scatter(
            grad_values.reshape(images, length * blocks, D).astype(jnp.bfloat16),
            "blk",
            scatter_dimension=1,
            tiled=True,
        ).astype(jnp.float32),
    )
    grad_qkv = jnp.concatenate(
        [grad_queries.reshape(images, length, D), grad_keys_own, grad_values_own], axis=-1
    ).astype(jnp.bfloat16)
    grad_w_qkv = jnp.einsum("ipd,ipc->dc", normed_b, grad_qkv, preferred_element_type=jnp.float32)
    grad_normed = jnp.einsum("ipc,dc->ipd", grad_qkv, w_qkv, preferred_element_type=jnp.float32)
    grad_tok_part, grad_gain_one, grad_bias_one = norm_one_pull(grad_normed)
    patch_grad = grad_residual + grad_tok_part
    grad_front = jnp.concatenate([grad_w_qkv, grad_w_out], axis=1)
    grad_vectors = jnp.stack(
        [
            grad_gain_one,
            grad_bias_one,
            grad_gain_two,
            grad_bias_two,
            grad_gain_three,
            grad_bias_three,
            grad_probe,
        ],
        axis=1,
    )
    grad_weights = jnp.concatenate([grad_front, grad_tail], axis=1)
    weight_share, vector_share = (
        lax.psum_scatter(grad_weights, ("blk", "img"), scatter_dimension=0, tiled=True),
        lax.psum_scatter(grad_vectors, ("blk", "img"), scatter_dimension=0, tiled=True),
    )
    squares = jnp.sum(weight_share * weight_share) + jnp.sum(vector_share * vector_share)
    square_total = lax.psum(squares, ("blk", "img"))
    grad_norm = jnp.sqrt(square_total + jnp.sum(scalar_total * scalar_total))
    factor = CLIP_AT / jnp.maximum(grad_norm, CLIP_AT)
    new_w, new_wm, new_wv = adamw(
        master_weights, weight_share * factor, first_moments, second_moments, 0.03, 0.1
    )
    new_v, new_vm, new_vv = adamw(
        master_vectors, vector_share * factor, vector_first, vector_second, 0.3, 0.0
    )
    new_s, new_sm, new_sv = adamw(
        loss_scalars, scalar_total * factor, scalar_first, scalar_second, 0.3, 0.0
    )
    return (
        loss_total,
        grad_norm,
        patch_grad,
        new_w,
        new_wm,
        new_wv,
        new_w.astype(jnp.bfloat16),
        new_v,
        new_vm,
        new_vv,
        new_v.astype(jnp.bfloat16),
        new_s,
        new_sm,
        new_sv,
    )


def solution(mesh):
    in_specs = (
        P("img", "blk", None),
        P("img", None),
        P("img", None),
        P(("blk", "img"), None),
        P(("blk", "img"), None),
        P(("blk", "img"), None),
        P(("blk", "img"), None),
        P(("blk", "img"), None),
        P(("blk", "img"), None),
        P(),
        P(),
        P(),
    )
    out_specs = (
        P(),
        P(),
        P("img", "blk", None),
        P(("blk", "img"), None),
        P(("blk", "img"), None),
        P(("blk", "img"), None),
        P(("blk", "img"), None),
        P(("blk", "img"), None),
        P(("blk", "img"), None),
        P(("blk", "img"), None),
        P(("blk", "img"), None),
        P(),
        P(),
        P(),
    )
    return jax.shard_map(local, mesh=mesh, in_specs=in_specs, out_specs=out_specs, check_vma=False)
```

profile of v0, /device:TPU:0, one launch (start us, length us, event | category | flops | bytes accessed | tf_op | source)
XLA Modules:
  0.0 945.6 jit_solution(10902879551893291917)
XLA Ops:
  9.6 43.9 %all-gather.2 = bf16[32,24,7]{1,2,0:T(8,128)(2,1)S(1)} all-gather(bf16[1,24,7]{1,2,0:T(8,128)(2,1)S(1)} %convert_bitcast_fusion.1), channel_id=1, replica_groups=mesh['blk'=4,'img'=8] {'blk','img'}, dimensions={0}, use_global_device_ids=true | all-gather | bytes 11088 | tf_op jit(solution)/shard_map/all_gather | solution.py:124
  54.9 84.3 %all-gather.9.cloned.1.call-done = bf16[768,12288]{1,0:T(8,128)(2,1)} async-done(((bf16[24,12288]{1,0:T(8,128)(2,1)}), bf16[768,12288]{1,0:T(8,128)(2,1)}) %all-gather.9.cloned.1.call-update) | async-done | bytes 18874384 | tf_op jit(solution)/shard_map/all_gather | solution.py:123
  148.0 15.7 %all-gather.5 = bf16[8,50,768]{2,1,0:T(8,128)(2,1)S(1)} all-gather(bf16[1,50,768]{2,1,0:T(8,128)(2,1)S(1)} %bitcast.202), channel_id=1, replica_groups=mesh['blk'=4,'img'=8] {'img'}, dimensions={0}, use_global_device_ids=true | all-gather | bytes 691200 | tf_op jit(solution)/shard_map/all_gather | solution.py:178
  169.4 52.3 %all-gather.11.cloned.1.call-done = bf16[4,576,1536]{2,1,0:T(8,128)(2,1)} async-done(((bf16[4,144,1536]{2,1,0:T(8,128)(2,1)}), bf16[4,576,1536]{2,1,0:T(8,128)(2,1)}) %all-gather.11.cloned.1.call-update) | async-done | bytes 7077904 | tf_op jit(solution)/shard_map/all_gather | solution.py:141
  221.7 5.3 fusion.101
  227.0 5.9 copy.59
  237.0 5.4 multiply_reduce_fusion.1
  250.3 8.7 fusion.36
  263.0 5.2 fusion.17
  268.2 9.3 fusion.104
  290.8 8.0 all-gather.4
  299.4 7.1 all-gather.3
  316.7 16.7 %psum.28 = f32[4,768]{1,0:T(4,128)} all-reduce(f32[4,768]{1,0:T(4,128)} %reshape.220), channel_id=1, replica_groups=mesh['blk'=4,'img'=8] {'blk'}, use_global_device_ids=true, to_apply=%region_12.0 | all-reduce | flops 3072 | bytes 24576 | tf_op jit(solution)/shard_map/psum | solution.py:175
  353.5 6.8 multiply_reduce_fusion.2
  362.5 8.5 fusion.15
  371.0 7.5 multiply_reduce_fusion.3
  387.3 9.7 %fusion.25 = bf16[4,12,64,576]{3,2,1,0:T(8,128)(2,1)} fusion(bf16[4,144,12,64]{1,3,2,0:T(8,128)(2,1)} %bitcast.190, f32[4,12,144,576]{3,2,1,0:T(8,128)} %copy-done, f32[4,12,144]{2,1,0:T(8,128)} %log_add_fusion), kind=kOutput, calls=%fused_computation.57 | convolution fusion | flops 523321344 | bytes 20376576 | tf_op jit(solution)/shard_map/ihqk,iqhe->ikhe/dot_general | solution.py:69
  397.0 6.1 copy.65
  403.2 16.0 %multiply_reduce_fusion = (f32[4,12,144]{2,1,0:T(8,128)S(1)}, f32[4,12,144,576]{3,2,1,0:T(8,128)}) fusion(f32[4,12,144,576]{3,2,1,0:T(8,128)} %copy-done, f32[4,12,144]{2,1,0:T(8,128)} %log_add_fusion, bf16[4,144,12,64]{1,3,2,0:T(8,128)(2,1)} %bitcast.191, bf16[4,576,12,64]{1,3,2,0:T(8,128)(2,1)} %bitcast.186), kind=kOutput, calls=%fused_computation.6 | convolution fusion | flops 525526272 | bytes 36329472 | tf_op jit(solution)/shard_map/iqhe,ikhe->ihqk/dot_general | solution.py:75
  419.3 13.2 %multiply_convert_fusion = bf16[4,12,144,576]{3,2,1,0:T(8,128)(2,1)S(1)} fusion(f32[4,12,144,576]{3,2,1,0:T(8,128)} %get-tuple-element.218, f32[4,12,144,576]{3,2,1,0:T(8,128)} %copy-done, f32[4,12,144]{2,1,0:T(8,128)S(1)} %get-tuple-element.217, f32[4,12,144]{2,1,0:T(8,128)S(1)} %copy-done.18), kind=kLoop, calls=%fused_computation.5 | loop fusion | flops 19906560 | bytes 39868416 | tf_op jit(solution)/shard_map/convert_element_type | solution.py:79
  437.1 6.4 copy.64
  447.7 9.6 %multiply_convert_fusion.3 = bf16[4,12,64,144]{3,2,1,0:T(8,128)(2,1)} fusion(bf16[4,576,12,64]{1,3,2,0:T(8,128)(2,1)} %bitcast.185, bf16[4,12,144,576]{3,2,1,0:T(8,128)(2,1)} %copy-done.1), kind=kOutput, calls=%fused_computation.41 | convolution fusion | flops 510492672 | bytes 12386304 | tf_op jit(solution)/shard_map/ihqk,ikhe->iqhe/dot_general | solution.py:81
  459.7 41.0 %reduce-scatter.5.cloned.1.call-done = bf16[4,144,768]{2,1,0:T(8,128)(2,1)} async-done(((bf16[4,576,768]{2,1,0:T(8,128)(2,1)}), bf16[4,144,768]{2,1,0:T(8,128)(2,1)}) %reduce-scatter.5.cloned.1.call-update) | async-done | bytes 884752 | tf_op jit(solution)/shard_map/reduce_scatter | solution.py:277
  500.8 8.2 bitcast_dynamic-update-slice_fusion.2
  511.6 6.8 bitcast_dynamic-update-slice_fusion.1
  518.4 6.6 bitcast_dynamic-update-slice_fusion
  527.2 5.0 bitcast_dynamic-update-slice_fusion.3
  536.9 17.2 %all-reduce.3 = (f32[]{:T(128)}, f32[2]{0:T(128)}) all-reduce(f32[]{:T(128)S(6)} %div.131, f32[2]{0:T(128)} %pad_add_fusion), channel_id=1, replica_groups=mesh['blk'=4,'img'=8] {'img'}, use_global_device_ids=true, to_apply=%region_16.17 | all-reduce | flops 3 | bytes 24 | tf_op jit(solution)/shard_map/psum | solution.py:195
  564.3 5.7 fusion.35
  574.4 37.6 %all-reduce.2 = f32[768,7]{0,1:T(8,128)} all-reduce(f32[768,7]{0,1:T(8,128)} %stack.46), channel_id=7, replica_groups=mesh['blk'=4,'img'=8] {'blk','img'}, use_global_device_ids=true, to_apply=%region_34.35.clone | all-reduce | flops 5376 | bytes 43008
  614.7 268.1 %reduce-scatter.9.cloned.1.call-done = f32[24,12288]{1,0:T(8,128)} async-done(((f32[768,12288]{1,0:T(8,128)}), f32[24,12288]{1,0:T(8,128)}) %reduce-scatter.9.cloned.1.call-update) | async-done | bytes 1179664 | tf_op jit(solution)/shard_map/reduce_scatter | solution.py:312
  889.4 39.4 %psum.30 = f32[]{:T(128)} all-reduce(f32[]{:T(128)S(6)} %add.255), channel_id=1, replica_groups=mesh['blk'=4,'img'=8] {'blk','img'}, use_global_device_ids=true, to_apply=%region_36.37 | all-reduce | flops 1 | bytes 8 | tf_op jit(solution)/shard_map/psum | solution.py:316
  (252 shorter events, 141.1 us)
Async XLA Ops:
  7.2 47.1 %copy-start.6 = (bf16[4,144,768]{2,1,0:T(8,128)(2,1)S(1)}, bf16[4,144,768]{2,1,0:T(8,128)(2,1)}, u32[]{:S(2)}) copy-start(bf16[4,144,768]{2,1,0:T(8,128)(2,1)} %param.14) | copy-start | bytes 2654212
  7.2 132.1 %all-gather.9.cloned.1.call-start = ((), (), s32[]{:S(2)}) async-start(), calls=%async_computation.3 | async-start | bytes 19464192 | tf_op jit(solution)/shard_map/all_gather | solution.py:123
  9.5 212.2 %all-gather.11.cloned.1.call-start = ((), (), s32[]{:S(2)}) async-start(), calls=%async_computation.4 | async-start | bytes 8847360 | tf_op jit(solution)/shard_map/all_gather | solution.py:141
  54.2 89.4 %copy-start.32 = (f32[768]{0:T(1024)}, f32[768]{0:T(1024)S(1)}, u32[]{:S(2)}) copy-start(f32[768]{0:T(1024)S(1)} %get-tuple-element.164) | copy-start | bytes 9220
  54.2 89.4 %copy-start.60 = (f32[768]{0:T(1024)}, f32[768]{0:T(1024)S(1)}, u32[]{:S(2)}) copy-start(f32[768]{0:T(1024)S(1)} %get-tuple-element.163) | copy-start | bytes 9220
  54.5 89.2 %copy-start.26 = (f32[4,144]{1,0:T(4,128)}, f32[4,144]{1,0:T(4,128)S(1)}, u32[]{:S(2)}) copy-start(f32[4,144]{1,0:T(4,128)S(1)} %broadcast_multiply_fusion.2) | copy-start | bytes 6916
  54.9 88.8 %copy-start.39 = (f32[4,144]{1,0:T(4,128)}, f32[4,144]{1,0:T(4,128)S(1)}, u32[]{:S(2)}) copy-start(f32[4,144]{1,0:T(4,128)S(1)} %fusion.34) | copy-start | bytes 6916
  54.9 88.8 %copy-start.34 = (f32[4,144]{1,0:T(4,128)}, f32[4,144]{1,0:T(4,128)S(1)}, u32[]{:S(2)}) copy-start(f32[4,144]{1,0:T(4,128)S(1)} %fusion.77) | copy-start | bytes 6916
  146.7 313.1 %reduce-scatter.7.cloned.1.call-start = ((), (), s32[]{:S(2)}) async-start(), calls=%async_computation.6 | async-start | bytes 4423680 | tf_op jit(solution)/shard_map/reduce_scatter | solution.py:283
  250.3 8.7 copy-start.7
  268.2 9.4 copy-start.63
  268.2 11.1 %copy-start.48 = (f32[768]{0:T(1024)S(1)}, f32[768]{0:T(1024)}, u32[]{:S(2)}) copy-start(f32[768]{0:T(1024)} %get-tuple-element.160) | copy-start | bytes 9220
  268.2 11.1 %copy-start.58 = (f32[768]{0:T(1024)S(1)}, f32[768]{0:T(1024)}, u32[]{:S(2)}) copy-start(f32[768]{0:T(1024)} %get-tuple-element.159) | copy-start | bytes 9220
  277.6 75.8 %copy-start.10 = (f32[4,144,768]{2,1,0:T(8,128)}, f32[4,144,768]{2,1,0:T(8,128)S(1)}, u32[]{:S(2)}) copy-start(f32[4,144,768]{2,1,0:T(8,128)S(1)} %get-tuple-element.210) | copy-start | bytes 5308420
  298.8 8.3 copy-start.30
  352.8 9.7 %slice-start.1 = ((s8[7077888]{0:T(1024)(128)(4,1)}), s8[4194304]{0:T(1024)(128)(4,1)S(1)}, s32[]{:S(2)}) async-start(s8[7077888]{0:T(1024)(128)(4,1)} %bitcast.208), calls=%async_computation.9 | async-start | bytes 8388608
  353.5 9.0 slice-start.2
  362.4 16.8 %copy-start.45 = (f32[4,144]{1,0:T(4,128)}, f32[4,144]{1,0:T(4,128)S(1)}, u32[]{:S(2)}) copy-start(f32[4,144]{1,0:T(4,128)S(1)} %negate_multiply_fusion.2) | copy-start | bytes 6916
  403.2 97.6 %reduce-scatter.5.cloned.1.call-start = ((), (), s32[]{:S(2)}) async-start(), calls=%async_computation.5 | async-start | bytes 4423680 | tf_op jit(solution)/shard_map/reduce_scatter | solution.py:277
  403.2 16.0 %copy-start.18 = (f32[4,12,144]{2,1,0:T(8,128)S(1)}, f32[4,12,144]{2,1,0:T(8,128)}, u32[]{:S(2)}) copy-start(f32[4,12,144]{2,1,0:T(8,128)} %log_add_fusion) | copy-start | bytes 82948
  419.3 13.3 %copy-start.5 = (bf16[4,144,768]{1,2,0:T(8,128)(2,1)S(1)}, bf16[4,144,768]{1,2,0:T(8,128)(2,1)}, u32[]{:S(2)}) copy-start(bf16[4,144,768]{1,2,0:T(8,128)(2,1)} %copy.58) | copy-start | bytes 2654212
  443.5 439.2 %reduce-scatter.9.cloned.1.call-start = ((), (), s32[]{:S(2)}) async-start(), calls=%async_computation.7 | async-start | bytes 38928384 | tf_op jit(solution)/shard_map/reduce_scatter | solution.py:312
  500.8 8.2 copy-start.21
  500.8 8.2 copy-start.62
  509.0 9.4 slice-start.3
  518.4 8.3 copy-start.17
  534.2 19.9 %copy-start.25 = (f32[12,64]{1,0:T(8,128)S(1)}, f32[12,64]{1,0:T(8,128)}, u32[]{:S(2)}) copy-start(f32[12,64]{1,0:T(8,128)} %bitcast_multiply_fusion.2) | copy-start | bytes 9220
  534.2 30.0 %copy-start.8 = (bf16[4,144,768]{2,1,0:T(8,128)(2,1)S(1)}, bf16[4,144,768]{2,1,0:T(8,128)(2,1)}, u32[]{:S(2)}) copy-start(bf16[4,144,768]{2,1,0:T(8,128)(2,1)} %param.14) | copy-start | bytes 2654212
  534.2 30.0 %copy-start.19 = (bf16[4,144,768]{2,1,0:T(8,128)(2,1)S(1)}, bf16[4,144,768]{2,1,0:T(8,128)(2,1)}, u32[]{:S(2)}) copy-start(bf16[4,144,768]{2,1,0:T(8,128)(2,1)} %copy.66) | copy-start | bytes 2654212
  534.2 30.0 %copy-start.27 = (f32[4,144]{1,0:T(4,128)S(1)}, f32[4,144]{1,0:T(4,128)}, u32[]{:S(2)}) copy-start(f32[4,144]{1,0:T(4,128)} %copy-done.26) | copy-start | bytes 6916
  534.2 30.0 %copy-start.33 = (f32[768]{0:T(1024)S(1)}, f32[768]{0:T(1024)}, u32[]{:S(2)}) copy-start(f32[768]{0:T(1024)} %copy-done.32) | copy-start | bytes 9220
  570.0 316.2 %copy-start.3 = (f32[4,144,768]{2,1,0:T(8,128)S(1)}, f32[4,144,768]{2,1,0:T(8,128)}, u32[]{:S(2)}) copy-start(f32[4,144,768]{2,1,0:T(8,128)} %copy-done.2) | copy-start | bytes 5308420
  (42 other events, 143.7 us)
Sparse Core Ops, SparseCore 0:
  11.6 127.5 all-gather.8
  146.8 74.8 all-gather.10
  403.3 47.2 reduce-scatter.6
  453.5 47.2 reduce-scatter.4
  534.4 348.3 reduce-scatter.8
where the time goes:
time: 951 us; the launch traced here: 946 us
  waiting for transfers between devices  446 us (47%)
  blocking collectives  186 us (20%)
  matrix products  163 us (17%)
  local copies, waits for them, and re-layouts  70.5 us (7%)
  other arithmetic  59.3 us (6%)
  between operations  20.8 us (2%)
    reduce_scatter x1, waiting for transfers between devices, local(): lax.psum_scatter(grad_weights, ('blk', 'img'), scatter_dimension=0, tiled...  268 us
    all_gather x1, waiting for transfers between devices, local(): lax.all_gather(master_weights.astype(jnp.bfloat16), ('blk', 'img'), axis=...  84.3 us
    all_gather x1, waiting for transfers between devices, local(): kv_full = lax.all_gather(qkv_b[:, :, D:], 'blk', axis=1, tiled=True)  52.3 us
    all_gather x1, blocking collectives, local(): lax.all_gather(master_vectors.astype(jnp.bfloat16), ('blk', 'img'), axis=...  43.9 us
    reduce_scatter x1, waiting for transfers between devices, local(): lax.psum_scatter(grad_keys.reshape(images, length * blocks, D).astype(jnp...  41 us
    psum x1, blocking collectives, local(): square_total = lax.psum(squares, ('blk', 'img'))  39.4 us
    unnamed x1, blocking collectives  37.6 us
  transfers between devices with their start and end apart: 5, of which 4 were waited for; matrix products, arithmetic and copies ran while one was open for 9% of the time, Pallas kernels for 0%

commit v1 on v0

--- a/solution.py
+++ b/solution.py
@@ -16,16 +16,6 @@
 CLIP_AT = 1.0
 
 
-def joined(value, axis, combine):
-    everything = jax.tree.map(lambda part: lax.all_gather(part, axis), value)
-    leading = jax.tree.map(lambda part: part[0], everything)
-
-    def step(k, so_far):
-        return combine(so_far, jax.tree.map(lambda part: part[k], everything))
-
-    return lax.fori_loop(1, lax.axis_size(axis), step, leading)
-
-
 def layer_norm(values, gain_vec, bias_vec):
     row_mean = jnp.mean(values, axis=-1, keepdims=True)
     centered = values - row_mean
@@ -35,14 +25,6 @@
 
 def unit_rows(pooled):
     return pooled * lax.rsqrt(jnp.sum(pooled * pooled, axis=-1, keepdims=True) + 1e-06)
-
-
-def merge_stats(earlier, later):
-    row_max = jnp.maximum(earlier[0], later[0])
-    return (
-        row_max,
-        earlier[1] * jnp.exp(earlier[0] - row_max) + later[1] * jnp.exp(later[0] - row_max),
-    )
 
 
 def attend(queries, keys_all, values_all):
@@ -113,24 +95,34 @@
     scalar_first,
     scalar_second,
 ):
-    images = patch_tokens.shape[0]
-    length = patch_tokens.shape[1]
     blocks = lax.axis_size("blk")
-    all_images = images * lax.axis_size("img")
+    block = lax.axis_index("blk")
+    all_images = patch_tokens.shape[0] * lax.axis_size("img")
+    images = patch_tokens.shape[0] // blocks
+    length = patch_tokens.shape[1] * blocks
     scale = HEAD_DIM ** (-0.5)
-    own_block = lax.axis_index("blk") == 0
-    full_weights, full_vectors = (
-        lax.all_gather(master_weights.astype(jnp.bfloat16), ("blk", "img"), axis=0, tiled=True),
-        lax.all_gather(master_vectors.astype(jnp.bfloat16), ("blk", "img"), axis=0, tiled=True),
-    )
+    both = ("blk", "img")
+    rows = master_weights.shape[0]
+    first_row = lax.axis_index(both) * rows
+    patch_tokens = lax.all_to_all(patch_tokens, "blk", 0, 1, tiled=True)
+    pair_labels = lax.dynamic_slice_in_dim(pair_labels, block * images, images, 0)
+    rounded = master_weights.astype(jnp.bfloat16)
+    full_vectors = lax.all_gather(master_vectors.astype(jnp.bfloat16), both, axis=0, tiled=True)
     vectors = full_vectors.astype(jnp.float32)
-    w_qkv = full_weights[:, : 3 * D]
-    w_out = full_weights[:, 3 * D : 4 * D]
-    w_up = full_weights[:, 4 * D : 4 * D + FF]
-    w_down = full_weights[:, 4 * D + FF : 4 * D + 2 * FF]
-    w_map_q = full_weights[:, 4 * D + 2 * FF : 5 * D + 2 * FF]
-    w_map_kv = full_weights[:, 5 * D + 2 * FF : 7 * D + 2 * FF]
-    w_map_out = full_weights[:, 7 * D + 2 * FF :]
+
+    def gather(start, stop):
+        return lax.all_gather(rounded[:, start:stop], both, axis=0, tiled=True)
+
+    w_front = gather(0, 4 * D)
+    w_qkv = w_front[:, : 3 * D]
+    w_out = w_front[:, 3 * D :]
+    w_up = gather(4 * D, 4 * D + FF)
+    w_down = gather(4 * D + FF, 4 * D + 2 * FF)
+    own_map_q = rounded[:, 4 * D + 2 * FF : 5 * D + 2 * FF]
+    w_map = gather(5 * D + 2 * FF, 8 * D + 2 * FF)
+    w_map_kv = w_map[:, : 2 * D]
+    w_map_out = w_map[:, 2 * D :]
+    own_vectors = master_vectors.astype(jnp.bfloat16)
     tokens = patch_tokens.astype(jnp.float32)
     normed, norm_one_pull = jax.vjp(layer_norm, tokens, vectors[:, 0], vectors[:, 1])
     normed_b = normed.astype(jnp.bfloat16)
@@ -138,9 +130,8 @@
         jnp.bfloat16
     )
     queries = qkv_b[:, :, :D].reshape(images, length, HEADS, HEAD_DIM)
-    kv_full = lax.all_gather(qkv_b[:, :, D:], "blk", axis=1, tiled=True)
-    keys_all = kv_full[:, :, :D].reshape(images, length * blocks, HEADS, HEAD_DIM)
-    values_all = kv_full[:, :, D:].reshape(images, length * blocks, HEADS, HEAD_DIM)
+    keys_all = qkv_b[:, :, D : 2 * D].reshape(images, length, HEADS, HEAD_DIM)
+    values_all = qkv_b[:, :, 2 * D :].reshape(images, length, HEADS, HEAD_DIM)
     mixed_heads, log_norm = attend(queries, keys_all, values_all)
     mixed_b = mixed_heads.reshape(images, length, D)
     residual = tokens + jnp.einsum(
@@ -158,21 +149,22 @@
     final_b = final_norm.astype(jnp.bfloat16)
     map_kv = jnp.einsum("ipd,dc->ipc", final_b, w_map_kv, preferred_element_type=jnp.float32)
     map_kv = map_kv.astype(jnp.bfloat16).reshape(images, length, 2, HEADS, HEAD_DIM)
-    probe_query = jnp.dot(full_vectors[:, 6], w_map_q, preferred_element_type=jnp.float32)
+    probe_query = lax.psum(
+        jnp.dot(own_vectors[:, 6], own_map_q, preferred_element_type=jnp.float32), both
+    )
     probe_query = probe_query.astype(jnp.bfloat16).reshape(HEADS, HEAD_DIM)
     pool_scores = (
         jnp.einsum("he,iphe->ihp", probe_query, map_kv[:, :, 0], preferred_element_type=jnp.float32)
         * scale
     )
-    local_max = jnp.max(pool_scores, axis=-1)
-    local_sum = jnp.sum(jnp.exp(pool_scores - local_max[..., None]), axis=-1)
-    row_max, row_sum = joined((local_max, local_sum), "blk", merge_stats)
+    row_max = jnp.max(pool_scores, axis=-1)
+    row_sum = jnp.sum(jnp.exp(pool_scores - row_max[..., None]), axis=-1)
     pool_probs = jnp.exp(pool_scores - row_max[..., None]) / row_sum[..., None]
     map_values = map_kv[:, :, 1].astype(jnp.float32)
     pooled_part = jnp.einsum(
         "ihp,iphe->ihe", pool_probs, map_values, precision=lax.Precision.HIGHEST
     )
-    pooled_heads = lax.psum(pooled_part.reshape(images, D), "blk")
+    pooled_heads = pooled_part.reshape(images, D)
     pooled_heads_b = pooled_heads.astype(jnp.bfloat16)
     pooled = jnp.dot(pooled_heads_b, w_map_out, preferred_element_type=jnp.float32)
     caption_all = lax.all_gather(captions, "img", axis=0, tiled=True).astype(jnp.float32)
@@ -192,7 +184,7 @@
 
     loss_local, loss_pull = jax.vjp(pair_loss, cosine, loss_scalars)
     grad_cosine, grad_scalars = loss_pull(jnp.ones((), jnp.float32))
-    loss_total, scalar_total = lax.psum((loss_local, grad_scalars), "img")
+    loss_total, scalar_total = lax.psum((loss_local, grad_scalars), both)
     grad_unit = jnp.einsum(
         "ic,cd->id",
         grad_cosine.astype(jnp.bfloat16),
@@ -201,9 +193,15 @@
     )
     (grad_pooled,) = unit_pull(grad_unit)
     grad_pooled_b = grad_pooled.astype(jnp.bfloat16)
-    owned_grad = jnp.where(own_block, grad_pooled_b, jnp.zeros_like(grad_pooled_b))
-    grad_w_map_out = jnp.einsum(
-        "id,ic->dc", pooled_heads_b, owned_grad, preferred_element_type=jnp.float32
+    pooled_all, grad_pooled_all = (
+        lax.all_gather(pooled_heads_b, both, axis=0, tiled=True),
+        lax.all_gather(grad_pooled_b, both, axis=0, tiled=True),
+    )
+    share_map_out = jnp.einsum(
+        "id,ic->dc",
+        lax.dynamic_slice_in_dim(pooled_all, first_row, rows, 1),
+        grad_pooled_all,
+        preferred_element_type=jnp.float32,
     )
     grad_heads_b = jnp.einsum(
         "ic,dc->id", grad_pooled_b, w_map_out, preferred_element_type=jnp.float32
@@ -242,9 +240,10 @@
         "ipc,dc->ipd", grad_map_kv, w_map_kv, preferred_element_type=jnp.float32
     )
     grad_layer_out, grad_gain_three, grad_bias_three = norm_three_pull(grad_final)
-    grad_w_map_q = jnp.outer(vectors[:, 6], grad_probe_query)
-    grad_probe = jnp.dot(
-        w_map_q.astype(jnp.float32), grad_probe_query, precision=lax.Precision.HIGHEST
+    probe_total = lax.psum(grad_probe_query, both)
+    share_map_q = jnp.outer(own_vectors[:, 6].astype(jnp.float32), probe_total)
+    share_probe = jnp.dot(
+        own_map_q.astype(jnp.float32), probe_total, precision=lax.Precision.HIGHEST
     )
     grad_branch_two = grad_layer_out.astype(jnp.bfloat16)
     grad_w_down = jnp.einsum(
@@ -259,9 +258,6 @@
     grad_hidden = jnp.einsum("ipf,df->ipd", grad_pre_b, w_up, preferred_element_type=jnp.float32)
     grad_res_part, grad_gain_two, grad_bias_two = norm_two_pull(grad_hidden)
     grad_residual = grad_layer_out + grad_res_part
-    grad_tail = jnp.concatenate(
-        [grad_w_up, grad_w_down, grad_w_map_q, grad_w_map_kv, grad_w_map_out], axis=1
-    )
     grad_branch_one = grad_residual.astype(jnp.bfloat16)
     grad_w_out = jnp.einsum(
         "ipd,ipc->dc", mixed_b, grad_branch_one, preferred_element_type=jnp.float32
@@ -273,28 +269,20 @@
     grad_queries, grad_keys, grad_values = attend_back(
         queries, keys_all, values_all, log_norm, grad_mixed.reshape(images, length, HEADS, HEAD_DIM)
     )
-    grad_keys_own, grad_values_own = (
-        lax.psum_scatter(
-            grad_keys.reshape(images, length * blocks, D).astype(jnp.bfloat16),
-            "blk",
-            scatter_dimension=1,
-            tiled=True,
-        ).astype(jnp.float32),
-        lax.psum_scatter(
-            grad_values.reshape(images, length * blocks, D).astype(jnp.bfloat16),
-            "blk",
-            scatter_dimension=1,
-            tiled=True,
-        ).astype(jnp.float32),
-    )
     grad_qkv = jnp.concatenate(
-        [grad_queries.reshape(images, length, D), grad_keys_own, grad_values_own], axis=-1
+        [
+            grad_queries.reshape(images, length, D),
+            grad_keys.reshape(images, length, D),
+            grad_values.reshape(images, length, D),
+        ],
+        axis=-1,
     ).astype(jnp.bfloat16)
     grad_w_qkv = jnp.einsum("ipd,ipc->dc", normed_b, grad_qkv, preferred_element_type=jnp.float32)
     grad_normed = jnp.einsum("ipc,dc->ipd", grad_qkv, w_qkv, preferred_element_type=jnp.float32)
     grad_tok_part, grad_gain_one, grad_bias_one = norm_one_pull(grad_normed)
-    patch_grad = grad_residual + grad_tok_part
-    grad_front = jnp.concatenate([grad_w_qkv, grad_w_out], axis=1)
+    patch_grad = lax.all_to_all(
+        (grad_residual + grad_tok_part).astype(jnp.bfloat16), "blk", 1, 0, tiled=True
+    ).astype(jnp.float32)
     grad_vectors = jnp.stack(
         [
             grad_gain_one,
@@ -303,14 +291,28 @@
             grad_bias_two,
             grad_gain_three,
             grad_bias_three,
-            grad_probe,
         ],
         axis=1,
     )
-    grad_weights = jnp.concatenate([grad_front, grad_tail], axis=1)
-    weight_share, vector_share = (
-        lax.psum_scatter(grad_weights, ("blk", "img"), scatter_dimension=0, tiled=True),
-        lax.psum_scatter(grad_vectors, ("blk", "img"), scatter_dimension=0, tiled=True),
+
+    def scatter(part):
+        return lax.psum_scatter(
+            part.astype(jnp.bfloat16), both, scatter_dimension=0, tiled=True
+        ).astype(jnp.float32)
+
+    share_map_kv = scatter(grad_w_map_kv)
+    share_down = scatter(grad_w_down)
+    share_up = scatter(grad_w_up)
+    share_front = scatter(jnp.concatenate([grad_w_qkv, grad_w_out], axis=1))
+    weight_share = jnp.concatenate(
+        [share_front, share_up, share_down, share_map_q, share_map_kv, share_map_out], axis=1
+    )
+    vector_share = jnp.concatenate(
+        [
+            lax.psum_scatter(grad_vectors, both, scatter_dimension=0, tiled=True),
+            share_probe[:, None],
+        ],
+        axis=1,
     )
     squares = jnp.sum(weight_share * weight_share) + jnp.sum(vector_share * vector_share)
     square_total = lax.psum(squares, ("blk", "img"))

time: 951 us -> 887 us (0.933)
  waiting for transfers between devices: 446 us -> 353 us
  blocking collectives: 186 us -> 264 us
  local copies, waits for them, and re-layouts: 70.5 us -> 30.9 us
  matrix products: 163 us -> 140 us
    all_gather x3, blocking collectives: 59 us -> 123 us  [the longest x1 41.6 us: local(): lax.all_gather(pooled_heads_b, both, axis=0, tiled=True)]
    psum x3, blocking collectives: 73.2 us -> 124 us  [the longest x1 46.7 us: local(): lax.psum(jnp.dot(own_vectors[:, 6], own_map_q, preferred_element_type=jnp...]
    all_gather x2 -> x4, waiting for transfers between devices: 137 us -> 88 us  [gather(): return lax.all_gather(rounded[:, start:stop], both, axis=0, tiled=True)]
    reduce_scatter x3 -> x4, waiting for transfers between devices: 309 us -> 263 us  [scatter(): lax.psum_scatter(part.astype(jnp.bfloat16), both, scatter_dimension=0, ti...]
    unnamed x1 -> x0, blocking collectives: 37.6 us -> none
    slice x7 -> x6, local copies, waits for them, and re-layouts: 18.4 us -> 6.25 us  [the longest x1 2.56 us: local(): values_all = qkv_b[:, :, 2 * D:].reshape(images, length, HEADS, HEAD_DIM)]
    convert_element_type x2 -> x6, local copies, waits for them, and re-layouts: 12.6 us -> 1.67 us  [the longest x1 1.37 us: local(): (grad_residual + grad_tok_part).astype(jnp.bfloat16)]
  transfers between devices with their start and end apart: 5 -> 10, of which waited for: 4 -> 5; matrix products, arithmetic and copies ran while one was open for 9% -> 13% of each run, Pallas kernels for 0% -> 0%
where the time goes in v1:
time: 887 us; the launch traced here: 881 us
  waiting for transfers between devices  353 us (40%)
  blocking collectives  264 us (30%)
  matrix products  140 us (16%)
  other arithmetic  61.8 us (7%)
  local copies, waits for them, and re-layouts  30.9 us (3%)
  between operations  22.8 us (3%)
  starting transfers between devices  9.14 us (1%)
    reduce_scatter x4, waiting for transfers between devices, scatter(): lax.psum_scatter(part.astype(jnp.bfloat16), both, scatter_dimension=0, ti...  263 us
    all_gather x4, waiting for transfers between devices, gather(): return lax.all_gather(rounded[:, start:stop], both, axis=0, tiled=True)  88 us
    psum x1, blocking collectives, local(): lax.psum(jnp.dot(own_vectors[:, 6], own_map_q, preferred_element_type=jnp...  46.7 us
    all_gather x1, blocking collectives, local(): lax.all_gather(pooled_heads_b, both, axis=0, tiled=True)  41.6 us
    all_gather x1, blocking collectives, local(): lax.all_gather(grad_pooled_b, both, axis=0, tiled=True)  40.9 us
    all_gather x1, blocking collectives, local(): lax.all_gather(master_vectors.astype(jnp.bfloat16), both, axis=0, tiled=T...  40.2 us
    psum x1, blocking collectives, local(): loss_total, scalar_total = lax.psum((loss_local, grad_scalars), both)  40 us
    psum x1, blocking collectives, local(): probe_total = lax.psum(grad_probe_query, both)  37.2 us
  transfers between devices with their start and end apart: 10, of which 5 were waited for; matrix products, arithmetic and copies ran while one was open for 13% of the time, Pallas kernels for 0%

profile of v1, /device:TPU:0, one launch (start us, length us, event | category | flops | bytes accessed | tf_op | source)
XLA Modules:
  0.0 881.1 jit_solution(16312426970209934404)
XLA Ops:
  10.9 5.2 all-to-all-start
  17.0 46.7 %psum.35 = bf16[768]{0:T(1024)(128)(2,1)S(1)} all-reduce(f32[768]{0:T(1024)S(1)} %convolution_reduce_fusion), channel_id=1, replica_groups=mesh['blk'=4,'img'=8] {'blk','img'}, use_global_device_ids=true, to_apply=%region_8.0 | all-reduce | flops 768 | bytes 4608 | tf_op jit(solution)/shard_map/psum | solution.py:152
  65.1 40.2 %all-gather.1 = bf16[32,24,7]{1,2,0:T(8,128)(2,1)S(1)} all-gather(bf16[1,24,7]{1,2,0:T(8,128)(2,1)S(1)} %convert_bitcast_fusion), channel_id=1, replica_groups=mesh['blk'=4,'img'=8] {'blk','img'}, dimensions={0}, use_global_device_ids=true | all-gather | bytes 11088 | tf_op jit(solution)/shard_map/all_gather | solution.py:110
  105.7 17.3 %all-gather.2 = bf16[8,50,768]{2,1,0:T(8,128)(2,1)S(1)} all-gather(bf16[1,50,768]{2,1,0:T(8,128)(2,1)S(1)} %bitcast.187), channel_id=1, replica_groups=mesh['blk'=4,'img'=8] {'img'}, dimensions={0}, use_global_device_ids=true | all-gather | bytes 691200 | tf_op jit(solution)/shard_map/all_gather | solution.py:170
  127.4 4.2 fusion.14
  138.3 7.7 multiply_reduce_fusion.1
  146.0 9.1 %fusion = f32[12,576]{1,0:T(8,128)S(1)} fusion(f32[12,576,576]{1,2,0:T(8,128)} %get-tuple-element.64, f32[12,576]{1,0:T(8,128)S(1)} %get-tuple-element.63), kind=kLoop, calls=%fused_computation.5 | loop fusion | flops 11937024 | bytes 15980544 | tf_op jit(solution)/shard_map/reduce_sum | solution.py:37
  155.2 8.3 fusion.23
  166.6 7.9 fusion.74
  174.4 37.7 %all-gather.14.cloned.1.call-done = bf16[768,3072]{1,0:T(8,128)(2,1)} async-done(((bf16[24,3072]{1,0:T(8,128)(2,1)}), bf16[768,3072]{1,0:T(8,128)(2,1)}) %all-gather.14.cloned.1.call-update) | async-done | bytes 4718608 | tf_op jit(solution)/shard_map/all_gather | solution.py:114
  212.2 9.8 %fusion.89 = (f32[576]{0:T(1024)S(1)}, f32[576,768]{1,0:T(8,128)}) fusion(f32[576,768]{1,0:T(8,128)S(1)} %get-tuple-element.66, bf16[768,3072]{1,0:T(8,128)(2,1)} %all-gather.14.cloned.1.call-done, f32[576,3072]{1,0:T(8,128)} %fusion.74), kind=kOutput, calls=%fused_computation.195 | convolution fusion | flops 2734718464 | bytes 15337728 | tf_op jit(solution)/shard_map/ipf,df->ipd/dot_general | solution.py:145
  223.8 50.3 %all-gather.16.cloned.1.call-done = bf16[768,2304]{1,0:T(8,128)(2,1)} async-done(((bf16[24,2304]{1,0:T(8,128)(2,1)}), bf16[768,2304]{1,0:T(8,128)(2,1)}) %all-gather.16.cloned.1.call-update) | async-done | bytes 3538960 | tf_op jit(solution)/shard_map/all_gather | solution.py:114
  274.1 5.1 convolution_convert_fusion.5
  302.2 5.1 multiply_reduce_fusion.3
  309.7 8.5 fusion.13
  330.8 9.3 %fusion.24 = bf16[12,64,576]{2,1,0:T(8,128)(2,1)S(1)} fusion(bf16[576,12,64]{0,2,1:T(8,128)(2,1)S(1)} %bitcast.164, f32[12,576,576]{1,2,0:T(8,128)} %get-tuple-element.64, f32[12,576]{1,0:T(8,128)S(1)} %log_add_fusion), kind=kOutput, calls=%fused_computation.66 | convolution fusion | flops 521994240 | bytes 17722368 | tf_op jit(solution)/shard_map/ihqk,iqhe->ikhe/dot_general | solution.py:51
  340.1 12.0 %multiply_reduce_fusion = (f32[12,576]{1,0:T(8,128)S(1)}, f32[12,576,576]{1,2,0:T(8,128)}) fusion(f32[12,576,576]{1,2,0:T(8,128)} %get-tuple-element.64, f32[12,576]{1,0:T(8,128)S(1)} %log_add_fusion, bf16[576,12,64]{0,2,1:T(8,128)(2,1)S(1)} %bitcast.165, bf16[576,12,64]{0,2,1:T(8,128)(2,1)S(1)} %bitcast.175), kind=kOutput, calls=%fused_computation.1 | convolution fusion | flops 525526272 | bytes 33675264 | tf_op jit(solution)/shard_map/iqhe,ikhe->ihqk/dot_general | solution.py:57
  352.1 12.8 %multiply_convert_fusion = bf16[12,576,576]{1,2,0:T(8,128)(2,1)S(1)} fusion(f32[12,576,576]{1,2,0:T(8,128)} %get-tuple-element.72, f32[12,576,576]{1,2,0:T(8,128)} %get-tuple-element.64, f32[12,576]{1,0:T(8,128)S(1)} %get-tuple-element.71, f32[12,576]{1,0:T(8,128)S(1)} %log_add_fusion), kind=kLoop, calls=%fused_computation | loop fusion | flops 19906560 | bytes 39868416 | tf_op jit(solution)/shard_map/convert_element_type | solution.py:61
  369.3 5.4 convolution_convert_fusion
  377.6 7.8 convolution_convert_fusion.2
  387.0 9.5 %convolution_convert_fusion.1 = bf16[768,3072]{1,0:T(8,128)(2,1)} fusion(f32[576,768]{1,0:T(8,128)S(1)} %copy-done.11, f32[576]{0:T(1024)S(1)} %negate_multiply_fusion.2, f32[576,3072]{1,0:T(8,128)} %fusion.74), kind=kOutput, calls=%fused_computation.23 | convolution fusion | flops 2737078272 | bytes 13568256 | tf_op jit(solution)/shard_map/ipd,ipf->df/dot_general | solution.py:249
  398.3 6.7 multiply_reduce_fusion.2
  407.9 5.3 convolution_convert_fusion.4
  417.7 6.2 reduce.73
  430.5 41.6 %all-gather.3 = bf16[32,1,768]{2,1,0:T(2,128)(2,1)S(1)} all-gather(bf16[1,1,768]{2,1,0:T(2,128)(2,1)S(1)} %reshape.781), channel_id=1, replica_groups=mesh['blk'=4,'img'=8] {'blk','img'}, dimensions={0}, use_global_device_ids=true | all-gather | bytes 50688 | tf_op jit(solution)/shard_map/all_gather | solution.py:197
  472.5 37.2 %all-reduce.4 = (f32[768]{0:T(1024)S(1)}, f32[768,6]{0,1:T(8,128)S(1)}) all-reduce(f32[768]{0:T(1024)S(1)} %mul.640, f32[768,6]{0,1:T(8,128)S(1)} %stack.39), channel_id=1, replica_groups=mesh['blk'=4,'img'=8] {'blk','img'}, use_global_device_ids=true, to_apply=%region_25.26 | all-reduce | flops 5376 | bytes 43008 | tf_op jit(solution)/shard_map/psum | solution.py:243
  512.0 40.9 %all-gather.4 = bf16[32,1,768]{2,1,0:T(2,128)(2,1)S(1)} all-gather(bf16[1,1,768]{2,1,0:T(2,128)(2,1)S(1)} %reshape.783), channel_id=2, replica_groups=mesh['blk'=4,'img'=8] {'blk','img'}, dimensions={0}, use_global_device_ids=true | all-gather | bytes 50688 | tf_op jit(solution)/shard_map/all_gather | solution.py:198
  555.4 49.3 %reduce-scatter.8.cloned.1.call-done = bf16[24,3072]{1,0:T(8,128)(2,1)} async-done(((bf16[768,3072]{1,0:T(8,128)(2,1)}), bf16[24,3072]{1,0:T(8,128)(2,1)}) %reduce-scatter.8.cloned.1.call-update) | async-done | bytes 147472 | tf_op jit(solution)/shard_map/reduce_scatter | solution.py:299
  605.7 110.6 %reduce-scatter.10.cloned.1.call-done = bf16[24,3072]{1,0:T(8,128)(2,1)} async-done(((bf16[768,3072]{1,0:T(8,128)(2,1)}), bf16[24,3072]{1,0:T(8,128)(2,1)}) %reduce-scatter.10.cloned.1.call-update) | async-done | bytes 147472 | tf_op jit(solution)/shard_map/reduce_scatter | solution.py:299
  717.3 103.3 %reduce-scatter.12.cloned.1.call-done = bf16[24,1536]{1,0:T(8,128)(2,1)} async-done(((bf16[768,1536]{1,0:T(8,128)(2,1)}), bf16[24,1536]{1,0:T(8,128)(2,1)}) %reduce-scatter.12.cloned.1.call-update) | async-done | bytes 73744 | tf_op jit(solution)/shard_map/reduce_scatter | solution.py:299
  825.2 40.0 %all-reduce.3 = (f32[]{:T(128)}, f32[]{:T(128)}, f32[2]{0:T(128)S(1)}) all-reduce(f32[]{:T(128)S(6)} %div.136, f32[]{:T(128)S(6)} %add.243, f32[2]{0:T(128)S(1)} %pad_add_fusion), channel_id=1, replica_groups=mesh['blk'=4,'img'=8] {'blk','img'}, use_global_device_ids=true, to_apply=%region_14.15 | all-reduce | flops 4 | bytes 32 | tf_op jit(solution)/shard_map/psum | solution.py:187
  868.4 4.6 fusion.79
  (277 shorter events, 92.7 us)
Async XLA Ops:
  7.2 119.3 %all-gather.10.cloned.1.call-start = ((), (), s32[]{:S(2)}) async-start(), calls=%async_computation.6 | async-start | bytes 4866048 | tf_op jit(solution)/shard_map/all_gather | solution.py:114
  8.6 55.3 %copy-start.15 = (bf16[24,12288]{1,0:T(8,128)(2,1)}, bf16[24,12288]{1,0:T(8,128)(2,1)S(1)}, u32[]{:S(2)}) copy-start(bf16[24,12288]{1,0:T(8,128)(2,1)S(1)} %convert_element_type.229) | copy-start | bytes 1769476
  8.6 55.3 %copy-start.43 = (f32[2]{0:T(128)S(1)}, f32[2]{0:T(128)}, u32[]{:S(2)}) copy-start(f32[2]{0:T(128)} %param.21) | copy-start | bytes 28
  9.4 96.3 %copy-start.27 = (bf16[50,768]{1,0:T(8,128)(2,1)S(1)}, bf16[50,768]{1,0:T(8,128)(2,1)}, u32[]{:S(2)}) copy-start(bf16[50,768]{1,0:T(8,128)(2,1)} %param.13) | copy-start | bytes 230404
  9.4 157.2 %all-gather.12.cloned.1.call-start = ((), (), s32[]{:S(2)}) async-start(), calls=%async_computation.7 | async-start | bytes 4866048 | tf_op jit(solution)/shard_map/all_gather | solution.py:114
  10.1 202.0 %all-gather.14.cloned.1.call-start = ((), (), s32[]{:S(2)}) async-start(), calls=%async_computation.8 | async-start | bytes 4866048 | tf_op jit(solution)/shard_map/all_gather | solution.py:114
  10.9 112.5 %all-to-all-start = ((bf16[4,144,768]{2,1,0:T(8,128)(2,1)}), bf16[4,144,768]{2,1,0:T(8,128)(2,1)S(1)}, u32[]{:S(2)}, u32[]{:S(2)}) async-start(bf16[4,144,768]{2,1,0:T(8,128)(2,1)} %param.12), calls=%async_computation | async-start | bytes 1769472 | tf_op jit(solution)/shard_map/all_to_all | solution.py:107
  16.1 258.1 %all-gather.16.cloned.1.call-start = ((), (), s32[]{:S(2)}) async-start(), calls=%async_computation.9 | async-start | bytes 3649536 | tf_op jit(solution)/shard_map/all_gather | solution.py:114
  16.7 537.8 %reduce-scatter.6.cloned.1.call-start = ((), (), s32[]{:S(2)}) async-start(), calls=%async_computation.10 | async-start | bytes 4866048 | tf_op jit(solution)/shard_map/reduce_scatter | solution.py:299
  16.8 88.8 %copy-start.55 = (bf16[24,7]{0,1:T(8,128)(2,1)}, bf16[24,7]{0,1:T(8,128)(2,1)S(1)}, u32[]{:S(2)}) copy-start(bf16[24,7]{0,1:T(8,128)(2,1)S(1)} %convert_element_type.226) | copy-start | bytes 1012
  123.2 150.9 %copy-start.53 = (f32[768]{0:T(1024)}, f32[768]{0:T(1024)S(1)}, u32[]{:S(2)}) copy-start(f32[768]{0:T(1024)S(1)} %get-tuple-element.24) | copy-start | bytes 9220
  123.2 184.1 %copy-start.39 = (f32[768]{0:T(1024)}, f32[768]{0:T(1024)S(1)}, u32[]{:S(2)}) copy-start(f32[768]{0:T(1024)S(1)} %get-tuple-element.23) | copy-start | bytes 9220
  309.6 13.2 %copy-start.10 = (f32[576,768]{1,0:T(8,128)}, f32[576,768]{1,0:T(8,128)S(1)}, u32[]{:S(2)}) copy-start(f32[576,768]{1,0:T(8,128)S(1)} %get-tuple-element.52) | copy-start | bytes 5308420
  340.0 29.2 %copy-start.23 = (bf16[12,64,576]{2,1,0:T(8,128)(2,1)}, bf16[12,64,576]{2,1,0:T(8,128)(2,1)S(1)}, u32[]{:S(2)}) copy-start(bf16[12,64,576]{2,1,0:T(8,128)(2,1)S(1)} %fusion.24) | copy-start | bytes 2654212
  352.1 12.8 %copy-start.8 = (bf16[1,576,768]{1,2,0:T(8,128)(2,1)S(1)}, bf16[1,576,768]{1,2,0:T(8,128)(2,1)}, u32[]{:S(2)}) copy-start(bf16[1,576,768]{1,2,0:T(8,128)(2,1)} %copy-done.7) | copy-start | bytes 2654212
  377.5 227.2 %reduce-scatter.8.cloned.1.call-start = ((), (), s32[]{:S(2)}) async-start(), calls=%async_computation.11 | async-start | bytes 4866048 | tf_op jit(solution)/shard_map/reduce_scatter | solution.py:299
  385.5 330.8 %reduce-scatter.10.cloned.1.call-start = ((), (), s32[]{:S(2)}) async-start(), calls=%async_computation.12 | async-start | bytes 4866048 | tf_op jit(solution)/shard_map/reduce_scatter | solution.py:299
  396.5 424.1 %reduce-scatter.12.cloned.1.call-start = ((), (), s32[]{:S(2)}) async-start(), calls=%async_computation.13 | async-start | bytes 2433024 | tf_op jit(solution)/shard_map/reduce_scatter | solution.py:299
  423.9 48.4 %copy-start.46 = (f32[768]{0:T(1024)S(1)}, f32[768]{0:T(1024)}, u32[]{:S(2)}) copy-start(f32[768]{0:T(1024)} %get-tuple-element.14) | copy-start | bytes 9220
  423.9 48.4 %copy-start.48 = (f32[768]{0:T(1024)S(1)}, f32[768]{0:T(1024)}, u32[]{:S(2)}) copy-start(f32[768]{0:T(1024)} %get-tuple-element.16) | copy-start | bytes 9220
  424.0 48.4 %copy-start.47 = (f32[768]{0:T(1024)S(1)}, f32[768]{0:T(1024)}, u32[]{:S(2)}) copy-start(f32[768]{0:T(1024)} %get-tuple-element.22) | copy-start | bytes 9220
  424.0 48.4 %copy-start.45 = (f32[768]{0:T(1024)S(1)}, f32[768]{0:T(1024)}, u32[]{:S(2)}) copy-start(f32[768]{0:T(1024)} %get-tuple-element.21) | copy-start | bytes 9220
  424.0 48.4 %copy-start.50 = (f32[768]{0:T(1024)S(1)}, f32[768]{0:T(1024)}, u32[]{:S(2)}) copy-start(f32[768]{0:T(1024)} %get-tuple-element.19) | copy-start | bytes 9220
  424.0 48.4 %copy-start.49 = (f32[768]{0:T(1024)S(1)}, f32[768]{0:T(1024)}, u32[]{:S(2)}) copy-start(f32[768]{0:T(1024)} %get-tuple-element.20) | copy-start | bytes 9220
  425.6 128.1 %all-to-all-start.1 = ((bf16[4,2,55296]{2,1,0:T(2,128)(2,1)}), bf16[4,2,55296]{2,1,0:T(2,128)(2,1)S(1)}, u32[]{:S(2)}, u32[]{:S(2)}) async-start(bf16[4,2,55296]{2,1,0:T(2,128)(2,1)} %reshape.828), calls=%async_computation.5 | async-start | bytes 1769472 | tf_op jit(solution)/shard_map/all_to_all | solution.py:283
  553.6 163.6 %copy-start.56 = (f32[24]{0:T(128)S(1)}, f32[24]{0:T(128)}, u32[]{:S(2)}) copy-start(f32[24]{0:T(128)} %bitcast_convert_fusion.1) | copy-start | bytes 292
  823.8 43.3 %copy-start.44 = (f32[2]{0:T(128)S(1)}, f32[2]{0:T(128)}, u32[]{:S(2)}) copy-start(f32[2]{0:T(128)} %param.21) | copy-start | bytes 28
  823.9 43.3 %copy-start.57 = (f32[2]{0:T(128)S(1)}, f32[2]{0:T(128)}, u32[]{:S(2)}) copy-start(f32[2]{0:T(128)} %param.22) | copy-start | bytes 28
  823.9 43.3 %copy-start.58 = (f32[2]{0:T(128)S(1)}, f32[2]{0:T(128)}, u32[]{:S(2)}) copy-start(f32[2]{0:T(128)} %param.23) | copy-start | bytes 28
  823.9 43.9 %copy-start.33 = (f32[24,7]{0,1:T(8,128)S(1)}, f32[24,7]{0,1:T(8,128)}, u32[]{:S(2)}) copy-start(f32[24,7]{0,1:T(8,128)} %param.18) | copy-start | bytes 2020
  823.9 43.9 %copy-start.51 = (f32[24,7]{0,1:T(8,128)S(1)}, f32[24,7]{0,1:T(8,128)}, u32[]{:S(2)}) copy-start(f32[24,7]{0,1:T(8,128)} %param.19) | copy-start | bytes 2020
  823.9 43.8 %copy-start.52 = (f32[24,7]{0,1:T(8,128)S(1)}, f32[24,7]{0,1:T(8,128)}, u32[]{:S(2)}) copy-start(f32[24,7]{0,1:T(8,128)} %param.20) | copy-start | bytes 2020
  (44 other events, 190.8 us)
Sparse Core Ops, SparseCore 0:
  11.6 69.0 all-gather.9
  83.7 62.8 all-gather.11
  149.6 62.4 all-gather.13
  215.0 59.0 all-gather.15
  377.7 114.6 reduce-scatter.5
  498.6 106.1 reduce-scatter.7
  610.2 106.0 reduce-scatter.9
  722.4 98.1 reduce-scatter.11

commit v2 on v1

--- a/solution.py
+++ b/solution.py
@@ -1,6 +1,8 @@
 import jax
 import jax.numpy as jnp
 from jax import lax
+from jax.experimental import pallas as pl
+from jax.experimental.pallas import tpu as pltpu
 from jax.sharding import PartitionSpec as P
 
 D = 768
@@ -14,6 +16,692 @@
 BETA_TWO = 0.999
 EPS_ADAM = 1e-08
 CLIP_AT = 1.0
+
+GATHER_SKEW = 2
+SCATTER_SKEW = 2
+MESH = pl.DeviceIdType.MESH
+CHIP_ROWS = 48
+GATHER_SECTIONS = ((0, 2560), (2560, 3840), (6400, 3072), (9472, 2304))
+SCATTER_SECTIONS = ((9472, 1536), (6400, 3072), (2560, 3840), (0, 2560))
+GATHER_COLS = 11776
+SCATTER_COLS = 11008
+
+
+def aligned(value, step):
+    return pl.multiple_of(value, step)
+
+
+class Place:
+    def __init__(self):
+        self.blk = lax.axis_index("blk")
+        self.img = lax.axis_index("img")
+        self.x = lax.rem(self.blk, 2)
+        self.y = self.blk // 2
+        self.z = self.img // 2
+        self.c = lax.rem(self.img, 2)
+        self.chip = self.blk * 4 + self.z
+        self.sibling = {"img": self.z * 2 + 1 - self.c}
+        self.up = {"img": self.img + 2}
+        self.down = {"img": self.img - 2}
+        self.a_near = {"blk": self.block(1, 0)}
+        self.b_near = {"blk": self.block(0, 1)}
+
+    def block(self, da, db):
+        flip_x = da * (1 - self.c) + db * self.c
+        flip_y = db * (1 - self.c) + da * self.c
+        other_x = self.x + flip_x * (1 - 2 * self.x)
+        other_y = self.y + flip_y * (1 - 2 * self.y)
+        return other_y * 2 + other_x
+
+
+def remote(src, dst, send_sem, recv_sem, device):
+    return pltpu.make_async_remote_copy(
+        src_ref=src,
+        dst_ref=dst,
+        send_sem=send_sem,
+        recv_sem=recv_sem,
+        device_id=device,
+        device_id_type=MESH,
+    )
+
+
+def greet_all(place):
+    barrier = pltpu.get_barrier_semaphore()
+    me = place.blk * 8 + place.img
+
+    def greet(step, carry):
+        other = lax.rem(me + step, 32)
+        pl.semaphore_signal(
+            barrier,
+            inc=1,
+            device_id={"blk": other // 8, "img": lax.rem(other, 8)},
+            device_id_type=MESH,
+        )
+        return carry
+
+    lax.fori_loop(1, 32, greet, 0)
+    pl.semaphore_wait(barrier, 31)
+
+
+class Gather:
+    def __init__(self, place, buf, rows, first, width, sems):
+        self.p, self.buf, self.rows, self.half = place, buf, rows, width // 2
+        self.mine = aligned(first + place.c * self.half, 128)
+        self.theirs = aligned(first + (1 - place.c) * self.half, 128)
+        self.near_recv, self.z_recv, self.b_recv, self.near_send, self.z_send, self.b_send, self.pair = sems
+
+    def item(self, da, db, level):
+        start = aligned((self.p.block(da, db) * 4 + level) * self.rows, self.rows)
+        return self.buf.at[pl.ds(start, self.rows), pl.ds(self.mine, self.half)]
+
+    def a_copy(self):
+        own = self.item(0, 0, self.p.z)
+        return remote(own, own, self.near_send, self.near_recv, self.p.a_near)
+
+    def z_copy(self, da, level, up):
+        part = self.item(da, 0, level)
+        device = self.p.up if up else self.p.down
+        return remote(part, part, self.z_send.at[up, da, level], self.z_recv.at[da, level], device)
+
+    def b_copy(self, da, level):
+        part = self.item(da, 0, level)
+        return remote(part, part, self.b_send.at[da, level], self.b_recv.at[da, level], self.p.b_near)
+
+    def pair_copy(self, da, db, level):
+        part = self.item(da, db, level)
+        return remote(part, part, self.pair.at[0], self.pair.at[1], self.p.sibling)
+
+    def onward(self, da, level, up, down):
+        self.b_copy(da, level).start()
+        if up:
+            pl.when(self.p.z < 3)(lambda: self.z_copy(da, level, 1).start())
+        if down:
+            pl.when(self.p.z > 0)(lambda: self.z_copy(da, level, 0).start())
+        self.pair_copy(da, 0, level).start()
+
+    def begin(self):
+        self.a_copy().start()
+        self.onward(0, self.p.z, True, True)
+
+    def near(self):
+        part = self.item(1, 0, self.p.z)
+        remote(part, part, self.near_send, self.near_recv, self.p.a_near).wait_recv()
+        self.onward(1, self.p.z, True, True)
+
+    def level(self, distance):
+        z = self.p.z
+
+        @pl.when(z >= distance)
+        def from_below():
+            for da in range(2):
+                self.z_copy(da, z - distance, 1).wait_recv()
+                self.onward(da, z - distance, True, False)
+
+        @pl.when(z + distance <= 3)
+        def from_above():
+            for da in range(2):
+                self.z_copy(da, z + distance, 0).wait_recv()
+                self.onward(da, z + distance, False, True)
+
+    def far(self):
+        for level in range(4):
+            for da in range(2):
+                part = self.item(da, 1, level)
+                remote(
+                    part, part, self.b_send.at[da, level], self.b_recv.at[da, level], self.p.b_near
+                ).wait_recv()
+                self.pair_copy(da, 1, level).start()
+
+    def finish(self):
+        whole = self.buf.at[pl.ds(0, 16 * self.rows), pl.ds(self.theirs, self.half)]
+        both = remote(whole, whole, self.pair.at[0], self.pair.at[1], self.p.sibling)
+        both.wait_recv()
+
+    def sent(self):
+        z = self.p.z
+        self.a_copy().wait_send()
+        whole = self.buf.at[pl.ds(0, 16 * self.rows), pl.ds(self.mine, self.half)]
+        remote(whole, whole, self.pair.at[0], self.pair.at[1], self.p.sibling).wait_send()
+        for level in range(4):
+            for da in range(2):
+                self.b_copy(da, level).wait_send()
+                if level < 3:
+                    pl.when((z >= level) & (z < 3))(
+                        lambda da=da, level=level: self.z_copy(da, level, 1).wait_send()
+                    )
+                if level > 0:
+                    pl.when((z <= level) & (z > 0))(
+                        lambda da=da, level=level: self.z_copy(da, level, 0).wait_send()
+                    )
+
+    def steps(self):
+        return [
+            self.begin,
+            self.near,
+            lambda: self.level(1),
+            lambda: self.level(2),
+            lambda: self.level(3),
+            self.far,
+        ]
+
+
+def gather_sems(count):
+    dma = pltpu.SemaphoreType.DMA
+    return [
+        dma((count,)),
+        dma((count, 2, 4)),
+        dma((count, 2, 4)),
+        dma((count,)),
+        dma((count, 2, 2, 4)),
+        dma((count, 2, 4)),
+        dma((count, 2)),
+    ]
+
+
+class Scatter:
+    def __init__(self, place, buf, share, first, width, bufs, sems):
+        self.p, self.buf, self.share, self.half = place, buf, share, width // 2
+        self.mine = aligned(first + place.c * self.half, 128)
+        self.theirs = aligned(first + (1 - place.c) * self.half, 128)
+        self.pair_in, self.b_in, self.z_in, self.a_in, self.last = bufs
+        self.pair, self.b_sem, self.z_send, self.z_recv, self.a_sem, self.end = sems
+
+    def run_rows(self, da, db):
+        return aligned(self.p.block(da, db) * 192, 192)
+
+    def run(self, da, db):
+        return self.buf.at[pl.ds(self.run_rows(da, db), 192), pl.ds(self.mine, self.half)]
+
+    def level_rows(self, da, level):
+        return aligned((self.p.block(da, 0) * 4 + level) * 48, 48)
+
+    def part(self, da, level):
+        return self.buf.at[pl.ds(self.level_rows(da, level), 48), pl.ds(self.mine, self.half)]
+
+    def add(self, row, source, count, offset=0):
+        def one(step, carry):
+            here = aligned(row + step * 48, 48)
+            there = aligned(offset + step * 48, 48)
+            self.buf[pl.ds(here, 48), pl.ds(self.mine, self.half)] += source[pl.ds(there, 48), :]
+            return carry
+
+        if count == 1:
+            one(0, 0)
+        else:
+            lax.fori_loop(0, count, one, 0)
+
+    def pair_copy(self):
+        return remote(
+            self.buf.at[pl.ds(0, 768), pl.ds(self.theirs, self.half)],
+            self.pair_in,
+            self.pair.at[0],
+            self.pair.at[1],
+            self.p.sibling,
+        )
+
+    def b_copy(self, da):
+        return remote(self.run(da, 1), self.b_in.at[da], self.b_sem.at[0, da], self.b_sem.at[1, da], self.p.b_near)
+
+    def z_copy(self, da, level, up):
+        return remote(
+            self.part(da, level),
+            self.z_in.at[up, da, level - up],
+            self.z_send.at[up, da, level - up],
+            self.z_recv.at[up, da, level - up],
+            self.p.up if up else self.p.down,
+        )
+
+    def a_copy(self):
+        return remote(self.part(1, self.p.z), self.a_in, self.a_sem.at[0], self.a_sem.at[1], self.p.a_near)
+
+    def end_copy(self):
+        return remote(
+            self.last.at[pl.ds(aligned((1 - self.p.c) * 24, 8), 24), :],
+            self.share.at[:, pl.ds(self.mine, self.half)],
+            self.end.at[0],
+            self.end.at[1],
+            self.p.sibling,
+        )
+
+    def begin(self):
+        self.pair_copy().start()
+
+    def pairs_far(self):
+        self.pair_copy().wait_recv()
+        for da in range(2):
+            row = self.run_rows(da, 1)
+            self.add(row, self.pair_in, 4, row)
+            self.b_copy(da).start()
+
+    def pairs_near(self):
+        for da in range(2):
+            row = self.run_rows(da, 0)
+            self.add(row, self.pair_in, 4, row)
+
+    def blocks(self):
+        for da in range(2):
+            self.b_copy(da).wait_recv()
+            self.add(self.run_rows(da, 0), self.b_in.at[da], 4)
+
+    def z_step(self, da, level, up, holds, takes, gives):
+        @pl.when(holds)
+        def step():
+            copy = self.z_copy(da, level, up)
+
+            @pl.when(takes)
+            def take():
+                copy.wait_recv()
+                self.add(self.level_rows(da, level), self.z_in.at[up, da, level - up], 1)
+
+            if gives:
+                copy.start()
+
+    def levels(self, slot):
+        z = self.p.z
+        for da in range(2):
+            self.z_step(
+                da, 3 - slot + z, 1, (z <= slot) & (z >= slot - 2), z >= 1, slot < 3
+            )
+            self.z_step(
+                da, slot - 3 + z, 0, (z >= 3 - slot) & (z <= 5 - slot), z <= 2, slot < 3
+            )
+
+    def across(self):
+        self.a_copy().start()
+
+    def close(self):
+        self.a_copy().wait_recv()
+        rows = self.level_rows(0, self.p.z)
+        self.last[...] = self.buf[pl.ds(rows, 48), pl.ds(self.mine, self.half)].astype(
+            jnp.float32
+        ) + self.a_in[...].astype(jnp.float32)
+        self.end_copy().start()
+        self.share[:, pl.ds(self.mine, self.half)] = self.last[
+            pl.ds(aligned(self.p.c * 24, 8), 24), :
+        ]
+
+    def finish(self):
+        z = self.p.z
+        theirs = self.share.at[:, pl.ds(self.theirs, self.half)]
+        remote(theirs, theirs, self.end.at[0], self.end.at[1], self.p.sibling).wait_recv()
+        self.end_copy().wait_send()
+        self.a_copy().wait_send()
+        self.pair_copy().wait_send()
+        for da in range(2):
+            self.b_copy(da).wait_send()
+            for number in range(3):
+                up, down = self.z_copy(da, 3 - number, 1), self.z_copy(da, number, 0)
+                pl.when(z < 3 - number)(lambda up=up: up.wait_send())
+                pl.when(z > number)(lambda down=down: down.wait_send())
+
+    def steps(self):
+        return [
+            self.begin,
+            self.pairs_far,
+            self.pairs_near,
+            self.blocks,
+            lambda: self.levels(0),
+            lambda: self.levels(1),
+            lambda: self.levels(2),
+            lambda: self.levels(3),
+            self.across,
+            self.close,
+        ]
+
+
+class Swap:
+    def __init__(self, place, own, buf, first_buf_row, rows, first, width, offset, sems):
+        self.p, self.rows, self.half = place, rows, width // 2
+        self.own, self.buf, self.sems, self.offset = own, buf, sems, offset
+        self.mine = aligned(first + place.c * self.half, 128)
+        self.theirs = aligned(first + (1 - place.c) * self.half, 128)
+        self.row = aligned(first_buf_row + place.c * rows, rows)
+        self.other_row = aligned(first_buf_row + (1 - place.c) * rows, rows)
+
+    def columns(self, start):
+        return pl.ds(start, self.half) if self.offset is None else pl.ds(self.offset, self.half)
+
+    def away(self):
+        return remote(
+            self.own.at[:, pl.ds(self.theirs, self.half)],
+            self.buf.at[pl.ds(self.row, self.rows), self.columns(self.theirs)],
+            self.sems.at[0],
+            self.sems.at[1],
+            self.p.sibling,
+        )
+
+    def here(self):
+        return pltpu.make_async_copy(
+            self.own.at[:, pl.ds(self.mine, self.half)],
+            self.buf.at[pl.ds(self.row, self.rows), self.columns(self.mine)],
+            self.sems.at[2],
+        )
+
+    def begin(self):
+        self.away().start()
+        self.here().start()
+
+    def finish(self):
+        landed = self.buf.at[pl.ds(self.other_row, self.rows), self.columns(self.mine)]
+        remote(landed, landed, self.sems.at[0], self.sems.at[1], self.p.sibling).wait_recv()
+        self.here().wait()
+        self.away().wait_send()
+
+
+def gather_kernel(own, tokens, caps, w_out, x, cap_all, w, stage, swap_sems, token_sems, *sems):
+    p = Place()
+    greet_all(p)
+    sections = []
+    swaps = []
+    for number, (first, width) in enumerate(GATHER_SECTIONS):
+        swap = Swap(p, own, stage, 0, 24, first, width, first // 2, swap_sems.at[number])
+        swap.begin()
+        swaps.append(swap)
+        sections.append(
+            Gather(p, w, CHIP_ROWS, first, width, [s.at[number] for s in sems])
+        )
+    count = len(GATHER_SECTIONS)
+    cap_swap = Swap(p, caps, cap_all, p.chip * 32, 16, 0, 768, None, swap_sems.at[count])
+    cap_swap.begin()
+    sections.append(Gather(p, cap_all, 32, 0, 768, [s.at[count] for s in sems]))
+    token_copies = []
+    for step in range(1, 4):
+        to = lax.rem(p.blk + step, 4)
+        copy = remote(
+            tokens.at[to],
+            x.at[pl.ds(aligned(p.blk * 144, 144), 144), :],
+            token_sems.at[0, step - 1],
+            token_sems.at[1, step - 1],
+            {"blk": to},
+        )
+        copy.start()
+        token_copies.append(copy)
+    own_tokens = pltpu.make_async_copy(
+        tokens.at[p.blk], x.at[pl.ds(aligned(p.blk * 144, 144), 144), :], token_sems.at[0, 3]
+    )
+    own_tokens.start()
+
+    def ready(number):
+        swaps[number].finish()
+        first, width = GATHER_SECTIONS[number]
+        w[
+            pl.ds(aligned(p.chip * 48, 48), 48), pl.ds(sections[number].mine, width // 2)
+        ] = stage[:, first // 2 : first // 2 + width // 2].astype(jnp.bfloat16)
+
+    plans = []
+    for number, section in enumerate(sections):
+        steps = section.steps()
+        if number < count:
+            steps[0] = lambda number=number, begin=steps[0]: (ready(number), begin())
+        else:
+            steps[0] = lambda begin=steps[0]: (cap_swap.finish(), begin())
+        plans.append(steps)
+    skew = GATHER_SKEW
+    last = max(len(s) + skew * n for n, s in enumerate(plans))
+    outs = []
+    for tick in range(last + 1):
+        for number, steps in enumerate(plans):
+            at = tick - skew * number
+            if 0 <= at < len(steps):
+                steps[at]()
+    for number, section in enumerate(sections):
+        section.finish()
+        if number < count:
+            first, width = GATHER_SECTIONS[number]
+            out = pltpu.make_async_copy(
+                w.at[:, first : first + width],
+                w_out.at[:, first : first + width],
+                swap_sems.at[number, 3],
+            )
+            out.start()
+            outs.append(out)
+    for step, copy in enumerate(token_copies):
+        source = lax.rem(p.blk + 3 - step, 4)
+        landed = x.at[pl.ds(aligned(source * 144, 144), 144), :]
+        remote(
+            landed, landed, token_sems.at[0, step], token_sems.at[1, step], {"blk": source}
+        ).wait_recv()
+        copy.wait_send()
+    own_tokens.wait()
+    for section in sections:
+        section.sent()
+    for out in outs:
+        out.wait()
+
+
+def gather_call(own, tokens, caps):
+    count = len(GATHER_SECTIONS) + 1
+    dma = pltpu.SemaphoreType.DMA
+    return pl.pallas_call(
+        gather_kernel,
+        out_shape=(
+            jax.ShapeDtypeStruct((768, GATHER_COLS), jnp.bfloat16),
+            jax.ShapeDtypeStruct((576, 768), jnp.bfloat16),
+            jax.ShapeDtypeStruct((512, 768), jnp.bfloat16),
+        ),
+        in_specs=[
+            pl.BlockSpec(memory_space=pl.ANY),
+            pl.BlockSpec(memory_space=pl.ANY),
+            pl.BlockSpec(memory_space=pltpu.VMEM),
+        ],
+        out_specs=(
+            pl.BlockSpec(memory_space=pl.ANY),
+            pl.BlockSpec(memory_space=pltpu.VMEM),
+            pl.BlockSpec(memory_space=pltpu.VMEM),
+        ),
+        scratch_shapes=[
+            pltpu.VMEM((768, GATHER_COLS), jnp.bfloat16),
+            pltpu.VMEM((48, GATHER_COLS // 2), jnp.float32),
+            dma((count, 4)),
+            dma((2, 4)),
+            *gather_sems(count),
+        ],
+        compiler_params=pltpu.CompilerParams(
+            collective_id=0, has_side_effects=True, vmem_limit_bytes=60 * 2**20
+        ),
+        name="gather_weights",
+    )(own, tokens, caps)
+
+
+class Spread:
+    def __init__(self, place, mine, everyone, send_sem, recv_sem):
+        self.p, self.mine, self.everyone = place, mine, everyone
+        self.send_sem, self.recv_sem = send_sem, recv_sem
+        self.me = place.blk * 8 + place.img
+
+    def copy(self, step):
+        other = lax.rem(self.me + step, 32)
+        return remote(
+            self.mine,
+            self.everyone.at[step - 1],
+            self.send_sem,
+            self.recv_sem,
+            {"blk": other // 8, "img": lax.rem(other, 8)},
+        )
+
+    def begin(self, tile):
+        self.mine[...] = tile
+
+        def start(step, carry):
+            self.copy(step).start()
+            return carry
+
+        lax.fori_loop(1, 32, start, 0)
+
+    def total(self):
+        remote(
+            self.everyone, self.everyone, self.send_sem, self.recv_sem, self.p.sibling
+        ).wait()
+        return self.mine[...] + jnp.sum(self.everyone[...], axis=0)
+
+
+def small_tail(p, small, map_q, probe, share, spread):
+    everything = small[...]
+    as_rows = everything.astype(jnp.bfloat16)
+    sums = jnp.sum(everything.reshape(32, 8, 768), axis=0)
+    query, scalars = sums[2:3], sums[3:4]
+    device = lax.broadcasted_iota(jnp.int32, (32, 256), 0) * 8
+    row = lax.broadcasted_iota(jnp.int32, (32, 256), 1)
+
+    def rows_of(kind):
+        pick = (row == device + kind).astype(jnp.float32).astype(jnp.bfloat16)
+        return jnp.dot(pick, as_rows, preferred_element_type=jnp.float32).astype(jnp.bfloat16)
+
+    pooled, grads = rows_of(0), rows_of(1)
+    first = (p.blk * 8 + p.img) * 24
+    picks = (
+        lax.broadcasted_iota(jnp.int32, (24, 768), 1)
+        == lax.broadcasted_iota(jnp.int32, (24, 768), 0) + first
+    ).astype(jnp.float32).astype(jnp.bfloat16)
+    rows = lax.dot_general(
+        picks, pooled, (((1,), (1,)), ((), ())), preferred_element_type=jnp.float32
+    ).astype(jnp.bfloat16)
+    map_out = jnp.dot(rows, grads, preferred_element_type=jnp.float32)
+    map_q_share = probe * query
+    probe_share = jnp.sum(map_q * query, axis=1, keepdims=True)
+    square = (
+        jnp.sum(map_out * map_out)
+        + jnp.sum(map_q_share * map_q_share)
+        + jnp.sum(probe_share * probe_share)
+    )
+
+    def one(step, total):
+        part = share[:, pl.ds(aligned(step * 256, 256), 256)]
+        return total + jnp.sum(part * part)
+
+    square = lax.fori_loop(0, SCATTER_COLS // 256, one, square)
+    spread.begin(jnp.full((8, 128), square, jnp.float32))
+    total = spread.total()
+    one_lane = lax.broadcasted_iota(jnp.int32, (1, 768), 1)
+    scalar_square = jnp.sum(
+        jnp.where((one_lane == 1) | (one_lane == 2), scalars * scalars, 0.0)
+    )
+    norm = jnp.sqrt(total + scalar_square)
+    return map_out, map_q_share, probe_share, scalars, norm
+
+
+def scatter_kernel(
+    grads, small_own, map_q, probe, patch, share, map_out, map_q_share, probe_share, facts, patch_out,
+    w, small, pair_in, b_in, z_in, a_in, last, mine, everyone,
+    load_sems, swap_sems, patch_sems, send_sem, recv_sem, *sems,
+):
+    p = Place()
+    loads = []
+    for number, (first, width) in enumerate(SCATTER_SECTIONS):
+        load = pltpu.make_async_copy(
+            grads.at[:, first : first + width], w.at[:, first : first + width], load_sems.at[number]
+        )
+        load.start()
+        loads.append(load)
+    greet_all(p)
+    gather, sems = sems[:7], sems[7:]
+    swap = Swap(p, small_own, small, p.chip * 16, 8, 0, 768, None, swap_sems)
+    swap.begin()
+    small_gather = Gather(p, small, 16, 0, 768, [s.at[0] for s in gather])
+    patch_copies = []
+    for step in range(1, 4):
+        to = lax.rem(p.blk + step, 4)
+        copy = remote(
+            patch.at[pl.ds(aligned(to * 144, 144), 144), :],
+            patch_out.at[p.blk],
+            patch_sems.at[0, step - 1],
+            patch_sems.at[1, step - 1],
+            {"blk": to},
+        )
+        copy.start()
+        patch_copies.append(copy)
+    own_patch = pltpu.make_async_copy(
+        patch.at[pl.ds(aligned(p.blk * 144, 144), 144), :], patch_out.at[p.blk], patch_sems.at[0, 3]
+    )
+    own_patch.start()
+    plans = []
+    sections = []
+    for number, (first, width) in enumerate(SCATTER_SECTIONS):
+        half = width // 2
+        bufs = (pair_in[number], b_in[number], z_in[number], a_in[number], last[number])
+        section = Scatter(p, w, share, first, width, bufs, [s.at[number] for s in sems])
+        sections.append(section)
+        steps = section.steps()
+        steps[0] = lambda begin=steps[0], load=loads[number]: (load.wait(), begin())
+        plans.append(steps)
+    small_steps = small_gather.steps()
+    small_steps[0] = lambda begin=small_steps[0]: (swap.finish(), begin())
+    plans.insert(1, small_steps)
+    skew = SCATTER_SKEW
+    last_tick = max(len(s) + skew * n for n, s in enumerate(plans))
+    for tick in range(last_tick + 1):
+        for number, steps in enumerate(plans):
+            at = tick - skew * number
+            if 0 <= at < len(steps):
+                steps[at]()
+    for section in sections:
+        section.finish()
+    small_gather.finish()
+    small_gather.sent()
+    for step, copy in enumerate(patch_copies):
+        source = lax.rem(p.blk + 3 - step, 4)
+        landed = patch_out.at[source]
+        remote(
+            landed, landed, patch_sems.at[0, step], patch_sems.at[1, step], {"blk": source}
+        ).wait_recv()
+        copy.wait_send()
+    own_patch.wait()
+    spread = Spread(p, mine, everyone, send_sem, recv_sem)
+    out = small_tail(p, small, map_q[...], probe[...], share, spread)
+    map_out[...], map_q_share[...] = out[0], out[1]
+    probe_share[...] = jnp.broadcast_to(out[2], (24, 128))
+    facts[...] = jnp.concatenate(
+        [jnp.broadcast_to(out[3][:, :128], (7, 128)), out[4][:1]], axis=0
+    )
+
+
+def scatter_call(grads, small_own, map_q, probe, patch):
+    dma = pltpu.SemaphoreType.DMA
+    count = len(SCATTER_SECTIONS)
+    widths = [w // 2 for _, w in SCATTER_SECTIONS]
+    vm = lambda *shape, dt=jnp.bfloat16: pltpu.VMEM(shape, dt)
+    f32 = jnp.float32
+    return pl.pallas_call(
+        scatter_kernel,
+        out_shape=(
+            jax.ShapeDtypeStruct((24, SCATTER_COLS), f32),
+            jax.ShapeDtypeStruct((24, 768), f32),
+            jax.ShapeDtypeStruct((24, 768), f32),
+            jax.ShapeDtypeStruct((24, 128), f32),
+            jax.ShapeDtypeStruct((8, 128), f32),
+            jax.ShapeDtypeStruct((4, 144, 768), jnp.bfloat16),
+        ),
+        in_specs=[pl.BlockSpec(memory_space=pl.ANY)]
+        + [pl.BlockSpec(memory_space=pltpu.VMEM)] * 4,
+        out_specs=tuple([pl.BlockSpec(memory_space=pltpu.VMEM)] * 6),
+        scratch_shapes=[
+            vm(768, SCATTER_COLS),
+            vm(256, 768, dt=f32),
+            [vm(768, w) for w in widths],
+            [vm(2, 192, w) for w in widths],
+            [vm(2, 2, 3, 48, w) for w in widths],
+            [vm(48, w) for w in widths],
+            [vm(48, w, dt=f32) for w in widths],
+            vm(8, 128, dt=f32),
+            vm(31, 8, 128, dt=f32),
+            dma((count,)),
+            dma((4,)),
+            dma((2, 4)),
+            dma,
+            dma,
+            *gather_sems(1),
+            dma((count, 2)),
+            dma((count, 2, 2)),
+            dma((count, 2, 2, 3)),
+            dma((count, 2, 2, 3)),
+            dma((count, 2)),
+            dma((count, 2)),
+        ],
+        compiler_params=pltpu.CompilerParams(
+            collective_id=1, has_side_effects=True, vmem_limit_bytes=62 * 2**20
+        ),
+        name="scatter_grads",
+    )(grads, small_own, map_q, probe, patch)
 
 
 def layer_norm(values, gain_vec, bias_vec):
@@ -345,6 +1033,284 @@
     )
 
 
+def local_kernels(
+    patch_tokens,
+    captions,
+    pair_labels,
+    master_weights,
+    first_moments,
+    second_moments,
+    master_vectors,
+    vector_first,
+    vector_second,
+    loss_scalars,
+    scalar_first,
+    scalar_second,
+):
+    blocks = lax.axis_size("blk")
+    block = lax.axis_index("blk")
+    all_images = patch_tokens.shape[0] * lax.axis_size("img")
+    images = patch_tokens.shape[0] // blocks
+    length = patch_tokens.shape[1] * blocks
+    scale = HEAD_DIM ** (-0.5)
+    pair_labels = lax.dynamic_slice_in_dim(pair_labels, block, 1, 0)
+    rounded = master_weights.astype(jnp.bfloat16)
+    own_map_q = rounded[:, 4 * D + 2 * FF : 5 * D + 2 * FF]
+    own_vectors = master_vectors.astype(jnp.bfloat16)
+    query_part = jnp.dot(own_vectors[:, 6], own_map_q, preferred_element_type=jnp.float32)
+    query_high = query_part.astype(jnp.bfloat16).astype(jnp.float32)
+    query_rows = jnp.concatenate(
+        [
+            query_high.reshape(6, 128),
+            (query_part - query_high).reshape(6, 128),
+            jnp.zeros((12, 128), jnp.float32),
+        ]
+    )
+    own_all = jnp.concatenate(
+        [
+            master_weights[:, : 3 * D],
+            jnp.pad(own_vectors.astype(jnp.float32), ((0, 0), (0, 121))),
+            query_rows,
+            master_weights[:, 3 * D : 4 * D + 2 * FF],
+            master_weights[:, 5 * D + 2 * FF :],
+        ],
+        axis=1,
+    )
+    caption_rows = unit_rows(captions.astype(jnp.float32)).astype(jnp.bfloat16)
+    caption_rows = jnp.pad(caption_rows, ((0, 14), (0, 0)))
+    caption_rows = lax.dynamic_slice_in_dim(caption_rows, block * 16, 16, 0)
+    weights, patch_tokens, caption_unit = gather_call(own_all, patch_tokens, caption_rows)
+    patch_tokens = patch_tokens[None]
+    w_qkv = weights[:, : 3 * D]
+    vectors = weights[:, 2304:2432].astype(jnp.float32)
+    query_all = weights[:, 2432:2560].astype(jnp.float32).reshape(32, 24, 128)
+    w_out = weights[:, 2560:3328]
+    w_up = weights[:, 3328:6400]
+    w_down = weights[:, 6400:9472]
+    w_map_kv = weights[:, 9472:11008]
+    w_map_out = weights[:, 11008:]
+    tokens = patch_tokens.astype(jnp.float32)
+    normed, norm_one_pull = jax.vjp(layer_norm, tokens, vectors[:, 0], vectors[:, 1])
+    normed_b = normed.astype(jnp.bfloat16)
+    qkv_b = jnp.einsum("ipd,dc->ipc", normed_b, w_qkv, preferred_element_type=jnp.float32).astype(
+        jnp.bfloat16
+    )
+    queries = qkv_b[:, :, :D].reshape(images, length, HEADS, HEAD_DIM)
+    keys_all = qkv_b[:, :, D : 2 * D].reshape(images, length, HEADS, HEAD_DIM)
+    values_all = qkv_b[:, :, 2 * D :].reshape(images, length, HEADS, HEAD_DIM)
+    mixed_heads, log_norm = attend(queries, keys_all, values_all)
+    mixed_b = mixed_heads.reshape(images, length, D)
+    residual = tokens + jnp.einsum(
+        "ipd,dc->ipc", mixed_b, w_out, preferred_element_type=jnp.float32
+    )
+    hidden, norm_two_pull = jax.vjp(layer_norm, residual, vectors[:, 2], vectors[:, 3])
+    hidden_b = hidden.astype(jnp.bfloat16)
+    pre_act = jnp.einsum("ipd,df->ipf", hidden_b, w_up, preferred_element_type=jnp.float32)
+    activation, gelu_pull = jax.vjp(jax.nn.gelu, pre_act)
+    activation_b = activation.astype(jnp.bfloat16)
+    layer_out = residual + jnp.einsum(
+        "ipf,df->ipd", activation_b, w_down, preferred_element_type=jnp.float32
+    )
+    final_norm, norm_three_pull = jax.vjp(layer_norm, layer_out, vectors[:, 4], vectors[:, 5])
+    final_b = final_norm.astype(jnp.bfloat16)
+    map_kv = jnp.einsum("ipd,dc->ipc", final_b, w_map_kv, preferred_element_type=jnp.float32)
+    map_kv = map_kv.astype(jnp.bfloat16).reshape(images, length, 2, HEADS, HEAD_DIM)
+    query_total = jnp.sum(query_all, axis=0)
+    probe_query = (query_total[:6] + query_total[6:12]).reshape(D)
+    probe_query = probe_query.astype(jnp.bfloat16).reshape(HEADS, HEAD_DIM)
+    pool_scores = (
+        jnp.einsum("he,iphe->ihp", probe_query, map_kv[:, :, 0], preferred_element_type=jnp.float32)
+        * scale
+    )
+    row_max = jnp.max(pool_scores, axis=-1)
+    row_sum = jnp.sum(jnp.exp(pool_scores - row_max[..., None]), axis=-1)
+    pool_probs = jnp.exp(pool_scores - row_max[..., None]) / row_sum[..., None]
+    map_values = map_kv[:, :, 1].astype(jnp.float32)
+    pooled_part = jnp.einsum(
+        "ihp,iphe->ihe", pool_probs, map_values, precision=lax.Precision.HIGHEST
+    )
+    pooled_heads = pooled_part.reshape(images, D)
+    pooled_heads_b = pooled_heads.astype(jnp.bfloat16)
+    pooled = jnp.dot(pooled_heads_b, w_map_out, preferred_element_type=jnp.float32)
+    unit_image, unit_pull = jax.vjp(unit_rows, pooled)
+    cosine = jnp.einsum(
+        "id,cd->ic",
+        unit_image.astype(jnp.bfloat16),
+        caption_unit,
+        preferred_element_type=jnp.float32,
+    )
+    signs = 2.0 * pair_labels.astype(jnp.float32) - 1.0
+    signs = jnp.pad(signs.reshape(8, 50), ((0, 0), (0, 14))).reshape(8, 4, 16)
+    signs = signs.transpose(1, 0, 2).reshape(1, 512)
+
+    def pair_loss(cosine_in, scalars_in):
+        logits = jnp.exp(scalars_in[0]) * cosine_in + scalars_in[1]
+        return jnp.sum(jnp.where(signs == 0, 0.0, jax.nn.softplus(-signs * logits))) / all_images
+
+    loss_local, loss_pull = jax.vjp(pair_loss, cosine, loss_scalars)
+    grad_cosine, grad_scalars = loss_pull(jnp.ones((), jnp.float32))
+    grad_unit = jnp.einsum(
+        "ic,cd->id",
+        grad_cosine.astype(jnp.bfloat16),
+        caption_unit,
+        preferred_element_type=jnp.float32,
+    )
+    (grad_pooled,) = unit_pull(grad_unit)
+    grad_pooled_b = grad_pooled.astype(jnp.bfloat16)
+    grad_heads_b = jnp.einsum(
+        "ic,dc->id", grad_pooled_b, w_map_out, preferred_element_type=jnp.float32
+    )
+    grad_heads_b = grad_heads_b.astype(jnp.bfloat16).reshape(images, HEADS, HEAD_DIM)
+    grad_heads = grad_heads_b.astype(jnp.float32)
+    centre = jnp.sum(grad_heads * pooled_heads.reshape(images, HEADS, HEAD_DIM), axis=-1)
+    grad_probs = jnp.einsum(
+        "ihe,iphe->ihp", grad_heads_b, map_kv[:, :, 1], preferred_element_type=jnp.float32
+    )
+    grad_pool_scores = (pool_probs * (grad_probs - centre[..., None])).astype(jnp.bfloat16)
+    grad_map_keys = (
+        jnp.einsum(
+            "ihp,he->iphe", grad_pool_scores, probe_query, preferred_element_type=jnp.float32
+        )
+        * scale
+    )
+    grad_map_values = jnp.einsum(
+        "ihp,ihe->iphe", pool_probs, grad_heads, precision=lax.Precision.HIGHEST
+    )
+    grad_probe_query = (
+        jnp.einsum(
+            "ihp,iphe->he", grad_pool_scores, map_kv[:, :, 0], preferred_element_type=jnp.float32
+        ).reshape(D)
+        * scale
+    )
+    grad_map_kv = (
+        jnp.stack([grad_map_keys, grad_map_values], axis=2)
+        .astype(jnp.bfloat16)
+        .reshape(images, length, 2 * D)
+    )
+    grad_w_map_kv = jnp.einsum(
+        "ipd,ipc->dc", final_b, grad_map_kv, preferred_element_type=jnp.float32
+    )
+    grad_final = jnp.einsum(
+        "ipc,dc->ipd", grad_map_kv, w_map_kv, preferred_element_type=jnp.float32
+    )
+    grad_layer_out, grad_gain_three, grad_bias_three = norm_three_pull(grad_final)
+    grad_branch_two = grad_layer_out.astype(jnp.bfloat16)
+    grad_w_down = jnp.einsum(
+        "ipd,ipf->df", grad_branch_two, activation_b, preferred_element_type=jnp.float32
+    )
+    grad_activation = jnp.einsum(
+        "ipd,df->ipf", grad_branch_two, w_down, preferred_element_type=jnp.float32
+    )
+    (grad_pre,) = gelu_pull(grad_activation)
+    grad_pre_b = grad_pre.astype(jnp.bfloat16)
+    grad_w_up = jnp.einsum("ipd,ipf->df", hidden_b, grad_pre_b, preferred_element_type=jnp.float32)
+    grad_hidden = jnp.einsum("ipf,df->ipd", grad_pre_b, w_up, preferred_element_type=jnp.float32)
+    grad_res_part, grad_gain_two, grad_bias_two = norm_two_pull(grad_hidden)
+    grad_residual = grad_layer_out + grad_res_part
+    grad_branch_one = grad_residual.astype(jnp.bfloat16)
+    grad_w_out = jnp.einsum(
+        "ipd,ipc->dc", mixed_b, grad_branch_one, preferred_element_type=jnp.float32
+    )
+    grad_mixed = jnp.einsum(
+        "ipc,dc->ipd", grad_branch_one, w_out, preferred_element_type=jnp.float32
+    )
+    grad_mixed = grad_mixed.astype(jnp.bfloat16)
+    grad_queries, grad_keys, grad_values = attend_back(
+        queries, keys_all, values_all, log_norm, grad_mixed.reshape(images, length, HEADS, HEAD_DIM)
+    )
+    grad_qkv = jnp.concatenate(
+        [
+            grad_queries.reshape(images, length, D),
+            grad_keys.reshape(images, length, D),
+            grad_values.reshape(images, length, D),
+        ],
+        axis=-1,
+    ).astype(jnp.bfloat16)
+    grad_w_qkv = jnp.einsum("ipd,ipc->dc", normed_b, grad_qkv, preferred_element_type=jnp.float32)
+    grad_normed = jnp.einsum("ipc,dc->ipd", grad_qkv, w_qkv, preferred_element_type=jnp.float32)
+    grad_tok_part, grad_gain_one, grad_bias_one = norm_one_pull(grad_normed)
+    grad_vectors = jnp.stack(
+        [
+            grad_gain_one,
+            grad_bias_one,
+            grad_gain_two,
+            grad_bias_two,
+            grad_gain_three,
+            grad_bias_three,
+        ],
+        axis=1,
+    )
+    to_send = jnp.concatenate(
+        [
+            part.astype(jnp.bfloat16)
+            for part in (
+                grad_w_qkv,
+                jnp.pad(grad_vectors, ((0, 0), (0, 250))),
+                grad_w_out,
+                grad_w_up,
+                grad_w_down,
+                grad_w_map_kv,
+            )
+        ],
+        axis=1,
+    )
+    small_own = jnp.concatenate(
+        [
+            pooled_heads_b.astype(jnp.float32),
+            grad_pooled_b.astype(jnp.float32),
+            grad_probe_query[None],
+            jnp.pad(jnp.stack([loss_local, grad_scalars[0], grad_scalars[1]]), (0, D - 3))[None],
+            jnp.zeros((4, D), jnp.float32),
+        ]
+    )
+    share, share_map_out, share_map_q, share_probe, facts, patch_grad = scatter_call(
+        to_send,
+        small_own,
+        own_map_q.astype(jnp.float32),
+        own_vectors[:, 6:7].astype(jnp.float32),
+        (grad_residual + grad_tok_part)[0].astype(jnp.bfloat16),
+    )
+    patch_grad = patch_grad.astype(jnp.float32)
+    loss_total, scalar_total, grad_norm = facts[0, 0], facts[0, 1:3], facts[7, 0]
+    weight_share = jnp.concatenate(
+        [
+            share[:, :2304],
+            share[:, 2560:9472],
+            share_map_q,
+            share[:, 9472:],
+            share_map_out,
+        ],
+        axis=1,
+    )
+    vector_share = jnp.concatenate([share[:, 2304:2310], share_probe[:, :1]], axis=1)
+    factor = CLIP_AT / jnp.maximum(grad_norm, CLIP_AT)
+    new_w, new_wm, new_wv = adamw(
+        master_weights, weight_share * factor, first_moments, second_moments, 0.03, 0.1
+    )
+    new_v, new_vm, new_vv = adamw(
+        master_vectors, vector_share * factor, vector_first, vector_second, 0.3, 0.0
+    )
+    new_s, new_sm, new_sv = adamw(
+        loss_scalars, scalar_total * factor, scalar_first, scalar_second, 0.3, 0.0
+    )
+    return (
+        loss_total,
+        grad_norm,
+        patch_grad,
+        new_w,
+        new_wm,
+        new_wv,
+        new_w.astype(jnp.bfloat16),
+        new_v,
+        new_vm,
+        new_vv,
+        new_v.astype(jnp.bfloat16),
+        new_s,
+        new_sm,
+        new_sv,
+    )
+
+
 def solution(mesh):
     in_specs = (
         P("img", "blk", None),
@@ -376,4 +1342,5 @@
         P(),
         P(),
     )
-    return jax.shard_map(local, mesh=mesh, in_specs=in_specs, out_specs=out_specs, check_vma=False)
+    body = local_kernels if tuple(mesh.shape.values()) == (4, 8) else local
+    return jax.shard_map(body, mesh=mesh, in_specs=in_specs, out_specs=out_specs, check_vma=False)

time: 887 us -> 469 us (0.53)
  waiting for transfers between devices: 353 us -> 0 us
  blocking collectives: 264 us -> 0 us
  Pallas kernels: 0 us -> 243 us
  between operations: 22.8 us -> 5.78 us
  other arithmetic: 61.8 us -> 48.3 us
  starting transfers between devices: 9.14 us -> 0 us
    reduce_scatter x4 -> x0, waiting for transfers between devices: 263 us -> none  [scatter(): lax.psum_scatter(part.astype(jnp.bfloat16), both, scatter_dimension=0, ti...]
    pallas_call x0 -> x2, Pallas kernels: none -> 243 us  [the longest x1 130 us: scatter_call(): pl.pallas_call(scatter_kernel, out_shape=(jax.ShapeDtypeStruct((24, SCATT...]
    all_gather x4 -> x0, blocking collectives: 140 us -> none  [the longest x1 41.6 us: local(): lax.all_gather(pooled_heads_b, both, axis=0, tiled=True)]
    psum x3 -> x0, blocking collectives: 124 us -> none  [the longest x1 46.7 us: local(): lax.psum(jnp.dot(own_vectors[:, 6], own_map_q, preferred_element_type=jnp...]
    all_gather x4 -> x0, waiting for transfers between devices: 88 us -> none  [gather(): return lax.all_gather(rounded[:, start:stop], both, axis=0, tiled=True)]
    unnamed x10 -> x4, other arithmetic: 10 us -> 0.08 us
    dot_general x27 -> x25, matrix products: 106 us -> 99.4 us  [the longest x1 9.27 us: local_kernels(): jnp.einsum('ipd,df->ipf', grad_branch_two, w_down, preferred_element_type...]
  transfers between devices with their start and end apart: 10 -> 0, of which waited for: 5 -> 0; matrix products, arithmetic and copies ran while one was open for 13% -> 0% of each run, Pallas kernels for 0% -> 0%
where the time goes in v2:
time: 469 us; the launch traced here: 462 us
  Pallas kernels  243 us (52%)
  matrix products  133 us (28%)
  other arithmetic  48.3 us (10%)
  local copies, waits for them, and re-layouts  31.2 us (7%)
  between operations  5.78 us (1%)
    pallas_call x1, Pallas kernels, scatter_call(): pl.pallas_call(scatter_kernel, out_shape=(jax.ShapeDtypeStruct((24, SCATT...  130 us
    pallas_call x1, Pallas kernels, gather_call(): pl.pallas_call(gather_kernel, out_shape=(jax.ShapeDtypeStruct((768, GATHE...  113 us
    convert_element_type x1, other arithmetic, attend_back(): grad_scores = (attn_probs * (grad_probs - centre)).astype(jnp.bfloat16)  12.9 us
    dot_general x1, matrix products, attend_back(): jnp.einsum('iqhe,ikhe->ihqk', grad_mixed, values_all, preferred_element_t...  12.1 us
    unnamed x94, local copies, waits for them, and re-layouts  10.5 us

profile of v2, /device:TPU:0, one launch (start us, length us, event | category | flops | bytes accessed | tf_op | source)
XLA Modules:
  0.0 461.7 jit_solution(9384164469162499875)
XLA Ops:
  14.8 113.4 %gather_weights.1 = (bf16[768,11776]{1,0:T(8,128)(2,1)}, bf16[576,768]{1,0:T(8,128)(2,1)}, bf16[512,768]{1,0:T(8,128)(2,1)}) custom-call(f32[24,11776]{1,0:T(8,128)} %copy-done.20, bf16[4,144,768]{2,1,0:T(8,128)(2,1)} %tokens.1, bf16[16,768]{1,0:T(8,128)(2,1)} %pad_dynamic-slice_fusion.caps), custom_call_target="tpu_custom_call" | custom-call | tf_op jit(solution)/shard_map/gather_weights/pallas_call | solution.py:475
  133.8 4.4 fusion.17
  139.6 2.0 copy.101
  144.5 7.4 %multiply_reduce_fusion.1 = (f32[12,576]{1,0:T(8,128)S(1)}, f32[12,576,576]{1,2,0:T(8,128)}) fusion(bf16[576,12,64]{0,2,1:T(8,128)(2,1)S(1)} %bitcast.141, bf16[576,12,64]{0,2,1:T(8,128)(2,1)S(1)} %bitcast.137), kind=kOutput, calls=%fused_computation.6 | convolution fusion | flops 517563648 | bytes 17722368 | tf_op jit(solution)/shard_map/iqhe,ikhe->ihqk/dot_general | solution.py:736
  151.9 9.2 %fusion = f32[12,576]{1,0:T(8,128)S(1)} fusion(f32[12,576,576]{1,2,0:T(8,128)} %get-tuple-element.124, f32[12,576]{1,0:T(8,128)S(1)} %get-tuple-element.123), kind=kLoop, calls=%fused_computation.5 | loop fusion | flops 11937024 | bytes 15980544 | tf_op jit(solution)/shard_map/reduce_sum | solution.py:725
  161.1 8.1 %fusion.47 = bf16[12,64,576]{2,1,0:T(8,128)(2,1)S(1)} fusion(bf16[576,12,64]{0,2,1:T(8,128)(2,1)S(1)} %bitcast.147, f32[12,576,576]{1,2,0:T(8,128)} %get-tuple-element.124, f32[12,576]{1,0:T(8,128)S(1)} %fusion, f32[12,576]{1,0:T(8,128)S(1)} %get-tuple-element.123), kind=kOutput, calls=%fused_computation.84 | convolution fusion | flops 525975552 | bytes 17750016 | tf_op jit(solution)/shard_map/ihqk,ikhe->iqhe/dot_general | solution.py:727
  169.2 2.6 fusion.116
  172.2 5.4 %fusion.24 = f32[576,3072]{1,0:T(8,128)S(1)} fusion(bf16[768,11776]{1,0:T(8,128)(2,1)} %get-tuple-element.24, f32[576,768]{1,0:T(8,128)S(1)} %get-tuple-element.126, f32[768]{0:T(1024)S(1)} %get-tuple-element.85, f32[768]{0:T(1024)S(1)} %get-tuple-element.86, f32[576]{0:T(1024)S(1)} %fusion.85, f32[576]{0:T(1024)S(1)} %broadcast_multiply_fusion.1), kind=kOutput, calls=%fused_computation.36 | convolution fusion | flops 2720120832 | bytes 13576704 | tf_op jit(solution)/shard_map/ipd,df->ipf/dot_general | solution.py:1108
  177.6 9.3 %fusion.117 = (f32[576]{0:T(1024)S(1)}, f32[576,768]{1,0:T(8,128)S(1)}) fusion(f32[576,768]{1,0:T(8,128)S(1)} %get-tuple-element.126, bf16[768,11776]{1,0:T(8,128)(2,1)} %get-tuple-element.24, f32[576,3072]{1,0:T(8,128)S(1)} %fusion.24), kind=kOutput, calls=%fused_computation.223 | convolution fusion | flops 2734718464 | bytes 15337728 | tf_op jit(solution)/shard_map/ipf,df->ipd/dot_general | solution.py:1111
  188.1 4.5 convolution_convert_fusion.5
  192.5 3.9 copy.105
  198.4 2.2 fusion.64
  208.9 1.7 convolution_reduce_fusion.1
  215.8 1.6 copy-done.4
  217.4 4.4 multiply_reduce_fusion.2
  222.7 9.3 %fusion.13 = bf16[576,3072]{1,0:T(8,128)(2,1)S(1)} fusion(f32[576,3072]{1,0:T(8,128)S(1)} %bitcast.168, bf16[768,11776]{1,0:T(8,128)(2,1)} %get-tuple-element.24, f32[576,768]{1,0:T(8,128)S(1)} %get-tuple-element.107, f32[576]{0:T(1024)S(1)} %negate_multiply_fusion.2), kind=kOutput, calls=%fused_computation.20 | convolution fusion | flops 2754183168 | bytes 17107200 | tf_op jit(solution)/shard_map/ipd,df->ipf/dot_general | solution.py:1201
  232.0 6.9 %multiply_reduce_fusion.3 = (bf16[768]{0:T(1024)(128)(2,1)S(1)}, f32[576]{0:T(1024)S(1)}, bf16[768]{0:T(1024)(128)(2,1)S(1)}, f32[576,768]{1,0:T(8,128)S(1)}) fusion(f32[576,768]{1,0:T(8,128)S(1)} %copy-done.7, f32[576]{0:T(1024)S(1)} %fusion.85, f32[576]{0:T(1024)S(1)} %broadcast_multiply_fusion.1, f32[768]{0:T(1024)S(1)} %get-tuple-element.86, ...), kind=kOutput, calls=%fused_computation.72 | convolution fusion | flops 2721445888 | bytes 11809536 | tf_op jit(solution)/shard_map/ipf,df->ipd/dot_general | solution.py:1207
  241.1 3.1 convolution_convert_fusion.7
  245.8 9.3 %fusion.48 = bf16[12,64,576]{2,1,0:T(8,128)(2,1)S(1)} fusion(bf16[576,12,64]{0,2,1:T(8,128)(2,1)S(1)} %bitcast.139, f32[12,576,576]{1,2,0:T(8,128)} %get-tuple-element.124, f32[12,576]{1,0:T(8,128)S(1)} %log_add_fusion), kind=kOutput, calls=%fused_computation.85 | convolution fusion | flops 521994240 | bytes 17722368 | tf_op jit(solution)/shard_map/ihqk,iqhe->ikhe/dot_general | solution.py:739
  255.1 12.1 %multiply_reduce_fusion = (f32[12,576]{1,0:T(8,128)S(1)}, f32[12,576,576]{1,2,0:T(8,128)}) fusion(f32[12,576,576]{1,2,0:T(8,128)} %get-tuple-element.124, f32[12,576]{1,0:T(8,128)S(1)} %log_add_fusion, bf16[576,12,64]{0,2,1:T(8,128)(2,1)S(1)} %bitcast.140, bf16[576,12,64]{0,2,1:T(8,128)(2,1)S(1)} %bitcast.148), kind=kOutput, calls=%fused_computation.1 | convolution fusion | flops 525526272 | bytes 33675264 | tf_op jit(solution)/shard_map/iqhe,ikhe->ihqk/dot_general | solution.py:745
  267.2 12.9 %multiply_convert_fusion = bf16[12,576,576]{1,2,0:T(8,128)(2,1)S(1)} fusion(f32[12,576,576]{1,2,0:T(8,128)} %get-tuple-element.132, f32[12,576,576]{1,2,0:T(8,128)} %get-tuple-element.124, f32[12,576]{1,0:T(8,128)S(1)} %get-tuple-element.131, f32[12,576]{1,0:T(8,128)S(1)} %log_add_fusion), kind=kLoop, calls=%fused_computation | loop fusion | flops 19906560 | bytes 39868416 | tf_op jit(solution)/shard_map/convert_element_type | solution.py:749
  280.1 2.7 multiply_convert_fusion.2
  282.8 1.7 multiply_convert_fusion.3
  284.5 5.1 %fusion.45 = (f32[576]{0:T(1024)S(1)}, f32[576,768]{1,0:T(8,128)S(1)}) fusion(bf16[576,768]{1,0:T(8,128)(2,1)S(1)} %copy-done, f32[768]{0:T(1024)S(1)} %get-tuple-element.88, f32[576]{0:T(1024)S(1)} %broadcast_multiply_fusion.2, bf16[768,11776]{1,0:T(8,128)(2,1)} %get-tuple-element.24, bf16[576,768]{0,1:T(8,128)(2,1)S(1)} %bitcast.153, ...), kind=kOutput, calls=%fused_computation.69 | convolution fusion | flops 2048605696 | bytes 8855040 | tf_op jit(solution)/shard_map/ipc,dc->ipd/dot_general | solution.py:1230
  292.9 7.1 %fusion.14 = bf16[768,11008]{1,0:T(8,128)(2,1)} fusion(bf16[576,768]{0,1:T(8,128)(2,1)} %bitcast.154, bf16[576,768]{0,1:T(8,128)(2,1)} %bitcast.156, bf16[576,768]{0,1:T(8,128)(2,1)} %bitcast.150, bf16[576,768]{1,0:T(8,128)(2,1)S(1)} %copy-done, f32[768]{0:T(1024)S(1)} %get-tuple-element.87, f32[768]{0:T(1024)S(1)} %get-tuple-element.88, ...), kind=kOutput, calls=%fused_computation.23 | convolution fusion | flops 2050818048 | bytes 7088640 | tf_op jit(solution)/shard_map/ipd,ipc->dc/dot_general | solution.py:1229
  300.8 2.2 fusion.46
  303.0 6.3 %fusion.16 = bf16[768,11008]{1,0:T(8,128)(2,1)} fusion(bf16[768,11008]{1,0:T(8,128)(2,1)} %fusion.46, bf16[576,3072]{1,0:T(8,128)(2,1)S(1)} %copy-done.38, f32[576,768]{1,0:T(8,128)S(1)} %copy-done.8, f32[768]{0:T(1024)S(1)} %get-tuple-element.85, f32[768]{0:T(1024)S(1)} %get-tuple-element.86, f32[576]{0:T(1024)S(1)} %fusion.85, ...), kind=kOutput, calls=%fused_computation.27 | convolution fusion | flops 2722480128 | bytes 10037760 | tf_op jit(solution)/shard_map/ipd,ipf->df/dot_general | solution.py:1206
  309.4 6.0 %fusion.15 = bf16[768,11008]{1,0:T(8,128)(2,1)} fusion(bf16[768,11008]{1,0:T(8,128)(2,1)} %fusion.16, f32[576,768]{1,0:T(8,128)S(1)} %copy-done.10, f32[576]{0:T(1024)S(1)} %negate_multiply_fusion.2, f32[576,3072]{1,0:T(8,128)S(1)} %bitcast.170), kind=kOutput, calls=%fused_computation.25 | convolution fusion | flops 2737078272 | bytes 13568256 | tf_op jit(solution)/shard_map/ipd,ipf->df/dot_general | solution.py:1198
  315.4 3.9 fusion.26.grads
  319.3 129.8 %scatter_grads.1 = (f32[24,11008]{1,0:T(8,128)}, f32[24,768]{1,0:T(8,128)}, f32[24,768]{1,0:T(8,128)}, f32[24,128]{1,0:T(8,128)}, f32[8,128]{1,0:T(8,128)}, /*index=5*/bf16[4,144,768]{2,1,0:T(8,128)(2,1)}) custom-call(bf16[768,11008]{1,0:T(8,128)(2,1)} %fusion.26.grads, f32[8,768]{1,0:T(8,128)} %concatenate.44.small_own, f32[24,768]{1,0:T(8,128)} %fusion.78.map_q, ...), custom_call_target="tpu_custom_call" | custom-call | tf_op jit(solution)/shard_map/scatter_grads/pallas_call | solution.py:664
  454.7 2.6 convert_element_type.273
  459.0 2.6 fusion.105
  (204 shorter events, 52.4 us)
Async XLA Ops:
  144.5 7.4 %copy-start.1 = (bf16[1,576,768]{1,2,0:T(8,128)(2,1)}, bf16[1,576,768]{1,2,0:T(8,128)(2,1)S(1)}, u32[]{:S(2)}) copy-start(bf16[1,576,768]{1,2,0:T(8,128)(2,1)S(1)} %copy.102) | copy-start | bytes 2654212
  151.9 9.2 %copy-start.14 = (bf16[1,576,768]{1,2,0:T(8,128)(2,1)S(1)}, bf16[1,576,768]{1,2,0:T(8,128)(2,1)}, u32[]{:S(2)}) copy-start(bf16[1,576,768]{1,2,0:T(8,128)(2,1)} %copy.103) | copy-start | bytes 2654212
  171.8 5.8 %copy-start.6 = (f32[576,768]{1,0:T(8,128)}, f32[576,768]{1,0:T(8,128)S(1)}, u32[]{:S(2)}) copy-start(f32[576,768]{1,0:T(8,128)S(1)} %get-tuple-element.126) | copy-start | bytes 5308420
  177.6 9.3 %copy-start.36 = (f32[576,3072]{1,0:T(8,128)}, f32[576,3072]{1,0:T(8,128)S(1)}, u32[]{:S(2)}) copy-start(f32[576,3072]{1,0:T(8,128)S(1)} %fusion.24) | copy-start | bytes 21233668
  196.5 7.3 %copy-start.16 = (bf16[512,768]{1,0:T(8,128)(2,1)S(1)}, bf16[512,768]{1,0:T(8,128)(2,1)}, u32[]{:S(2)}) copy-start(bf16[512,768]{1,0:T(8,128)(2,1)} %get-tuple-element.25) | copy-start | bytes 2359300
  215.4 7.2 %slice-start = ((s8[7077888]{0:T(1024)(128)(4,1)}), s8[4194304]{0:T(1024)(128)(4,1)S(1)}, s32[]{:S(2)}) async-start(s8[7077888]{0:T(1024)(128)(4,1)} %bitcast.167), calls=%async_computation | async-start | bytes 8388608
  215.7 6.1 %copy-start.18 = (bf16[1,576,2,12,64]{1,4,3,2,0:T(8,128)(2,1)}, bf16[1,576,2,12,64]{1,4,3,2,0:T(8,128)(2,1)S(1)}, u32[]{:S(2)}) copy-start(bf16[1,576,2,12,64]{1,4,3,2,0:T(8,128)(2,1)S(1)} %pad_maximum_fusion.1) | copy-start | bytes 5308420
  217.4 5.3 %slice-start.1 = ((s8[7077888]{0:T(1024)(128)(4,1)}), s8[2883584]{0:T(1024)(128)(4,1)S(1)}, s32[]{:S(2)}) async-start(s8[7077888]{0:T(1024)(128)(4,1)} %bitcast.167), calls=%async_computation.1 | async-start | bytes 5767168
  222.6 17.1 %copy-start.9 = (f32[576,768]{1,0:T(8,128)}, f32[576,768]{1,0:T(8,128)S(1)}, u32[]{:S(2)}) copy-start(f32[576,768]{1,0:T(8,128)S(1)} %get-tuple-element.107) | copy-start | bytes 5308420
  222.6 9.3 %copy-start.7 = (f32[576,768]{1,0:T(8,128)S(1)}, f32[576,768]{1,0:T(8,128)}, u32[]{:S(2)}) copy-start(f32[576,768]{1,0:T(8,128)} %copy-done.6) | copy-start | bytes 5308420
  231.9 6.9 %copy-start.37 = (bf16[576,3072]{1,0:T(8,128)(2,1)}, bf16[576,3072]{1,0:T(8,128)(2,1)S(1)}, u32[]{:S(2)}) copy-start(bf16[576,3072]{1,0:T(8,128)(2,1)S(1)} %fusion.13) | copy-start | bytes 10616836
  245.8 9.3 %copy-start.15 = (bf16[1,576,768]{1,2,0:T(8,128)(2,1)S(1)}, bf16[1,576,768]{1,2,0:T(8,128)(2,1)}, u32[]{:S(2)}) copy-start(bf16[1,576,768]{1,2,0:T(8,128)(2,1)} %copy.103) | copy-start | bytes 2654212
  255.0 29.5 %copy-start.24 = (bf16[12,64,576]{2,1,0:T(8,128)(2,1)}, bf16[12,64,576]{2,1,0:T(8,128)(2,1)S(1)}, u32[]{:S(2)}) copy-start(bf16[12,64,576]{2,1,0:T(8,128)(2,1)S(1)} %fusion.48) | copy-start | bytes 2654212
  267.2 12.9 %copy-start.2 = (bf16[1,576,768]{1,2,0:T(8,128)(2,1)S(1)}, bf16[1,576,768]{1,2,0:T(8,128)(2,1)}, u32[]{:S(2)}) copy-start(bf16[1,576,768]{1,2,0:T(8,128)(2,1)} %copy-done.1) | copy-start | bytes 2654212
  284.5 5.1 %copy-start.17 = (bf16[12,64,576]{2,1,0:T(8,128)(2,1)}, bf16[12,64,576]{2,1,0:T(8,128)(2,1)S(1)}, u32[]{:S(2)}) copy-start(bf16[12,64,576]{2,1,0:T(8,128)(2,1)S(1)} %multiply_convert_fusion.3) | copy-start | bytes 2654212
  292.9 7.9 %copy-start.35 = (bf16[12,64,576]{2,1,0:T(8,128)(2,1)S(1)}, bf16[12,64,576]{2,1,0:T(8,128)(2,1)}, u32[]{:S(2)}) copy-start(bf16[12,64,576]{2,1,0:T(8,128)(2,1)} %copy-done.34) | copy-start | bytes 2654212
  292.9 10.1 %copy-start.38 = (bf16[576,3072]{1,0:T(8,128)(2,1)S(1)}, bf16[576,3072]{1,0:T(8,128)(2,1)}, u32[]{:S(2)}) copy-start(bf16[576,3072]{1,0:T(8,128)(2,1)} %copy-done.37) | copy-start | bytes 10616836
  300.8 8.5 %slice-start.2 = ((s8[7077888]{0:T(1024)(128)(4,1)}), s8[4194304]{0:T(1024)(128)(4,1)S(1)}, s32[]{:S(2)}) async-start(s8[7077888]{0:T(1024)(128)(4,1)} %bitcast.169), calls=%async_computation.2 | async-start | bytes 8388608
  303.0 6.3 %copy-start.10 = (f32[576,768]{1,0:T(8,128)S(1)}, f32[576,768]{1,0:T(8,128)}, u32[]{:S(2)}) copy-start(f32[576,768]{1,0:T(8,128)} %copy-done.9) | copy-start | bytes 5308420
  303.0 6.3 %slice-start.3 = ((s8[7077888]{0:T(1024)(128)(4,1)}), s8[2883584]{0:T(1024)(128)(4,1)S(1)}, s32[]{:S(2)}) async-start(s8[7077888]{0:T(1024)(128)(4,1)} %bitcast.169), calls=%async_computation.3 | async-start | bytes 5767168
  309.4 6.1 %copy-start.5 = (f32[576,768]{1,0:T(8,128)S(1)}, f32[576,768]{1,0:T(8,128)}, u32[]{:S(2)}) copy-start(f32[576,768]{1,0:T(8,128)} %copy-done.3) | copy-start | bytes 5308420
  309.4 6.0 %copy-start.19 = (bf16[1,576,2,12,64]{1,4,3,2,0:T(8,128)(2,1)S(1)}, bf16[1,576,2,12,64]{1,4,3,2,0:T(8,128)(2,1)}, u32[]{:S(2)}) copy-start(bf16[1,576,2,12,64]{1,4,3,2,0:T(8,128)(2,1)} %copy-done.18) | copy-start | bytes 5308420
  319.3 132.7 %copy-start.29 = (f32[2]{0:T(128)S(1)}, f32[2]{0:T(128)}, u32[]{:S(2)}) copy-start(f32[2]{0:T(128)} %param.21) | copy-start | bytes 28
  319.3 132.7 %copy-start.32 = (f32[2]{0:T(128)S(1)}, f32[2]{0:T(128)}, u32[]{:S(2)}) copy-start(f32[2]{0:T(128)} %param.22) | copy-start | bytes 28
  319.3 132.7 %copy-start.33 = (f32[2]{0:T(128)S(1)}, f32[2]{0:T(128)}, u32[]{:S(2)}) copy-start(f32[2]{0:T(128)} %param.23) | copy-start | bytes 28
  319.3 134.8 %copy-start.28 = (f32[24,7]{0,1:T(8,128)S(1)}, f32[24,7]{0,1:T(8,128)}, u32[]{:S(2)}) copy-start(f32[24,7]{0,1:T(8,128)} %param.18) | copy-start | bytes 2020
  319.3 134.8 %copy-start.30 = (f32[24,7]{0,1:T(8,128)S(1)}, f32[24,7]{0,1:T(8,128)}, u32[]{:S(2)}) copy-start(f32[24,7]{0,1:T(8,128)} %param.19) | copy-start | bytes 2020
  319.3 134.7 %copy-start.31 = (f32[24,7]{0,1:T(8,128)S(1)}, f32[24,7]{0,1:T(8,128)}, u32[]{:S(2)}) copy-start(f32[24,7]{0,1:T(8,128)} %param.20) | copy-start | bytes 2020
  449.1 8.2 %copy-start.23 = (f32[24,11008]{1,0:T(8,128)S(1)}, f32[24,11008]{1,0:T(8,128)}, u32[]{:S(2)}) copy-start(f32[24,11008]{1,0:T(8,128)} %get-tuple-element.28) | copy-start | bytes 3170308
  454.7 2.7 copy-start.27
  454.7 2.8 copy-start.26
  454.7 2.8 copy-start.22
  (11 other events, 19.0 us)

commit v3 on v1

--- a/solution.py
+++ b/solution.py
@@ -1,6 +1,10 @@
+import functools
+
 import jax
 import jax.numpy as jnp
 from jax import lax
+from jax.experimental import pallas as pl
+from jax.experimental.pallas import tpu as pltpu
 from jax.sharding import PartitionSpec as P
 
 D = 768
@@ -345,6 +349,1324 @@
     )
 
 
+LINK_SPEED = (1.0, 2.0)
+
+
+def gather_key(number, at):
+    return 0 if at == 0 else at + number
+
+
+MESH = pl.DeviceIdType.MESH
+CHIP_ROWS = 48
+GATHER_SECTIONS = ((0, 2560), (2560, 3840), (6400, 3072), (9472, 2304))
+SCATTER_SECTIONS = (
+    (9472, 1536, True),
+    (6400, 3072, False),
+    (2560, 3840, True),
+    (0, 1280, False),
+    (1280, 1280, False),
+)
+GATHER_COLS = 11776
+SCATTER_COLS = 11008
+
+
+def aligned(value, step):
+    return pl.multiple_of(value, step)
+
+
+class Place:
+    def __init__(self):
+        self.blk = lax.axis_index("blk")
+        self.img = lax.axis_index("img")
+        self.x = lax.rem(self.blk, 2)
+        self.y = self.blk // 2
+        self.z = self.img // 2
+        self.c = lax.rem(self.img, 2)
+        self.chip = self.blk * 4 + self.z
+        self.sibling = {"img": self.z * 2 + 1 - self.c}
+        self.up = {"img": self.img + 2}
+        self.down = {"img": self.img - 2}
+        self.a_near = {"blk": self.block(1, 0)}
+        self.b_near = {"blk": self.block(0, 1)}
+
+    def block(self, da, db):
+        flip_x = da * (1 - self.c) + db * self.c
+        flip_y = db * (1 - self.c) + da * self.c
+        other_x = self.x + flip_x * (1 - 2 * self.x)
+        other_y = self.y + flip_y * (1 - 2 * self.y)
+        return other_y * 2 + other_x
+
+
+def remote(src, dst, send_sem, recv_sem, device):
+    return pltpu.make_async_remote_copy(
+        src_ref=src,
+        dst_ref=dst,
+        send_sem=send_sem,
+        recv_sem=recv_sem,
+        device_id=device,
+        device_id_type=MESH,
+    )
+
+
+def greet_all(place):
+    barrier = pltpu.get_barrier_semaphore()
+    me = place.blk * 8 + place.img
+
+    def greet(step, carry):
+        other = lax.rem(me + step, 32)
+        pl.semaphore_signal(
+            barrier,
+            inc=1,
+            device_id={"blk": other // 8, "img": lax.rem(other, 8)},
+            device_id_type=MESH,
+        )
+        return carry
+
+    lax.fori_loop(1, 32, greet, 0)
+    pl.semaphore_wait(barrier, 31)
+
+
+class Gather:
+    def __init__(self, place, buf, rows, first, width, sems):
+        self.p, self.buf, self.rows, self.half = place, buf, rows, width // 2
+        self.mine = aligned(first + place.c * self.half, 128)
+        self.theirs = aligned(first + (1 - place.c) * self.half, 128)
+        self.near_recv, self.z_recv, self.b_recv, self.near_send, self.z_send, self.b_send, self.pair = sems
+
+    def item(self, da, db, level):
+        start = aligned((self.p.block(da, db) * 4 + level) * self.rows, self.rows)
+        return self.buf.at[pl.ds(start, self.rows), pl.ds(self.mine, self.half)]
+
+    def a_copy(self):
+        own = self.item(0, 0, self.p.z)
+        return remote(own, own, self.near_send, self.near_recv, self.p.a_near)
+
+    def z_copy(self, da, level, up):
+        part = self.item(da, 0, level)
+        device = self.p.up if up else self.p.down
+        return remote(part, part, self.z_send.at[up, da, level], self.z_recv.at[da, level], device)
+
+    def b_copy(self, da, level):
+        part = self.item(da, 0, level)
+        return remote(part, part, self.b_send.at[da, level], self.b_recv.at[da, level], self.p.b_near)
+
+    def pair_copy(self, da, db, level):
+        part = self.item(da, db, level)
+        return remote(part, part, self.pair.at[0], self.pair.at[1], self.p.sibling)
+
+    def onward(self, da, level, up, down):
+        self.b_copy(da, level).start()
+        if up:
+            pl.when(self.p.z < 3)(lambda: self.z_copy(da, level, 1).start())
+        if down:
+            pl.when(self.p.z > 0)(lambda: self.z_copy(da, level, 0).start())
+        self.pair_copy(da, 0, level).start()
+
+    def begin(self):
+        self.a_copy().start()
+        self.onward(0, self.p.z, True, True)
+
+    def near(self):
+        part = self.item(1, 0, self.p.z)
+        remote(part, part, self.near_send, self.near_recv, self.p.a_near).wait_recv()
+        self.onward(1, self.p.z, True, True)
+
+    def level(self, distance):
+        z = self.p.z
+
+        @pl.when(z >= distance)
+        def from_below():
+            for da in range(2):
+                self.z_copy(da, z - distance, 1).wait_recv()
+                self.onward(da, z - distance, True, False)
+
+        @pl.when(z + distance <= 3)
+        def from_above():
+            for da in range(2):
+                self.z_copy(da, z + distance, 0).wait_recv()
+                self.onward(da, z + distance, False, True)
+
+    def far(self):
+        for level in range(4):
+            for da in range(2):
+                part = self.item(da, 1, level)
+                remote(
+                    part, part, self.b_send.at[da, level], self.b_recv.at[da, level], self.p.b_near
+                ).wait_recv()
+                self.pair_copy(da, 1, level).start()
+
+    def finish(self):
+        whole = self.buf.at[pl.ds(0, 16 * self.rows), pl.ds(self.theirs, self.half)]
+        both = remote(whole, whole, self.pair.at[0], self.pair.at[1], self.p.sibling)
+        both.wait_recv()
+
+    def sent(self):
+        z = self.p.z
+        self.a_copy().wait_send()
+        whole = self.buf.at[pl.ds(0, 16 * self.rows), pl.ds(self.mine, self.half)]
+        remote(whole, whole, self.pair.at[0], self.pair.at[1], self.p.sibling).wait_send()
+        for level in range(4):
+            for da in range(2):
+                self.b_copy(da, level).wait_send()
+                if level < 3:
+                    pl.when((z >= level) & (z < 3))(
+                        lambda da=da, level=level: self.z_copy(da, level, 1).wait_send()
+                    )
+                if level > 0:
+                    pl.when((z <= level) & (z > 0))(
+                        lambda da=da, level=level: self.z_copy(da, level, 0).wait_send()
+                    )
+
+    def steps(self):
+        return [
+            self.begin,
+            self.near,
+            lambda: self.level(1),
+            lambda: self.level(2),
+            lambda: self.level(3),
+            self.far,
+        ]
+
+
+def gather_sems(count):
+    dma = pltpu.SemaphoreType.DMA
+    return [
+        dma((count,)),
+        dma((count, 2, 4)),
+        dma((count, 2, 4)),
+        dma((count,)),
+        dma((count, 2, 2, 4)),
+        dma((count, 2, 4)),
+        dma((count, 2)),
+    ]
+
+
+class Scatter:
+    def __init__(self, place, buf, share, first, width, z_first, bufs, sems):
+        self.p, self.buf, self.share, self.half = place, buf, share, width // 2
+        self.z_first = z_first
+        self.sides = 2 if z_first else 1
+        self.mine = aligned(first + place.c * self.half, 128)
+        self.theirs = aligned(first + (1 - place.c) * self.half, 128)
+        self.pair_in, self.b_in, self.z_in, self.a_in, self.last = bufs
+        self.pair, self.b_sem, self.z_send, self.z_recv, self.a_sem, self.end = sems
+
+    def run_rows(self, da, db):
+        return aligned(self.p.block(da, db) * 192, 192)
+
+    def run(self, da, db):
+        return self.buf.at[pl.ds(self.run_rows(da, db), 192), pl.ds(self.mine, self.half)]
+
+    def level_rows(self, da, level):
+        return aligned((self.p.block(da, 0) * 4 + level) * 48, 48)
+
+    def part(self, da, level):
+        return self.buf.at[pl.ds(self.level_rows(da, level), 48), pl.ds(self.mine, self.half)]
+
+    def add(self, row, source, count, offset=0):
+        def one(step, carry):
+            here = aligned(row + step * 48, 48)
+            there = aligned(offset + step * 48, 48)
+            self.buf[pl.ds(here, 48), pl.ds(self.mine, self.half)] += source[pl.ds(there, 48), :]
+            return carry
+
+        if count == 1:
+            one(0, 0)
+        else:
+            lax.fori_loop(0, count, one, 0)
+
+    def pair_copy(self):
+        return remote(
+            self.buf.at[pl.ds(0, 768), pl.ds(self.theirs, self.half)],
+            self.pair_in,
+            self.pair.at[0],
+            self.pair.at[1],
+            self.p.sibling,
+        )
+
+    def b_copy(self, da):
+        return remote(
+            self.run(da, 1),
+            self.b_in.at[da * 192 : da * 192 + 192, :],
+            self.b_sem.at[0, da],
+            self.b_sem.at[1, da],
+            self.p.b_near,
+        )
+
+    def z_slot(self, da, level, up):
+        return aligned(((up * self.sides + da) * 3 + level - up) * 48, 48)
+
+    def z_copy(self, da, level, up):
+        return remote(
+            self.part(da, level),
+            self.z_in.at[pl.ds(self.z_slot(da, level, up), 48), :],
+            self.z_send.at[up, da, level - up],
+            self.z_recv.at[up, da, level - up],
+            self.p.up if up else self.p.down,
+        )
+
+    def a_copy(self):
+        source = self.part(1, self.p.z) if self.z_first else self.run(1, 0)
+        return remote(source, self.a_in, self.a_sem.at[0], self.a_sem.at[1], self.p.a_near)
+
+    def end_copy(self):
+        return remote(
+            self.last.at[pl.ds(aligned((1 - self.p.c) * 24, 8), 24), :],
+            self.share.at[:, pl.ds(self.mine, self.half)],
+            self.end.at[0],
+            self.end.at[1],
+            self.p.sibling,
+        )
+
+    def begin(self):
+        self.pair_copy().start()
+
+    def pairs_far(self):
+        self.pair_copy().wait_recv()
+        for da in range(2):
+            row = self.run_rows(da, 1)
+            self.add(row, self.pair_in, 4, row)
+            self.b_copy(da).start()
+
+    def pairs_near(self):
+        for da in range(2):
+            row = self.run_rows(da, 0)
+            self.add(row, self.pair_in, 4, row)
+
+    def blocks(self):
+        for da in (1, 0):
+            self.b_copy(da).wait_recv()
+            self.add(self.run_rows(da, 0), self.b_in, 4, da * 192)
+            if da == 1 and not self.z_first:
+                self.a_copy().start()
+
+    def z_step(self, da, level, up, holds, takes, gives):
+        @pl.when(holds)
+        def step():
+            copy = self.z_copy(da, level, up)
+
+            @pl.when(takes)
+            def take():
+                copy.wait_recv()
+                self.add(self.level_rows(da, level), self.z_in, 1, self.z_slot(da, level, up))
+
+            if gives:
+                copy.start()
+
+    def levels(self, slot):
+        z = self.p.z
+        for da in range(self.sides):
+            self.z_step(da, 3 - slot + z, 1, (z <= slot) & (z >= slot - 2), z >= 1, slot < 3)
+            self.z_step(da, slot - 3 + z, 0, (z >= 3 - slot) & (z <= 5 - slot), z <= 2, slot < 3)
+
+    def across(self):
+        self.a_copy().start()
+
+    def joined(self):
+        self.a_copy().wait_recv()
+        self.add(self.run_rows(0, 0), self.a_in, 4)
+
+    def close(self):
+        rows = self.level_rows(0, self.p.z)
+        total = self.buf[pl.ds(rows, 48), pl.ds(self.mine, self.half)].astype(jnp.float32)
+        if self.z_first:
+            self.a_copy().wait_recv()
+            total += self.a_in[...].astype(jnp.float32)
+        self.last[...] = total
+        self.end_copy().start()
+        self.share[:, pl.ds(self.mine, self.half)] = self.last[
+            pl.ds(aligned(self.p.c * 24, 8), 24), :
+        ]
+
+    def finish(self):
+        z = self.p.z
+        theirs = self.share.at[:, pl.ds(self.theirs, self.half)]
+        remote(theirs, theirs, self.end.at[0], self.end.at[1], self.p.sibling).wait_recv()
+        self.end_copy().wait_send()
+        self.a_copy().wait_send()
+        self.pair_copy().wait_send()
+        for da in range(2):
+            self.b_copy(da).wait_send()
+        for da in range(self.sides):
+            for number in range(3):
+                up, down = self.z_copy(da, 3 - number, 1), self.z_copy(da, number, 0)
+                pl.when(z < 3 - number)(lambda up=up: up.wait_send())
+                pl.when(z > number)(lambda down=down: down.wait_send())
+
+
+class Links:
+    def __init__(self, slow=1.0, hop=2.0):
+        self.flat = self.high = 0.0
+        self.slow, self.hop = slow, hop
+
+    def use(self, name, start, time):
+        start = max(start, getattr(self, name))
+        setattr(self, name, start + time * self.slow)
+        return start + time * self.slow + self.hop
+
+    def steps(self, section, start, width):
+        size = width / 256
+        out = []
+        now = start + 0.35 * size * self.slow + 1.0
+        out += [(now, section.pairs_far), (now + 0.5, section.pairs_near)]
+        now = self.use("flat", now + 0.5, 1.01 * size)
+        out.append((now, section.blocks))
+        if not section.z_first:
+            now = self.use("flat", now, 0.5 * size)
+            out.append((now, section.joined))
+        for slot in range(4):
+            out.append((now, functools.partial(section.levels, slot)))
+            if slot < 3:
+                now = self.use("high", now, 0.2525 * section.sides * size)
+        if section.z_first:
+            out.append((now, section.across))
+            now = self.use("flat", now, 0.13 * size)
+        out.append((now, section.close))
+        return out
+
+
+class Program:
+    def __init__(self):
+        self.now, self.places, self.wanted = 0.0, [], []
+        self.plans = {}
+        self.tail = []
+
+    def loop(self, name, count, each):
+        self.plans[name] = {}
+        for index in range(count):
+            self.now += each
+            self.places.append((self.now, name, index))
+
+    def gap(self, time):
+        self.now += time
+
+    def want(self, steps):
+        self.wanted += [(time, len(self.wanted) + n, step) for n, (time, step) in enumerate(steps)]
+
+    def settle(self):
+        for time, _, step in sorted(self.wanted, key=lambda entry: entry[:2]):
+            for place, name, index in self.places:
+                if place >= time:
+                    self.plans[name].setdefault(index, []).append(step)
+                    break
+            else:
+                self.tail.append(step)
+
+
+class Swap:
+    def __init__(self, place, pieces, buf, first_buf_row, rows, first, width, offset, sems):
+        self.p, self.rows, self.half = place, rows, width // 2
+        self.buf, self.sems = buf, sems
+        self.row = aligned(first_buf_row + place.c * rows, rows)
+        self.other_row = aligned(first_buf_row + (1 - place.c) * rows, rows)
+        self.halves = []
+        for core in range(2):
+            low, here = first + core * self.half, []
+            for array, source, target, size in pieces:
+                start, stop = max(low, target), min(low + self.half, target + size)
+                if start < stop:
+                    at = start - low + offset if offset is not None else start
+                    here.append((array, source + start - target, at, stop - start))
+            self.halves.append(here)
+        self.at = (
+            pl.ds(aligned(first + place.c * self.half, 128), self.half)
+            if offset is None
+            else pl.ds(offset, self.half)
+        )
+        self.away_at = (
+            pl.ds(aligned(first + (1 - place.c) * self.half, 128), self.half)
+            if offset is None
+            else pl.ds(offset, self.half)
+        )
+
+    def begin(self, late=None):
+        for core in range(2):
+            for array, source, at, size in self.halves[core]:
+                if late is not None and (array is late[0]) != late[1]:
+                    continue
+                part = array.at[:, source : source + size]
+                goal = self.buf.at[pl.ds(self.row, self.rows), at : at + size]
+
+                @pl.when(self.p.c == core)
+                def here(part=part, goal=goal):
+                    pltpu.make_async_copy(part, goal, self.sems.at[2]).start()
+
+                @pl.when(self.p.c != core)
+                def away(part=part, goal=goal):
+                    remote(part, goal, self.sems.at[0], self.sems.at[1], self.p.sibling).start()
+
+    def finish(self):
+        landed = self.buf.at[pl.ds(self.other_row, self.rows), self.at]
+        own = self.buf.at[pl.ds(self.row, self.rows), self.at]
+        gone = self.buf.at[pl.ds(self.row, self.rows), self.away_at]
+        remote(landed, landed, self.sems.at[0], self.sems.at[1], self.p.sibling).wait_recv()
+        pltpu.make_async_copy(own, own, self.sems.at[2]).wait()
+        remote(gone, gone, self.sems.at[0], self.sems.at[1], self.p.sibling).wait_send()
+
+
+class Spread:
+    def __init__(self, place, mine, everyone, send_sem, recv_sem):
+        self.p, self.mine, self.everyone = place, mine, everyone
+        self.send_sem, self.recv_sem = send_sem, recv_sem
+        self.me = place.blk * 8 + place.img
+
+    def copy(self, step):
+        other = lax.rem(self.me + step, 32)
+        return remote(
+            self.mine,
+            self.everyone.at[step - 1],
+            self.send_sem,
+            self.recv_sem,
+            {"blk": other // 8, "img": lax.rem(other, 8)},
+        )
+
+    def begin(self, tile):
+        self.mine[...] = tile
+
+        def start(step, carry):
+            self.copy(step).start()
+            return carry
+
+        lax.fori_loop(1, 32, start, 0)
+
+    def finish(self):
+        lane = lax.broadcasted_iota(jnp.int32, (1, 768), 1)
+        scalars = self.sums
+        square = jnp.sum(jnp.where((lane == 1) | (lane == 2), scalars * scalars, 0.0))
+        return scalars, jnp.sqrt(self.total() + square)
+
+    def total(self):
+        remote(
+            self.everyone, self.everyone, self.send_sem, self.recv_sem, self.p.sibling
+        ).wait()
+        return self.mine[...] + jnp.sum(self.everyone[...], axis=0)
+
+
+def small_tail(p, small, map_q, probe, share, spread, map_out_ref, map_q_ref):
+    everything = small[...]
+    as_rows = everything.astype(jnp.bfloat16)
+    sums = jnp.sum(everything.reshape(32, 8, 768), axis=0)
+    query, scalars = sums[2:3], sums[3:4]
+    device = lax.broadcasted_iota(jnp.int32, (32, 256), 0) * 8
+    row = lax.broadcasted_iota(jnp.int32, (32, 256), 1)
+
+    def rows_of(kind):
+        pick = (row == device + kind).astype(jnp.float32).astype(jnp.bfloat16)
+        return jnp.dot(pick, as_rows, preferred_element_type=jnp.float32).astype(jnp.bfloat16)
+
+    pooled, grads = rows_of(0), rows_of(1)
+    first = (p.blk * 8 + p.img) * 24
+    picks = (
+        lax.broadcasted_iota(jnp.int32, (24, 768), 1)
+        == lax.broadcasted_iota(jnp.int32, (24, 768), 0) + first
+    ).astype(jnp.float32).astype(jnp.bfloat16)
+    rows = lax.dot_general(
+        picks, pooled, (((1,), (1,)), ((), ())), preferred_element_type=jnp.float32
+    ).astype(jnp.bfloat16)
+    map_out = jnp.dot(rows, grads, preferred_element_type=jnp.float32)
+    map_q_share = probe * query
+    probe_share = jnp.sum(map_q * query, axis=1, keepdims=True)
+    square = (
+        jnp.sum(map_out * map_out)
+        + jnp.sum(map_q_share * map_q_share)
+        + jnp.sum(probe_share * probe_share)
+    )
+
+    def one(step, total):
+        part = share[:, pl.ds(aligned(step * 256, 256), 256)]
+        return total + jnp.sum(part * part)
+
+    square = lax.fori_loop(0, SCATTER_COLS // 256, one, square)
+    spread.begin(jnp.full((8, 128), square, jnp.float32))
+    spread.sums = scalars
+    map_out_ref[...], map_q_ref[...] = map_out, map_q_share
+    return probe_share
+
+
+COL_VECTORS = 2304
+COL_QUERY = 2432
+COL_OUT = 2560
+COL_UP = 3328
+COL_DOWN = 6400
+COL_MAP_KV = 9472
+COL_MAP_OUT = 11008
+TOKENS = 576
+CHUNK = 96
+TILE = 256
+SCALE = 0.125
+GELU_A = 0.7978845608028654
+GELU_B = 0.044715
+NT = (((1,), (1,)), ((), ()))
+TN = (((0,), (0,)), ((), ()))
+
+
+def dot(lhs, rhs, dims=(((1,), (0,)), ((), ()))):
+    return lax.dot_general(lhs, rhs, dims, preferred_element_type=jnp.float32)
+
+
+def loop(count, body, plan=None):
+    def one(index, carry):
+        body(index)
+        for at, steps in (plan or {}).items():
+
+            @pl.when(index == at)
+            def run(steps=steps):
+                for step in steps:
+                    step()
+
+        return carry
+
+    lax.fori_loop(0, count, one, 0)
+
+
+def columns(index, first=0, width=TILE):
+    return pl.ds(aligned(first + index * width, 128), width)
+
+
+def chunk_rows(index):
+    return pl.ds(aligned(index * CHUNK, 32), CHUNK)
+
+
+def normalize(values):
+    row_mean = jnp.mean(values, axis=-1, keepdims=True)
+    centered = values - row_mean
+    row_var = jnp.mean(centered * centered, axis=-1, keepdims=True)
+    rate = lax.rsqrt(row_var + 1e-06)
+    return centered * rate, rate
+
+
+def normalize_back(scaled, rate, grad, gain):
+    inner = grad * gain
+    first = jnp.mean(inner, axis=-1, keepdims=True)
+    second = jnp.mean(inner * scaled, axis=-1, keepdims=True)
+    return (
+        rate * (inner - first - scaled * second),
+        jnp.sum(grad * scaled, axis=0, keepdims=True),
+        jnp.sum(grad, axis=0, keepdims=True),
+    )
+
+
+class Tower:
+    def __init__(self, **refs):
+        self.__dict__.update(refs)
+
+    def unpack(self):
+        turned = jnp.transpose(self.w[:, COL_VECTORS : COL_VECTORS + 128].astype(jnp.float32))
+        self.vec[0:8, :] = turned[0:8]
+        packed = self.w[:, COL_QUERY : COL_QUERY + 128].astype(jnp.float32)
+        total = jnp.sum(packed.reshape(32, 24, 128), axis=0)
+        query = total[0:6] + total[6:12]
+        row = jnp.concatenate([query[i : i + 1] for i in range(6)], axis=1)
+        self.vec[8:16, :] = jnp.broadcast_to(row, (8, 768)).astype(jnp.bfloat16).astype(jnp.float32)
+
+    def norm(self, source, gain, bias, out):
+        def body(index):
+            rows = chunk_rows(index)
+            scaled, _ = normalize(source[rows, :].astype(jnp.float32))
+            out[rows, :] = (scaled * gain + bias).astype(jnp.bfloat16)
+
+        loop(TOKENS // CHUNK, body)
+
+    def first_norm(self):
+        self.norm(self.x, self.vec[0:1, :], self.vec[1:2, :], self.h)
+
+    def project(self, plan=None):
+        def body(index):
+            self.qkv[:, columns(index)] = dot(self.h[...], self.w[:, columns(index)]).astype(jnp.bfloat16)
+
+        loop(9, body, plan)
+
+    def pair_of(self, pair, which):
+        return self.qkv[:, columns(pair, which * D, 128)]
+
+    def attend(self, plan=None):
+        lanes = lax.broadcasted_iota(jnp.int32, (TOKENS, 128), 1)
+
+        def body(pair):
+            queries = self.pair_of(pair, 0) * jnp.bfloat16(SCALE)
+            keys = self.pair_of(pair, 1)
+            values_turned = jnp.transpose(self.pair_of(pair, 2))
+            mixed = []
+            for head in range(2):
+                mine = (lanes < 64) if head == 0 else (lanes >= 64)
+                masked = jnp.where(mine, queries, jnp.bfloat16(0))
+                scores = dot(keys, masked, NT)
+                most = jnp.max(scores, axis=0, keepdims=True)
+                expos = jnp.exp(scores - most)
+                total = jnp.sum(expos, axis=0, keepdims=True)
+                part = dot(values_turned[head * 64 : head * 64 + 64], expos.astype(jnp.bfloat16))
+                mixed.append(part * (1.0 / total))
+                self.lse[pl.ds(pair * 2 + head, 1), :] = most + jnp.log(total)
+            self.a[:, columns(pair, 0, 128)] = jnp.transpose(
+                jnp.concatenate(mixed, axis=0)
+            ).astype(jnp.bfloat16)
+
+        loop(6, body, plan)
+
+    def attend_out(self, plan=None):
+        def body(index):
+            self.r[:, columns(index)] = self.x[:, columns(index)].astype(jnp.float32) + dot(
+                self.a[...], self.w[:, columns(index, COL_OUT)]
+            )
+
+        loop(3, body, plan)
+        self.norm(self.r, self.vec[2:3, :], self.vec[3:4, :], self.h2)
+
+    def feed_up(self, plan=None):
+        def body(index):
+            value = dot(self.h2[...], self.w[:, columns(index, COL_UP)])
+            square = value * value
+            bend = jnp.tanh(GELU_A * value * (1.0 + GELU_B * square))
+            half = 0.5 + 0.5 * bend
+            self.g[:, columns(index)] = (value * half).astype(jnp.bfloat16)
+            slope = half + 0.5 * value * (1.0 - bend * bend) * (
+                GELU_A + 3.0 * GELU_A * GELU_B * square
+            )
+            self.gp[:, columns(index)] = slope.astype(jnp.bfloat16)
+
+        loop(12, body, plan)
+
+    def feed_down(self, plan=None):
+        def body(index):
+            self.y[:, columns(index)] = self.r[:, columns(index)] + dot(
+                self.g[...], self.w[columns(index), COL_DOWN : COL_DOWN + FF], NT
+            )
+
+        loop(3, body, plan)
+        self.norm(self.y, self.vec[4:5, :], self.vec[5:6, :], self.f)
+
+    def pool_project(self, plan=None):
+        def body(index):
+            self.kvp[:, columns(index)] = dot(
+                self.f[...], self.w[:, columns(index, COL_MAP_KV)]
+            ).astype(jnp.bfloat16)
+
+        loop(6, body, plan)
+
+    def pool(self, signs, temperature, offset, images):
+        head = lax.broadcasted_iota(jnp.int32, (16, D), 0)
+        owner = lax.broadcasted_iota(jnp.int32, (16, D), 1) // HEAD_DIM
+        own = head == owner
+        heads_query = jnp.where(own, self.vec[8:9, :], 0.0).astype(jnp.bfloat16)
+        keys, values = self.kvp[:, :D], self.kvp[:, D:]
+        scores = dot(heads_query, keys, NT) * SCALE
+        expos = jnp.exp(scores - jnp.max(scores, axis=1, keepdims=True))
+        probs = expos / jnp.sum(expos, axis=1, keepdims=True)
+        probs_high = probs.astype(jnp.bfloat16)
+        probs_low = (probs - probs_high.astype(jnp.float32)).astype(jnp.bfloat16)
+        spread = dot(probs_high, values) + dot(probs_low, values)
+        pooled = jnp.sum(jnp.where(own, spread, 0.0), axis=0, keepdims=True)
+        pooled_b = pooled.astype(jnp.bfloat16)
+        w_out = self.w[:, COL_MAP_OUT : COL_MAP_OUT + D]
+        many = jnp.broadcast_to(pooled, (16, D)).astype(jnp.bfloat16)
+        embed = dot(many, w_out)[0:1]
+        rate = lax.rsqrt(jnp.sum(embed * embed, axis=1, keepdims=True) + 1e-06)
+        unit = jnp.broadcast_to(embed * rate, (16, D)).astype(jnp.bfloat16)
+        cosine = dot(unit, self.cap[...], NT)[0:1]
+        heat = jnp.exp(temperature)
+        logits = heat * cosine + offset
+        turned = -signs * logits
+        losses = jnp.maximum(turned, 0.0) + jnp.log1p(jnp.exp(-jnp.abs(turned)))
+        loss = jnp.sum(jnp.where(signs == 0.0, 0.0, losses), axis=1, keepdims=True) / images
+        grad_logits = -signs * (1.0 / (1.0 + jnp.exp(-turned))) / images
+        grad_heat = jnp.sum(grad_logits * cosine * heat, axis=1, keepdims=True)
+        grad_offset = jnp.sum(grad_logits, axis=1, keepdims=True)
+        grad_cosine = jnp.broadcast_to(grad_logits * heat, (16, cosine.shape[1])).astype(jnp.bfloat16)
+        grad_unit = dot(grad_cosine, self.cap[...])[0:1]
+        grad_embed = rate * grad_unit - embed * (
+            rate * rate * rate * jnp.sum(grad_unit * embed, axis=1, keepdims=True)
+        )
+        grad_many = jnp.broadcast_to(grad_embed, (16, D)).astype(jnp.bfloat16)
+        grad_pooled = dot(grad_many, w_out, NT).astype(jnp.bfloat16).astype(jnp.float32)
+        heads_grad = jnp.where(own, grad_pooled, 0.0).astype(jnp.bfloat16)
+        grad_probs = dot(heads_grad, values, NT)
+        centre = jnp.sum(probs * grad_probs, axis=1, keepdims=True)
+        grad_scores = (probs * (grad_probs - centre)).astype(jnp.bfloat16)
+        query_spread = dot(grad_scores, keys) * SCALE
+        grad_query = jnp.sum(jnp.where(own, query_spread, 0.0), axis=0, keepdims=True)
+        self.small_own[0:1, :] = pooled_b.astype(jnp.float32)
+        self.small_own[1:2, :] = grad_many[0:1].astype(jnp.float32)
+        self.small_own[2:3, :] = grad_query
+        lane = lax.broadcasted_iota(jnp.int32, (1, D), 1)
+        self.small_own[3:4, :] = jnp.where(
+            lane == 0, loss, jnp.where(lane == 1, grad_heat, jnp.where(lane == 2, grad_offset, 0.0))
+        )
+        self.small_own[4:8, :] = jnp.zeros((4, D), jnp.float32)
+        self.kvp[:, :D] = (dot(grad_scores, heads_query, TN) * SCALE).astype(jnp.bfloat16)
+        both_probs = jnp.concatenate([probs_high, probs_low], axis=0)
+        both_grads = jnp.concatenate([heads_grad, heads_grad], axis=0)
+        self.kvp[:, D:] = dot(both_probs, both_grads, TN).astype(jnp.bfloat16)
+
+    def turn(self, source):
+        def body(index):
+            self.turned[columns(index), :] = jnp.transpose(source[:, columns(index)])
+
+        loop(3, body)
+
+    def weight_grad(self, first, source, tiles, plan=None):
+        def body(index):
+            self.w[:, columns(index, first)] = dot(
+                self.turned[...], source[:, columns(index)]
+            ).astype(jnp.bfloat16)
+
+        loop(tiles, body, plan)
+
+    def input_grad(self, source, first, width, plan=None):
+        def body(index):
+            self.acc[:, columns(index)] = dot(
+                source[...], self.w[columns(index), first : first + width], NT
+            )
+
+        loop(3, body, plan)
+
+    def norm_back(self, source, added, number, out, rounded):
+        gain = self.vec[2 * number : 2 * number + 1, :]
+
+        def body(index, carry):
+            rows = chunk_rows(index)
+            scaled, rate = normalize(source[rows, :].astype(jnp.float32))
+            grad, grad_gain, grad_bias = normalize_back(scaled, rate, self.acc[rows, :], gain)
+            if added is not None:
+                grad = grad + added[rows, :]
+            if out is not None:
+                out[rows, :] = grad
+            rounded[rows, :] = grad.astype(jnp.bfloat16)
+            return carry[0] + grad_gain, carry[1] + grad_bias
+
+        zero = jnp.zeros((1, D), jnp.float32)
+        grad_gain, grad_bias = lax.fori_loop(0, TOKENS // CHUNK, body, (zero, zero))
+        self.vec_grad[2 * number : 2 * number + 1, :] = grad_gain
+        self.vec_grad[2 * number + 1 : 2 * number + 2, :] = grad_bias
+
+    def pool_back(self, plan=None, after=None):
+        self.input_grad(self.kvp, COL_MAP_KV, 2 * D)
+        self.turn(self.f)
+        self.weight_grad(COL_MAP_KV, self.kvp, 6, plan)
+        if after is not None:
+            after()
+        self.norm_back(self.y, None, 2, self.y, self.f)
+
+    def down_back(self, plan=None):
+        self.turn(self.f)
+
+        def body(index):
+            here = columns(index)
+            grad = dot(self.f[...], self.w[:, columns(index, COL_DOWN)])
+            self.gp[:, here] = (grad * self.gp[:, here].astype(jnp.float32)).astype(jnp.bfloat16)
+            self.w[:, columns(index, COL_DOWN)] = dot(self.turned[...], self.g[:, here]).astype(
+                jnp.bfloat16
+            )
+
+        loop(12, body, plan)
+
+    def up_input(self, plan=None):
+        self.input_grad(self.gp, COL_UP, FF, plan)
+
+    def up_weight(self, plan=None):
+        self.turn(self.h2)
+        self.weight_grad(COL_UP, self.gp, 12, plan)
+
+    def up_norm(self):
+        self.norm_back(self.r, self.y, 1, self.r, self.f)
+
+    def out_back(self, plan=None):
+        self.turn(self.a)
+
+        def body(index):
+            self.a[:, columns(index)] = dot(
+                self.f[...], self.w[columns(index), COL_OUT : COL_OUT + D], NT
+            ).astype(jnp.bfloat16)
+
+        loop(3, body)
+        self.weight_grad(COL_OUT, self.f, 3, plan)
+
+    def attend_back(self, plan=None):
+        lanes = lax.broadcasted_iota(jnp.int32, (TOKENS, 128), 1)
+
+        def body(pair):
+            queries = self.pair_of(pair, 0) * jnp.bfloat16(SCALE)
+            keys, values = self.pair_of(pair, 1), self.pair_of(pair, 2)
+            grads = self.a[:, columns(pair, 0, 128)]
+            keys_turned = jnp.transpose(keys)
+            grad_queries = []
+            grad_keys = None
+            for head in range(2):
+                mine = (lanes < 64) if head == 0 else (lanes >= 64)
+                masked = jnp.where(mine, queries, jnp.bfloat16(0))
+                masked_grads = jnp.where(mine, grads, jnp.bfloat16(0))
+                scores = dot(keys, masked, NT)
+                probs = jnp.exp(scores - self.lse[pl.ds(pair * 2 + head, 1), :])
+                value_part = dot(probs.astype(jnp.bfloat16), masked_grads)
+                grad_probs = dot(values, masked_grads, NT)
+                centre = jnp.sum(probs * grad_probs, axis=0, keepdims=True)
+                grad_scores = (probs * (grad_probs - centre)).astype(jnp.bfloat16)
+                key_part = dot(grad_scores, masked)
+                grad_queries.append(dot(keys_turned[head * 64 : head * 64 + 64], grad_scores))
+                if head == 0:
+                    grad_keys, grad_values = key_part, value_part
+                else:
+                    grad_keys, grad_values = grad_keys + key_part, grad_values + value_part
+            self.qkv[:, columns(pair, 0, 128)] = (
+                jnp.transpose(jnp.concatenate(grad_queries, axis=0)) * SCALE
+            ).astype(jnp.bfloat16)
+            self.qkv[:, columns(pair, D, 128)] = grad_keys.astype(jnp.bfloat16)
+            self.qkv[:, columns(pair, 2 * D, 128)] = grad_values.astype(jnp.bfloat16)
+
+        loop(6, body, plan)
+
+    def project_input(self, plan=None):
+        self.first_norm()
+        self.input_grad(self.qkv, 0, 3 * D, plan)
+        self.turn(self.h)
+        self.norm_back(self.x, self.r, 0, None, self.h)
+
+    def project_weight(self, start, tiles, plan=None):
+        def body(index):
+            self.w[:, columns(index, start * TILE)] = dot(
+                self.turned[...], self.qkv[:, columns(index, start * TILE)]
+            ).astype(jnp.bfloat16)
+
+        loop(tiles, body, plan)
+
+    def vectors_back(self):
+        packed = jnp.concatenate([self.vec_grad[...], jnp.zeros((120, D), jnp.float32)], axis=0)
+        self.w[:, COL_VECTORS : COL_VECTORS + 128] = jnp.transpose(packed).astype(jnp.bfloat16)
+        self.w[:, COL_QUERY : COL_QUERY + 128] = jnp.zeros((D, 128), jnp.bfloat16)
+
+
+def spread_steps(steps, count):
+    plan = {}
+    for at, step in enumerate(steps):
+        plan.setdefault(min(count - 1, at * count // max(len(steps), 1)), []).append(step)
+    return plan
+
+
+TOWER_REFS = (
+    ("w", "x", "cap", "h", "qkv", "a", "r", "h2", "g", "gp", "y", "f", "kvp", "lse", "turned", "acc", "vec", "vec_grad", "small_own")
+)
+
+
+def layer_kernel(
+    master, tokens, captions, vectors, labels, scalars,
+    share_out, vector_out, facts, patch_out, *scratch,
+):
+    p = Place()
+    t = Tower(**dict(zip(TOWER_REFS, scratch)))
+    scratch = scratch[len(TOWER_REFS) :]
+    stage, small, pair_a, pair_b, b_in, z_in, a_in, last, mine, everyone = scratch[:10]
+    share, extra, caps, map_q, map_out, map_q_share, signs = scratch[10:17]
+    swap_sems, token_sems, patch_sems, own_sems, send_sem, recv_sem, grant = scratch[17:24]
+    gather_s, scatter_s = scratch[24:31], scratch[31:]
+    map_q_at = 4 * D + 2 * FF
+    map_q_copy = pltpu.make_async_copy(
+        master.at[:, map_q_at : map_q_at + D], map_q, own_sems.at[0]
+    )
+    map_q_copy.start()
+    greet_all(p)
+
+    count = len(GATHER_SECTIONS)
+    gathers, swaps = [], []
+    pieces = (
+        (master, 0, 0, 3 * D),
+        (extra, 0, 3 * D, 256),
+        (master, 3 * D, COL_OUT, D + 2 * FF),
+        (master, map_q_at + D, COL_MAP_KV, 3 * D),
+    )
+    for number, (first, width) in enumerate(GATHER_SECTIONS):
+        swaps.append(
+            Swap(p, pieces, stage, 0, 24, first, width, first // 2, swap_sems.at[number])
+        )
+        swaps[-1].begin((extra, False))
+        gathers.append(Gather(p, t.w, CHIP_ROWS, first, width, [s.at[number] for s in gather_s]))
+    own_vectors = vectors[...].astype(jnp.bfloat16).astype(jnp.float32)
+    map_q_copy.wait()
+    map_q[...] = map_q[...].astype(jnp.bfloat16).astype(jnp.float32)
+    part = jnp.sum(own_vectors[:, 6:7] * map_q[...], axis=0, keepdims=True)
+    high = part.astype(jnp.bfloat16).astype(jnp.float32)
+    for side in range(6):
+        lanes = slice(side * 128, side * 128 + 128)
+        extra[side : side + 1, 128:256] = high[:, lanes]
+        extra[6 + side : 7 + side, 128:256] = (part - high)[:, lanes]
+    extra[12:24, 128:256] = jnp.zeros((12, 128), jnp.float32)
+    extra[:, 0:128] = jnp.concatenate([own_vectors, jnp.zeros((24, 121), jnp.float32)], axis=1)
+    swaps[0].begin((extra, True))
+    each = captions.shape[0]
+    caps[...] = jnp.concatenate(
+        [unit_rows(captions[...].astype(jnp.float32)), jnp.zeros((64 - each, D), jnp.float32)], axis=0
+    ).astype(jnp.bfloat16)
+    own_caps = caps.at[pl.ds(aligned(p.blk * 16, 16), 16), :]
+    swaps.append(
+        Swap(p, ((own_caps, 0, 0, D),), t.cap, p.chip * 32, 16, 0, D, None, swap_sems.at[count])
+    )
+    swaps[-1].begin()
+    gathers.append(Gather(p, t.cap, 32, 0, D, [s.at[count] for s in gather_s]))
+    token_copies = []
+    for step in range(1, 4):
+        to = lax.rem(p.blk + step, 4)
+        token_copies.append(
+            remote(
+                tokens.at[to],
+                t.x.at[pl.ds(aligned(p.blk * 144, 144), 144), :],
+                token_sems.at[0, step - 1],
+                token_sems.at[1, step - 1],
+                {"blk": to},
+            )
+        )
+        token_copies[-1].start()
+    own_tokens = pltpu.make_async_copy(
+        tokens.at[p.blk], t.x.at[pl.ds(aligned(p.blk * 144, 144), 144), :], token_sems.at[0, 3]
+    )
+    own_tokens.start()
+
+    def ready(number):
+        swaps[number].finish()
+        if number < count:
+            first, width = GATHER_SECTIONS[number]
+            t.w[
+                pl.ds(aligned(p.chip * 48, 48), 48), pl.ds(gathers[number].mine, width // 2)
+            ] = stage[:, first // 2 : first // 2 + width // 2].astype(jnp.bfloat16)
+        gathers[number].begin()
+
+    order = []
+    for number, gather in enumerate(gathers):
+        for at, step in enumerate(gather.steps()):
+            call = step if at else (lambda number=number: ready(number))
+            order.append((gather_key(number, at), number, at, call))
+    order.sort(key=lambda entry: entry[:3])
+    ends = [
+        max(i for i, entry in enumerate(order) if entry[1] <= number)
+        for number in range(count + 1)
+    ]
+
+    def between(number):
+        return [entry[3] for entry in order[ends[number - 1] + 1 : ends[number] + 1]]
+
+    for entry in order[: ends[0] + 1]:
+        entry[3]()
+    slot = lax.broadcasted_iota(jnp.int32, (8 * each, 512), 1)
+    within = (slot >> 7) * 16 + (slot & 15)
+    source = ((slot >> 5) & 3) * (2 * each) + ((slot >> 4) & 1) * each + within
+    label = lax.broadcasted_iota(jnp.int32, (8 * each, 512), 0)
+    pick = ((label == source) & (within < each)).astype(jnp.float32).astype(jnp.bfloat16)
+    row = 2.0 * labels[pl.ds(p.blk, 1), :].astype(jnp.float32) - 1.0
+    signs[...] = dot(jnp.broadcast_to(row, (16, 8 * each)).astype(jnp.bfloat16), pick)
+    for step in range(3):
+        source = lax.rem(p.blk + 3 - step, 4)
+        landed = t.x.at[pl.ds(aligned(source * 144, 144), 144), :]
+        remote(
+            landed, landed, token_sems.at[0, step], token_sems.at[1, step], {"blk": source}
+        ).wait_recv()
+    own_tokens.wait()
+    gathers[0].finish()
+
+    t.unpack()
+    t.first_norm()
+    t.project()
+    t.attend(spread_steps(between(1), 6))
+    gathers[1].finish()
+    t.attend_out()
+    t.feed_up(spread_steps(between(2), 12))
+    gathers[2].finish()
+    t.feed_down(spread_steps(between(3), 3))
+    gathers[3].finish()
+    t.pool_project(spread_steps(between(4), 6))
+    gathers[4].finish()
+    t.vec_grad[...] = jnp.zeros((8, D), jnp.float32)
+    images = tokens.shape[0] * 8
+    t.pool(signs[0:1, :], jnp.full((1, 512), scalars[0], jnp.float32), scalars[1], images)
+    swap = Swap(
+        p, ((t.small_own, 0, 0, D),), small, p.chip * 16, 8, 0, D, None, swap_sems.at[count + 1]
+    )
+    swap.begin()
+    small_gather = Gather(p, small, 16, 0, D, [s.at[count + 1] for s in gather_s])
+    small_steps = small_gather.steps()
+    for gather in gathers:
+        gather.sent()
+    for copy in token_copies:
+        copy.wait_send()
+
+    sections = []
+    for number, (first, width, z_first) in enumerate(SCATTER_SECTIONS):
+        half = width // 2
+        rest = (number - 3) * 640
+        bufs = (
+            (pair_b if number in (1, 3, 4) else pair_a).at[
+                :, (half if number == 4 else 0) : (2 * half if number == 4 else half)
+            ],
+            b_in[number] if number < 3 else t.g.at[0:384, rest : rest + half],
+            z_in[number]
+            if number < 2
+            else (t.gp.at[:, 0:half] if number == 2 else t.g.at[0:288, 1280 + rest : 1280 + rest + half]),
+            a_in[number] if number < 3 else t.g.at[384:576, rest : rest + half],
+            last[number],
+        )
+        sections.append(
+            Scatter(p, t.w, share, first, width, z_first, bufs, [s.at[number] for s in scatter_s])
+        )
+    pool_part, down_part, up_part, front_part, end_part = sections
+
+    def small_begin():
+        swap.finish()
+        small_steps[0]()
+
+    links, program = Links(*LINK_SPEED), Program()
+    timed = []
+
+    def leaves(section, number):
+        timed.append((section, program.now, SCATTER_SECTIONS[number][1]))
+
+    leaves(pool_part, 0)
+    program.want(zip((0.5, 1.5, 4.5, 7.0, 9.5, 12.0), [small_begin] + small_steps[1:]))
+    program.gap(2.0)
+    program.loop("down", 12, 0.75)
+    leaves(down_part, 1)
+    program.loop("up_input", 3, 1.4)
+    program.loop("up_weight", 12, 0.46)
+    program.gap(1.7)
+    program.loop("out", 3, 1.1)
+    leaves(up_part, 2)
+    program.loop("attend", 6, 2.05)
+    program.gap(1.0)
+    program.loop("project_input", 3, 1.0)
+    program.gap(2.2)
+    program.loop("front", 5, 0.5)
+    leaves(front_part, 3)
+    program.loop("end", 4, 0.5)
+    program.gap(1.0)
+    leaves(end_part, 4)
+    for entry in timed:
+        program.want(links.steps(*entry))
+    program.settle()
+    plans = program.plans
+    t.pool_back(None, pool_part.begin)
+    t.down_back(plans["down"])
+    down_part.begin()
+    t.up_input(plans["up_input"])
+    t.up_weight(plans["up_weight"])
+    near = (p.z < 3).astype(jnp.int32) + (p.z > 0).astype(jnp.int32)
+    for device in (p.sibling, p.a_near, p.b_near):
+        pl.semaphore_signal(grant, inc=1, device_id=device, device_id_type=MESH)
+    pl.when(p.z < 3)(
+        lambda: pl.semaphore_signal(grant, inc=1, device_id=p.up, device_id_type=MESH)
+    )
+    pl.when(p.z > 0)(
+        lambda: pl.semaphore_signal(grant, inc=1, device_id=p.down, device_id_type=MESH)
+    )
+    t.up_norm()
+    t.out_back(plans["out"])
+    pl.semaphore_wait(grant, 3 + near)
+    up_part.begin()
+    t.attend_back(plans["attend"])
+    t.project_input(plans["project_input"])
+    patch_copies = []
+    for step in range(1, 4):
+        to = lax.rem(p.blk + step, 4)
+        patch_copies.append(
+            remote(
+                t.h.at[pl.ds(aligned(to * 144, 144), 144), :],
+                patch_out.at[p.blk],
+                patch_sems.at[0, step - 1],
+                patch_sems.at[1, step - 1],
+                {"blk": to},
+            )
+        )
+        patch_copies[-1].start()
+    own_patch = pltpu.make_async_copy(
+        t.h.at[pl.ds(aligned(p.blk * 144, 144), 144), :], patch_out.at[p.blk], patch_sems.at[0, 3]
+    )
+    own_patch.start()
+    t.project_weight(0, 5, plans["front"])
+    front_part.begin()
+    t.project_weight(5, 4, plans["end"])
+    t.vectors_back()
+    end_part.begin()
+    for step in program.tail:
+        step()
+    for section in sections:
+        section.finish()
+    outs = [
+        pltpu.make_async_copy(
+            share.at[:, source : source + width],
+            share_out.at[:, target : target + width],
+            own_sems.at[1 + number],
+        )
+        for number, (source, target, width) in enumerate(
+            (
+                (0, 0, 3 * D),
+                (COL_OUT, 3 * D, D + 2 * FF),
+                (COL_MAP_KV, map_q_at + D, 2 * D),
+            )
+        )
+    ]
+    for out in outs:
+        out.start()
+    small_gather.finish()
+    small_gather.sent()
+    for step, copy in enumerate(patch_copies):
+        source = lax.rem(p.blk + 3 - step, 4)
+        landed = patch_out.at[source]
+        remote(
+            landed, landed, patch_sems.at[0, step], patch_sems.at[1, step], {"blk": source}
+        ).wait_recv()
+        copy.wait_send()
+    own_patch.wait()
+    spread = Spread(p, mine, everyone, send_sem, recv_sem)
+    tail = small_tail(p, small, map_q[...], own_vectors[:, 6:7], share, spread, map_out, map_q_share)
+    for number, (source, target) in enumerate(((map_q_share, map_q_at), (map_out, map_q_at + 3 * D))):
+        outs.append(
+            pltpu.make_async_copy(
+                source, share_out.at[:, target : target + D], own_sems.at[4 + number]
+            )
+        )
+        outs[-1].start()
+    lane = lax.broadcasted_iota(jnp.int32, (24, 128), 1)
+    vector_out[...] = jnp.where(lane == 6, tail, share[:, COL_VECTORS : COL_VECTORS + 128])
+    sums, norm = spread.finish()
+    facts[...] = jnp.concatenate([jnp.broadcast_to(sums[:, :128], (7, 128)), norm[:1]], axis=0)
+    for out in outs:
+        out.wait()
+
+
+def layer_call(master, tokens, captions, vectors, labels, scalars):
+    dma = pltpu.SemaphoreType.DMA
+    f32 = jnp.float32
+    gathers = len(GATHER_SECTIONS) + 2
+    count = len(SCATTER_SECTIONS)
+    widths = [entry[1] // 2 for entry in SCATTER_SECTIONS]
+
+    def vm(*shape, dt=jnp.bfloat16):
+        return pltpu.VMEM(shape, dt)
+
+    vmem = pl.BlockSpec(memory_space=pltpu.VMEM)
+    return pl.pallas_call(
+        layer_kernel,
+        out_shape=(
+            jax.ShapeDtypeStruct((24, 8 * D + 2 * FF), f32),
+            jax.ShapeDtypeStruct((24, 128), f32),
+            jax.ShapeDtypeStruct((8, 128), f32),
+            jax.ShapeDtypeStruct((4, 144, D), jnp.bfloat16),
+        ),
+        in_specs=[
+            pl.BlockSpec(memory_space=pl.ANY),
+            pl.BlockSpec(memory_space=pl.ANY),
+            vmem,
+            vmem,
+            vmem,
+            pl.BlockSpec(memory_space=pltpu.SMEM),
+        ],
+        out_specs=(
+            pl.BlockSpec(memory_space=pl.ANY),
+            vmem,
+            vmem,
+            pl.BlockSpec(memory_space=pl.ANY),
+        ),
+        scratch_shapes=[
+            vm(D, GATHER_COLS),
+            vm(TOKENS, D),
+            vm(512, D),
+            vm(TOKENS, D),
+            vm(TOKENS, 3 * D),
+            vm(TOKENS, D),
+            vm(TOKENS, D, dt=f32),
+            vm(TOKENS, D),
+            vm(TOKENS, FF),
+            vm(TOKENS, FF),
+            vm(TOKENS, D, dt=f32),
+            vm(TOKENS, D),
+            vm(TOKENS, 2 * D),
+            vm(16, TOKENS, dt=f32),
+            vm(D, TOKENS),
+            vm(TOKENS, D, dt=f32),
+            vm(16, D, dt=f32),
+            vm(8, D, dt=f32),
+            vm(8, D, dt=f32),
+            vm(48, GATHER_COLS // 2, dt=f32),
+            vm(256, D, dt=f32),
+            vm(D, widths[2]),
+            vm(D, widths[1]),
+            [vm(384, w) for w in widths[:3]],
+            [vm(576, widths[0]), vm(288, widths[1])],
+            [vm(48, widths[0]), vm(192, widths[1]), vm(48, widths[2])],
+            [vm(48, w, dt=f32) for w in widths],
+            vm(8, 128, dt=f32),
+            vm(31, 8, 128, dt=f32),
+            vm(24, SCATTER_COLS, dt=f32),
+            vm(24, 256, dt=f32),
+            vm(64, D),
+            vm(24, D, dt=f32),
+            vm(24, D, dt=f32),
+            vm(24, D, dt=f32),
+            vm(16, 512, dt=f32),
+            dma((gathers, 4)),
+            dma((2, 4)),
+            dma((2, 4)),
+            dma((6,)),
+            dma,
+            dma,
+            pltpu.SemaphoreType.REGULAR,
+            *gather_sems(gathers),
+            dma((count, 2)),
+            dma((count, 2, 2)),
+            dma((count, 2, 2, 3)),
+            dma((count, 2, 2, 3)),
+            dma((count, 2)),
+            dma((count, 2)),
+        ],
+        compiler_params=pltpu.CompilerParams(
+            collective_id=0, has_side_effects=True, vmem_limit_bytes=63 * 2**20
+        ),
+        name="layer_step",
+    )(master, tokens, captions, vectors, labels, scalars)
+
+
+def local_kernel(
+    patch_tokens,
+    captions,
+    pair_labels,
+    master_weights,
+    first_moments,
+    second_moments,
+    master_vectors,
+    vector_first,
+    vector_second,
+    loss_scalars,
+    scalar_first,
+    scalar_second,
+):
+    weight_share, vector_share, facts, patch_grad = layer_call(
+        master_weights, patch_tokens, captions, master_vectors, pair_labels, loss_scalars
+    )
+    vector_share = vector_share[:, :7]
+    patch_grad = patch_grad.astype(jnp.float32)
+    loss_total, scalar_total, grad_norm = facts[0, 0], facts[0, 1:3], facts[7, 0]
+    factor = CLIP_AT / jnp.maximum(grad_norm, CLIP_AT)
+    new_w, new_wm, new_wv = adamw(
+        master_weights, weight_share * factor, first_moments, second_moments, 0.03, 0.1
+    )
+    new_v, new_vm, new_vv = adamw(
+        master_vectors, vector_share * factor, vector_first, vector_second, 0.3, 0.0
+    )
+    new_s, new_sm, new_sv = adamw(
+        loss_scalars, scalar_total * factor, scalar_first, scalar_second, 0.3, 0.0
+    )
+    return (
+        loss_total,
+        grad_norm,
+        patch_grad,
+        new_w,
+        new_wm,
+        new_wv,
+        new_w.astype(jnp.bfloat16),
+        new_v,
+        new_vm,
+        new_vv,
+        new_v.astype(jnp.bfloat16),
+        new_s,
+        new_sm,
+        new_sv,
+    )
+
+
 def solution(mesh):
     in_specs = (
         P("img", "blk", None),
@@ -376,4 +1698,5 @@
         P(),
         P(),
     )
-    return jax.shard_map(local, mesh=mesh, in_specs=in_specs, out_specs=out_specs, check_vma=False)
+    body = local_kernel if tuple(mesh.shape.values()) == (4, 8) else local
+    return jax.shard_map(body, mesh=mesh, in_specs=in_specs, out_specs=out_specs, check_vma=False)

time: 887 us -> 273 us (0.31)
  waiting for transfers between devices: 353 us -> 0 us
  blocking collectives: 264 us -> 0 us
  Pallas kernels: 0 us -> 257 us
  matrix products: 140 us -> 0 us
  other arithmetic: 61.8 us -> 8.36 us
  local copies, waits for them, and re-layouts: 30.9 us -> 5.5 us
  between operations: 22.8 us -> 1.39 us
  starting transfers between devices: 9.14 us -> 0 us
    reduce_scatter x4 -> x0, waiting for transfers between devices: 263 us -> none  [scatter(): lax.psum_scatter(part.astype(jnp.bfloat16), both, scatter_dimension=0, ti...]
    pallas_call x0 -> x1, Pallas kernels: none -> 257 us  [layer_call(): pl.pallas_call(layer_kernel, out_shape=(jax.ShapeDtypeStruct((24, 8 * D +...]
    all_gather x4 -> x0, blocking collectives: 140 us -> none  [the longest x1 41.6 us: local(): lax.all_gather(pooled_heads_b, both, axis=0, tiled=True)]
    dot_general x32 -> x0, matrix products: 140 us -> none  [the longest x1 12 us: attend_back(): jnp.einsum('iqhe,ikhe->ihqk', grad_mixed, values_all, preferred_element_t...]
    psum x3 -> x0, blocking collectives: 124 us -> none  [the longest x1 46.7 us: local(): lax.psum(jnp.dot(own_vectors[:, 6], own_map_q, preferred_element_type=jnp...]
    all_gather x4 -> x0, waiting for transfers between devices: 88 us -> none  [gather(): return lax.all_gather(rounded[:, start:stop], both, axis=0, tiled=True)]
    reduce_sum x18 -> x0, other arithmetic: 21.4 us -> none  [the longest x1 9.13 us: attend(): row_sum = jnp.sum(expos, axis=-1, keepdims=True)]
    convert_element_type x11 -> x3, other arithmetic: 21.7 us -> 7.08 us  [the longest x1 5 us: local_kernel(): new_w.astype(jnp.bfloat16)]
  transfers between devices with their start and end apart: 10 -> 0, of which waited for: 5 -> 0; matrix products, arithmetic and copies ran while one was open for 13% -> 0% of each run, Pallas kernels for 0% -> 0%
where the time goes in v3:
time: 273 us; the launch traced here: 272 us
  Pallas kernels  257 us (94%)
  other arithmetic  8.36 us (3%)
  local copies, waits for them, and re-layouts  5.5 us (2%)
    pallas_call x1, Pallas kernels, layer_call(): pl.pallas_call(layer_kernel, out_shape=(jax.ShapeDtypeStruct((24, 8 * D +...  257 us

profile of v3, /device:TPU:0, one launch (start us, length us, event | category | flops | bytes accessed | tf_op | source)
XLA Modules:
  0.0 272.5 jit_solution(12467317493769114873)
XLA Ops:
  0.6 0.0 copy-start.2
  0.7 0.0 copy-start.3
  0.7 1.4 copy.35.vectors
  2.0 0.0 copy-start.1
  2.0 257.2 %layer_step.1 = (f32[24,12288]{1,0:T(8,128)}, f32[24,128]{1,0:T(8,128)}, f32[8,128]{1,0:T(8,128)}, bf16[4,144,768]{2,1,0:T(8,128)(2,1)}) custom-call(f32[24,12288]{1,0:T(8,128)} %master.1, bf16[4,144,768]{2,1,0:T(8,128)(2,1)} %tokens.1, bf16[50,768]{1,0:T(8,128)(2,1)} %captions.1, f32[24,7]{1,0:T(8,128)} %copy.35.vectors, s32[4,400]{1,0:T(4,128)} %labels.1, ...), custom_call_target="tpu_custom_call" | custom-call | tf_op jit(solution)/shard_map/layer_step/pallas_call | solution.py:1541
  259.3 1.3 fusion.10
  261.2 0.0 copy-done.2
  261.3 0.1 copy.36
  261.3 0.0 copy-done.3
  261.3 0.1 copy.38
  261.4 0.0 copy-done.1
  261.4 0.7 fusion.6
  262.2 0.7 copy.41
  262.8 0.7 copy.42
  263.5 0.7 copy.43
  264.2 0.7 copy.44
  264.8 0.0 copy-start.4
  264.8 0.0 copy-start.5
  264.8 0.0 copy-start.6
  264.8 0.0 copy-start
  264.9 5.0 %fusion.8 = (bf16[24,12288]{1,0:T(8,128)(2,1)}, f32[24,12288]{1,0:T(8,128)}, f32[24,12288]{1,0:T(8,128)}, f32[24,12288]{1,0:T(8,128)}) fusion(f32[24,12288]{1,0:T(8,128)} %master.1, f32[24,12288]{1,0:T(8,128)} %get-tuple-element.20, f32[]{:T(128)S(6)} %div.42, f32[24,12288]{1,0:T(8,128)} %param.16, f32[24,12288]{1,0:T(8,128)} %param.17), kind=kLoop, calls=%fused_computation.16 | loop fusion | flops 5013504 | bytes 8847364 | tf_op jit(solution)/shard_map/convert_element_type | solution.py:1659
  269.8 0.0 copy-done.4
  269.8 0.0 copy-done.5
  269.9 0.0 copy-done.6
  269.9 1.3 multiply_subtract_fusion.2
  271.1 0.0 copy-done
  271.1 1.4 convert_element_type.9
Async XLA Ops:
  0.6 260.6 %copy-start.2 = (f32[24,7]{0,1:T(8,128)S(1)}, f32[24,7]{0,1:T(8,128)}, u32[]{:S(2)}) copy-start(f32[24,7]{0,1:T(8,128)} %param.19) | copy-start | bytes 2020
  0.7 260.7 %copy-start.3 = (f32[24,7]{0,1:T(8,128)S(1)}, f32[24,7]{0,1:T(8,128)}, u32[]{:S(2)}) copy-start(f32[24,7]{0,1:T(8,128)} %param.20) | copy-start | bytes 2020
  2.0 259.4 %copy-start.1 = (f32[24,7]{1,0:T(8,128)S(1)}, f32[24,7]{1,0:T(8,128)}, u32[]{:S(2)}) copy-start(f32[24,7]{1,0:T(8,128)} %copy.35.vectors) | copy-start | bytes 2020
  264.8 5.0 %copy-start.4 = (f32[2]{0:T(128)S(1)}, f32[2]{0:T(128)}, u32[]{:S(2)}) copy-start(f32[2]{0:T(128)} %scalars.1) | copy-start | bytes 28
  264.8 5.0 %copy-start.5 = (f32[2]{0:T(128)S(1)}, f32[2]{0:T(128)}, u32[]{:S(2)}) copy-start(f32[2]{0:T(128)} %param.22) | copy-start | bytes 28
  264.8 5.0 %copy-start.6 = (f32[2]{0:T(128)S(1)}, f32[2]{0:T(128)}, u32[]{:S(2)}) copy-start(f32[2]{0:T(128)} %param.23) | copy-start | bytes 28
  264.8 6.3 %copy-start = (bf16[4,144,768]{2,1,0:T(8,128)(2,1)S(1)}, bf16[4,144,768]{2,1,0:T(8,128)(2,1)}, u32[]{:S(2)}) copy-start(bf16[4,144,768]{2,1,0:T(8,128)(2,1)} %get-tuple-element.19) | copy-start | bytes 2654212

commit v4 on v3

--- a/solution.py
+++ b/solution.py
@@ -349,7 +349,7 @@
     )
 
 
-LINK_SPEED = (1.0, 2.0)
+LINK_SPEED = (1.1, 3.0)
 
 
 def gather_key(number, at):
@@ -360,12 +360,17 @@
 CHIP_ROWS = 48
 GATHER_SECTIONS = ((0, 2560), (2560, 3840), (6400, 3072), (9472, 2304))
 SCATTER_SECTIONS = (
-    (9472, 1536, True),
-    (6400, 3072, False),
-    (2560, 3840, True),
-    (0, 1280, False),
-    (1280, 1280, False),
+    (9472, 1536),
+    (6400, 1536),
+    (7936, 1536),
+    (3328, 1536),
+    (4864, 1536),
+    (2560, 768),
+    (0, 1280),
+    (1280, 1280),
 )
+PAIR_PLACES = ((0, 0), (0, 768), (1, 0), (1, 768), (0, 0), (0, 1536), (0, 768), (1, 0))
+LATE_PLACES = (0, 768, 1152, 1792)
 GATHER_COLS = 11776
 SCATTER_COLS = 11008
 
@@ -388,6 +393,9 @@
         self.down = {"img": self.img - 2}
         self.a_near = {"blk": self.block(1, 0)}
         self.b_near = {"blk": self.block(0, 1)}
+
+    def on_level(self, level):
+        return {"img": level * 2 + self.c}
 
     def block(self, da, db):
         flip_x = da * (1 - self.c) + db * self.c
@@ -542,14 +550,12 @@
 
 
 class Scatter:
-    def __init__(self, place, buf, share, first, width, z_first, bufs, sems):
+    def __init__(self, place, buf, share, first, width, bufs, sems):
         self.p, self.buf, self.share, self.half = place, buf, share, width // 2
-        self.z_first = z_first
-        self.sides = 2 if z_first else 1
         self.mine = aligned(first + place.c * self.half, 128)
         self.theirs = aligned(first + (1 - place.c) * self.half, 128)
-        self.pair_in, self.b_in, self.z_in, self.a_in, self.last = bufs
-        self.pair, self.b_sem, self.z_send, self.z_recv, self.a_sem, self.end = sems
+        self.pair_in, self.b_in, self.a_in, self.z_in, self.last = bufs
+        self.pair, self.b_sem, self.a_sem, self.z_sem, self.end = sems
 
     def run_rows(self, da, db):
         return aligned(self.p.block(da, db) * 192, 192)
@@ -593,21 +599,18 @@
             self.p.b_near,
         )
 
-    def z_slot(self, da, level, up):
-        return aligned(((up * self.sides + da) * 3 + level - up) * 48, 48)
-
-    def z_copy(self, da, level, up):
+    def a_copy(self):
+        return remote(self.run(1, 0), self.a_in, self.a_sem.at[0], self.a_sem.at[1], self.p.a_near)
+
+    def z_copy(self, step):
+        level = lax.rem(self.p.z + step, 4)
         return remote(
-            self.part(da, level),
-            self.z_in.at[pl.ds(self.z_slot(da, level, up), 48), :],
-            self.z_send.at[up, da, level - up],
-            self.z_recv.at[up, da, level - up],
-            self.p.up if up else self.p.down,
-        )
-
-    def a_copy(self):
-        source = self.part(1, self.p.z) if self.z_first else self.run(1, 0)
-        return remote(source, self.a_in, self.a_sem.at[0], self.a_sem.at[1], self.p.a_near)
+            self.part(0, level),
+            self.z_in.at[(3 - step) * 48 : (4 - step) * 48, :],
+            self.z_sem.at[0, 3 - step],
+            self.z_sem.at[1, 3 - step],
+            self.p.on_level(level),
+        )
 
     def end_copy(self):
         return remote(
@@ -637,41 +640,21 @@
         for da in (1, 0):
             self.b_copy(da).wait_recv()
             self.add(self.run_rows(da, 0), self.b_in, 4, da * 192)
-            if da == 1 and not self.z_first:
+            if da == 1:
                 self.a_copy().start()
-
-    def z_step(self, da, level, up, holds, takes, gives):
-        @pl.when(holds)
-        def step():
-            copy = self.z_copy(da, level, up)
-
-            @pl.when(takes)
-            def take():
-                copy.wait_recv()
-                self.add(self.level_rows(da, level), self.z_in, 1, self.z_slot(da, level, up))
-
-            if gives:
-                copy.start()
-
-    def levels(self, slot):
-        z = self.p.z
-        for da in range(self.sides):
-            self.z_step(da, 3 - slot + z, 1, (z <= slot) & (z >= slot - 2), z >= 1, slot < 3)
-            self.z_step(da, slot - 3 + z, 0, (z >= 3 - slot) & (z <= 5 - slot), z <= 2, slot < 3)
-
-    def across(self):
-        self.a_copy().start()
 
     def joined(self):
         self.a_copy().wait_recv()
         self.add(self.run_rows(0, 0), self.a_in, 4)
+        for step in (2, 1, 3):
+            self.z_copy(step).start()
 
     def close(self):
-        rows = self.level_rows(0, self.p.z)
-        total = self.buf[pl.ds(rows, 48), pl.ds(self.mine, self.half)].astype(jnp.float32)
-        if self.z_first:
-            self.a_copy().wait_recv()
-            total += self.a_in[...].astype(jnp.float32)
+        total = self.buf[pl.ds(self.level_rows(0, self.p.z), 48), pl.ds(self.mine, self.half)]
+        total = total.astype(jnp.float32)
+        for step in (1, 3, 2):
+            self.z_copy(step).wait_recv()
+            total += self.z_in[(3 - step) * 48 : (4 - step) * 48, :].astype(jnp.float32)
         self.last[...] = total
         self.end_copy().start()
         self.share[:, pl.ds(self.mine, self.half)] = self.last[
@@ -679,7 +662,6 @@
         ]
 
     def finish(self):
-        z = self.p.z
         theirs = self.share.at[:, pl.ds(self.theirs, self.half)]
         remote(theirs, theirs, self.end.at[0], self.end.at[1], self.p.sibling).wait_recv()
         self.end_copy().wait_send()
@@ -687,11 +669,8 @@
         self.pair_copy().wait_send()
         for da in range(2):
             self.b_copy(da).wait_send()
-        for da in range(self.sides):
-            for number in range(3):
-                up, down = self.z_copy(da, 3 - number, 1), self.z_copy(da, number, 0)
-                pl.when(z < 3 - number)(lambda up=up: up.wait_send())
-                pl.when(z > number)(lambda down=down: down.wait_send())
+        for step in range(1, 4):
+            self.z_copy(step).wait_send()
 
 
 class Links:
@@ -711,16 +690,9 @@
         out += [(now, section.pairs_far), (now + 0.5, section.pairs_near)]
         now = self.use("flat", now + 0.5, 1.01 * size)
         out.append((now, section.blocks))
-        if not section.z_first:
-            now = self.use("flat", now, 0.5 * size)
-            out.append((now, section.joined))
-        for slot in range(4):
-            out.append((now, functools.partial(section.levels, slot)))
-            if slot < 3:
-                now = self.use("high", now, 0.2525 * section.sides * size)
-        if section.z_first:
-            out.append((now, section.across))
-            now = self.use("flat", now, 0.13 * size)
+        now = self.use("flat", now, 0.5 * size)
+        out.append((now, section.joined))
+        now = self.use("high", now, 1.01 * size)
         out.append((now, section.close))
         return out
 
@@ -1146,10 +1118,9 @@
             after()
         self.norm_back(self.y, None, 2, self.y, self.f)
 
-    def down_back(self, plan=None):
-        self.turn(self.f)
-
-        def body(index):
+    def down_back(self, start, tiles, plan=None):
+        def body(step):
+            index = start + step
             here = columns(index)
             grad = dot(self.f[...], self.w[:, columns(index, COL_DOWN)])
             self.gp[:, here] = (grad * self.gp[:, here].astype(jnp.float32)).astype(jnp.bfloat16)
@@ -1157,14 +1128,19 @@
                 jnp.bfloat16
             )
 
-        loop(12, body, plan)
+        loop(tiles, body, plan)
 
     def up_input(self, plan=None):
         self.input_grad(self.gp, COL_UP, FF, plan)
 
-    def up_weight(self, plan=None):
-        self.turn(self.h2)
-        self.weight_grad(COL_UP, self.gp, 12, plan)
+    def up_weight(self, start, tiles, plan=None):
+        def body(step):
+            index = start + step
+            self.w[:, columns(index, COL_UP)] = dot(
+                self.turned[...], self.gp[:, columns(index)]
+            ).astype(jnp.bfloat16)
+
+        loop(tiles, body, plan)
 
     def up_norm(self):
         self.norm_back(self.r, self.y, 1, self.r, self.f)
@@ -1386,24 +1362,23 @@
         copy.wait_send()
 
     sections = []
-    for number, (first, width, z_first) in enumerate(SCATTER_SECTIONS):
+    for number, (first, width) in enumerate(SCATTER_SECTIONS):
         half = width // 2
-        rest = (number - 3) * 640
-        bufs = (
-            (pair_b if number in (1, 3, 4) else pair_a).at[
-                :, (half if number == 4 else 0) : (2 * half if number == 4 else half)
-            ],
-            b_in[number] if number < 3 else t.g.at[0:384, rest : rest + half],
-            z_in[number]
-            if number < 2
-            else (t.gp.at[:, 0:half] if number == 2 else t.g.at[0:288, 1280 + rest : 1280 + rest + half]),
-            a_in[number] if number < 3 else t.g.at[384:576, rest : rest + half],
-            last[number],
-        )
+        which, at = PAIR_PLACES[number]
+        pair_in = (pair_a, pair_b)[which].at[:, at : at + half]
+        if number < 4:
+            others = (b_in[number], a_in[number], z_in[number])
+        else:
+            here = slice(LATE_PLACES[number - 4], LATE_PLACES[number - 4] + half)
+            others = (
+                t.g.at[0:384, here],
+                t.g.at[384:576, here],
+                t.gp.at[0:144, here],
+            )
+        bufs = (pair_in, *others, last[number])
         sections.append(
-            Scatter(p, t.w, share, first, width, z_first, bufs, [s.at[number] for s in scatter_s])
-        )
-    pool_part, down_part, up_part, front_part, end_part = sections
+            Scatter(p, t.w, share, first, width, bufs, [s.at[number] for s in scatter_s])
+        )
 
     def small_begin():
         swap.finish()
@@ -1415,47 +1390,54 @@
     def leaves(section, number):
         timed.append((section, program.now, SCATTER_SECTIONS[number][1]))
 
-    leaves(pool_part, 0)
+    leaves(sections[0], 0)
     program.want(zip((0.5, 1.5, 4.5, 7.0, 9.5, 12.0), [small_begin] + small_steps[1:]))
-    program.gap(2.0)
-    program.loop("down", 12, 0.75)
-    leaves(down_part, 1)
+    program.gap(2.5)
+    program.loop("down_first", 6, 0.75)
+    leaves(sections[1], 1)
+    program.loop("down_second", 6, 0.75)
+    leaves(sections[2], 2)
     program.loop("up_input", 3, 1.4)
-    program.loop("up_weight", 12, 0.46)
+    program.gap(0.5)
+    program.loop("up_first", 6, 0.46)
+    leaves(sections[3], 3)
+    program.loop("up_second", 6, 0.46)
     program.gap(1.7)
+    leaves(sections[4], 4)
     program.loop("out", 3, 1.1)
-    leaves(up_part, 2)
+    leaves(sections[5], 5)
     program.loop("attend", 6, 2.05)
     program.gap(1.0)
     program.loop("project_input", 3, 1.0)
     program.gap(2.2)
     program.loop("front", 5, 0.5)
-    leaves(front_part, 3)
+    leaves(sections[6], 6)
     program.loop("end", 4, 0.5)
     program.gap(1.0)
-    leaves(end_part, 4)
+    leaves(sections[7], 7)
     for entry in timed:
         program.want(links.steps(*entry))
     program.settle()
     plans = program.plans
-    t.pool_back(None, pool_part.begin)
-    t.down_back(plans["down"])
-    down_part.begin()
+    t.pool_back(None, sections[0].begin)
+    t.turn(t.f)
+    t.down_back(0, 6, plans["down_first"])
+    sections[1].begin()
+    t.down_back(6, 6, plans["down_second"])
+    sections[2].begin()
     t.up_input(plans["up_input"])
-    t.up_weight(plans["up_weight"])
-    near = (p.z < 3).astype(jnp.int32) + (p.z > 0).astype(jnp.int32)
-    for device in (p.sibling, p.a_near, p.b_near):
+    t.turn(t.h2)
+    t.up_weight(0, 6, plans["up_first"])
+    sections[3].begin()
+    t.up_weight(6, 6, plans["up_second"])
+    levels = [p.on_level(lax.rem(p.z + step, 4)) for step in range(1, 4)]
+    for device in (p.sibling, p.a_near, p.b_near, *levels):
         pl.semaphore_signal(grant, inc=1, device_id=device, device_id_type=MESH)
-    pl.when(p.z < 3)(
-        lambda: pl.semaphore_signal(grant, inc=1, device_id=p.up, device_id_type=MESH)
-    )
-    pl.when(p.z > 0)(
-        lambda: pl.semaphore_signal(grant, inc=1, device_id=p.down, device_id_type=MESH)
-    )
     t.up_norm()
+    pl.semaphore_wait(grant, 6)
+    sections[4].begin()
     t.out_back(plans["out"])
-    pl.semaphore_wait(grant, 3 + near)
-    up_part.begin()
+    sections[5].begin()
     t.attend_back(plans["attend"])
     t.project_input(plans["project_input"])
     patch_copies = []
@@ -1476,10 +1458,10 @@
     )
     own_patch.start()
     t.project_weight(0, 5, plans["front"])
-    front_part.begin()
+    sections[6].begin()
     t.project_weight(5, 4, plans["end"])
     t.vectors_back()
-    end_part.begin()
+    sections[7].begin()
     for step in program.tail:
         step()
     for section in sections:
@@ -1582,11 +1564,11 @@
             vm(8, D, dt=f32),
             vm(48, GATHER_COLS // 2, dt=f32),
             vm(256, D, dt=f32),
-            vm(D, widths[2]),
-            vm(D, widths[1]),
-            [vm(384, w) for w in widths[:3]],
-            [vm(576, widths[0]), vm(288, widths[1])],
-            [vm(48, widths[0]), vm(192, widths[1]), vm(48, widths[2])],
+            vm(D, 1920),
+            vm(D, 1536),
+            [vm(384, w) for w in widths[:4]],
+            [vm(144, w) for w in widths[:4]],
+            [vm(192, w) for w in widths[:4]],
             [vm(48, w, dt=f32) for w in widths],
             vm(8, 128, dt=f32),
             vm(31, 8, 128, dt=f32),
@@ -1607,9 +1589,8 @@
             *gather_sems(gathers),
             dma((count, 2)),
             dma((count, 2, 2)),
-            dma((count, 2, 2, 3)),
-            dma((count, 2, 2, 3)),
             dma((count, 2)),
+            dma((count, 2, 3)),
             dma((count, 2)),
         ],
         compiler_params=pltpu.CompilerParams(

time: 273 us -> 253 us (0.927)
  Pallas kernels: 257 us -> 237 us
    pallas_call x1, Pallas kernels: 257 us -> 237 us  [layer_call(): pl.pallas_call(layer_kernel, out_shape=(jax.ShapeDtypeStruct((24, 8 * D +...]
where the time goes in v4:
time: 253 us; the launch traced here: 252 us
  Pallas kernels  237 us (94%)
  other arithmetic  8.36 us (3%)
  local copies, waits for them, and re-layouts  5.5 us (2%)
    pallas_call x1, Pallas kernels, layer_call(): pl.pallas_call(layer_kernel, out_shape=(jax.ShapeDtypeStruct((24, 8 * D +...  237 us

profile of v4, /device:TPU:0, one launch (start us, length us, event | category | flops | bytes accessed | tf_op | source)
XLA Modules:
  0.0 252.4 jit_solution(6054657224367483583)
XLA Ops:
  0.6 0.0 copy-start.2
  0.7 0.0 copy-start.3
  0.7 1.4 copy.35.vectors
  2.0 0.0 copy-start.1
  2.0 237.2 %layer_step.1 = (f32[24,12288]{1,0:T(8,128)}, f32[24,128]{1,0:T(8,128)}, f32[8,128]{1,0:T(8,128)}, bf16[4,144,768]{2,1,0:T(8,128)(2,1)}) custom-call(f32[24,12288]{1,0:T(8,128)} %master.1, bf16[4,144,768]{2,1,0:T(8,128)(2,1)} %tokens.1, bf16[50,768]{1,0:T(8,128)(2,1)} %captions.1, f32[24,7]{1,0:T(8,128)} %copy.35.vectors, s32[4,400]{1,0:T(4,128)} %labels.1, ...), custom_call_target="tpu_custom_call" | custom-call | tf_op jit(solution)/shard_map/layer_step/pallas_call | solution.py:1523
  239.2 1.3 fusion.10
  241.2 0.0 copy-done.2
  241.2 0.1 copy.36
  241.3 0.0 copy-done.3
  241.3 0.1 copy.38
  241.4 0.0 copy-done.1
  241.4 0.7 fusion.6
  242.1 0.7 copy.41
  242.8 0.7 copy.42
  243.4 0.7 copy.43
  244.1 0.7 copy.44
  244.8 0.0 copy-start.4
  244.8 0.0 copy-start.5
  244.8 0.0 copy-start.6
  244.8 0.0 copy-start
  244.8 5.0 %fusion.8 = (bf16[24,12288]{1,0:T(8,128)(2,1)}, f32[24,12288]{1,0:T(8,128)}, f32[24,12288]{1,0:T(8,128)}, f32[24,12288]{1,0:T(8,128)}) fusion(f32[24,12288]{1,0:T(8,128)} %master.1, f32[24,12288]{1,0:T(8,128)} %get-tuple-element.20, f32[]{:T(128)S(6)} %div.42, f32[24,12288]{1,0:T(8,128)} %param.16, f32[24,12288]{1,0:T(8,128)} %param.17), kind=kLoop, calls=%fused_computation.16 | loop fusion | flops 5013504 | bytes 8847364 | tf_op jit(solution)/shard_map/convert_element_type | solution.py:1640
  249.8 0.0 copy-done.4
  249.8 0.0 copy-done.5
  249.8 0.0 copy-done.6
  249.8 1.3 multiply_subtract_fusion.2
  251.1 0.0 copy-done
  251.1 1.4 convert_element_type.9
Async XLA Ops:
  0.6 240.5 %copy-start.2 = (f32[24,7]{0,1:T(8,128)S(1)}, f32[24,7]{0,1:T(8,128)}, u32[]{:S(2)}) copy-start(f32[24,7]{0,1:T(8,128)} %param.19) | copy-start | bytes 2020
  0.7 240.6 %copy-start.3 = (f32[24,7]{0,1:T(8,128)S(1)}, f32[24,7]{0,1:T(8,128)}, u32[]{:S(2)}) copy-start(f32[24,7]{0,1:T(8,128)} %param.20) | copy-start | bytes 2020
  2.0 239.3 %copy-start.1 = (f32[24,7]{1,0:T(8,128)S(1)}, f32[24,7]{1,0:T(8,128)}, u32[]{:S(2)}) copy-start(f32[24,7]{1,0:T(8,128)} %copy.35.vectors) | copy-start | bytes 2020
  244.8 5.0 %copy-start.4 = (f32[2]{0:T(128)S(1)}, f32[2]{0:T(128)}, u32[]{:S(2)}) copy-start(f32[2]{0:T(128)} %scalars.1) | copy-start | bytes 28
  244.8 5.0 %copy-start.5 = (f32[2]{0:T(128)S(1)}, f32[2]{0:T(128)}, u32[]{:S(2)}) copy-start(f32[2]{0:T(128)} %param.22) | copy-start | bytes 28
  244.8 5.0 %copy-start.6 = (f32[2]{0:T(128)S(1)}, f32[2]{0:T(128)}, u32[]{:S(2)}) copy-start(f32[2]{0:T(128)} %param.23) | copy-start | bytes 28
  244.8 6.3 %copy-start = (bf16[4,144,768]{2,1,0:T(8,128)(2,1)S(1)}, bf16[4,144,768]{2,1,0:T(8,128)(2,1)}, u32[]{:S(2)}) copy-start(bf16[4,144,768]{2,1,0:T(8,128)(2,1)} %get-tuple-element.19) | copy-start | bytes 2654212

commit v5 on v4

--- a/solution.py
+++ b/solution.py
@@ -358,16 +358,16 @@
 
 MESH = pl.DeviceIdType.MESH
 CHIP_ROWS = 48
-GATHER_SECTIONS = ((0, 2560), (2560, 3840), (6400, 3072), (9472, 2304))
+GATHER_SECTIONS = ((0, 2560, False), (2560, 3840, True), (6400, 3072, False), (9472, 2304, False))
 SCATTER_SECTIONS = (
-    (9472, 1536),
-    (6400, 1536),
-    (7936, 1536),
-    (3328, 1536),
-    (4864, 1536),
-    (2560, 768),
-    (0, 1280),
-    (1280, 1280),
+    (9472, 1536, False),
+    (6400, 1536, False),
+    (7936, 1536, False),
+    (3328, 1536, False),
+    (4864, 1536, False),
+    (2560, 768, False),
+    (0, 1280, False),
+    (1280, 1280, False),
 )
 PAIR_PLACES = ((0, 0), (0, 768), (1, 0), (1, 768), (0, 0), (0, 1536), (0, 768), (1, 0))
 LATE_PLACES = (0, 768, 1152, 1792)
@@ -431,12 +431,16 @@
         return carry
 
     lax.fori_loop(1, 32, greet, 0)
-    pl.semaphore_wait(barrier, 31)
+
+
+def all_greeted():
+    pl.semaphore_wait(pltpu.get_barrier_semaphore(), 31)
 
 
 class Gather:
-    def __init__(self, place, buf, rows, first, width, sems):
+    def __init__(self, place, buf, rows, first, width, z_first, sems):
         self.p, self.buf, self.rows, self.half = place, buf, rows, width // 2
+        self.z_first = z_first
         self.mine = aligned(first + place.c * self.half, 128)
         self.theirs = aligned(first + (1 - place.c) * self.half, 128)
         self.near_recv, self.z_recv, self.b_recv, self.near_send, self.z_send, self.b_send, self.pair = sems
@@ -445,9 +449,9 @@
         start = aligned((self.p.block(da, db) * 4 + level) * self.rows, self.rows)
         return self.buf.at[pl.ds(start, self.rows), pl.ds(self.mine, self.half)]
 
-    def a_copy(self):
-        own = self.item(0, 0, self.p.z)
-        return remote(own, own, self.near_send, self.near_recv, self.p.a_near)
+    def a_copy(self, level, da=0):
+        part = self.item(da, 0, level)
+        return remote(part, part, self.near_send.at[level], self.near_recv.at[level], self.p.a_near)
 
     def z_copy(self, da, level, up):
         part = self.item(da, 0, level)
@@ -458,50 +462,65 @@
         part = self.item(da, 0, level)
         return remote(part, part, self.b_send.at[da, level], self.b_recv.at[da, level], self.p.b_near)
 
-    def pair_copy(self, da, db, level):
-        part = self.item(da, db, level)
+    def pair_copy(self, da, db):
+        start = aligned(self.p.block(da, db) * (4 * self.rows), 4 * self.rows)
+        part = self.buf.at[pl.ds(start, 4 * self.rows), pl.ds(self.mine, self.half)]
         return remote(part, part, self.pair.at[0], self.pair.at[1], self.p.sibling)
 
     def onward(self, da, level, up, down):
+        if self.z_first and da == 0:
+            self.a_copy(level).start()
         self.b_copy(da, level).start()
         if up:
             pl.when(self.p.z < 3)(lambda: self.z_copy(da, level, 1).start())
         if down:
             pl.when(self.p.z > 0)(lambda: self.z_copy(da, level, 0).start())
-        self.pair_copy(da, 0, level).start()
 
     def begin(self):
-        self.a_copy().start()
+        if not self.z_first:
+            self.a_copy(self.p.z).start()
         self.onward(0, self.p.z, True, True)
 
     def near(self):
-        part = self.item(1, 0, self.p.z)
-        remote(part, part, self.near_send, self.near_recv, self.p.a_near).wait_recv()
-        self.onward(1, self.p.z, True, True)
+        z = self.p.z
+        if not self.z_first:
+            self.a_copy(z, 1).wait_recv()
+            self.onward(1, z, True, True)
+            return
+        for step in range(4):
+            level = lax.rem(z + step, 4)
+            self.a_copy(level, 1).wait_recv()
+            self.onward(1, level, False, False)
+        self.pair_copy(1, 0).start()
 
     def level(self, distance):
         z = self.p.z
+        sides = 1 if self.z_first else 2
 
         @pl.when(z >= distance)
         def from_below():
-            for da in range(2):
+            for da in range(sides):
                 self.z_copy(da, z - distance, 1).wait_recv()
                 self.onward(da, z - distance, True, False)
 
         @pl.when(z + distance <= 3)
         def from_above():
-            for da in range(2):
+            for da in range(sides):
                 self.z_copy(da, z + distance, 0).wait_recv()
                 self.onward(da, z + distance, False, True)
 
+        if distance == 3:
+            for da in range(sides):
+                self.pair_copy(da, 0).start()
+
     def far(self):
-        for level in range(4):
-            for da in range(2):
+        for da in range(2):
+            for level in range(4):
                 part = self.item(da, 1, level)
                 remote(
                     part, part, self.b_send.at[da, level], self.b_recv.at[da, level], self.p.b_near
                 ).wait_recv()
-                self.pair_copy(da, 1, level).start()
+            self.pair_copy(da, 1).start()
 
     def finish(self):
         whole = self.buf.at[pl.ds(0, 16 * self.rows), pl.ds(self.theirs, self.half)]
@@ -510,12 +529,16 @@
 
     def sent(self):
         z = self.p.z
-        self.a_copy().wait_send()
         whole = self.buf.at[pl.ds(0, 16 * self.rows), pl.ds(self.mine, self.half)]
         remote(whole, whole, self.pair.at[0], self.pair.at[1], self.p.sibling).wait_send()
+        if not self.z_first:
+            self.a_copy(z).wait_send()
         for level in range(4):
+            if self.z_first:
+                self.a_copy(level).wait_send()
             for da in range(2):
                 self.b_copy(da, level).wait_send()
+            for da in range(1 if self.z_first else 2):
                 if level < 3:
                     pl.when((z >= level) & (z < 3))(
                         lambda da=da, level=level: self.z_copy(da, level, 1).wait_send()
@@ -526,23 +549,19 @@
                     )
 
     def steps(self):
-        return [
-            self.begin,
-            self.near,
-            lambda: self.level(1),
-            lambda: self.level(2),
-            lambda: self.level(3),
-            self.far,
-        ]
+        levels = [functools.partial(self.level, distance) for distance in (1, 2, 3)]
+        if self.z_first:
+            return [self.begin, *levels, self.near, self.far]
+        return [self.begin, self.near, *levels, self.far]
 
 
 def gather_sems(count):
     dma = pltpu.SemaphoreType.DMA
     return [
-        dma((count,)),
+        dma((count, 4)),
         dma((count, 2, 4)),
         dma((count, 2, 4)),
-        dma((count,)),
+        dma((count, 4)),
         dma((count, 2, 2, 4)),
         dma((count, 2, 4)),
         dma((count, 2)),
@@ -550,8 +569,9 @@
 
 
 class Scatter:
-    def __init__(self, place, buf, share, first, width, bufs, sems):
+    def __init__(self, place, buf, share, first, width, z_first, bufs, sems):
         self.p, self.buf, self.share, self.half = place, buf, share, width // 2
+        self.z_first = z_first
         self.mine = aligned(first + place.c * self.half, 128)
         self.theirs = aligned(first + (1 - place.c) * self.half, 128)
         self.pair_in, self.b_in, self.a_in, self.z_in, self.last = bufs
@@ -600,17 +620,33 @@
         )
 
     def a_copy(self):
-        return remote(self.run(1, 0), self.a_in, self.a_sem.at[0], self.a_sem.at[1], self.p.a_near)
-
-    def z_copy(self, step):
+        source = self.part(1, self.p.z) if self.z_first else self.run(1, 0)
+        return remote(source, self.a_in, self.a_sem.at[0], self.a_sem.at[1], self.p.a_near)
+
+    def z_slot(self, da, step):
+        return slice(da * 144 + (3 - step) * 48, da * 144 + (4 - step) * 48)
+
+    def z_copy(self, da, step):
         level = lax.rem(self.p.z + step, 4)
         return remote(
-            self.part(0, level),
-            self.z_in.at[(3 - step) * 48 : (4 - step) * 48, :],
-            self.z_sem.at[0, 3 - step],
-            self.z_sem.at[1, 3 - step],
+            self.part(da, level),
+            self.z_in.at[self.z_slot(da, step), :],
+            self.z_sem.at[0, da, 3 - step],
+            self.z_sem.at[1, da, 3 - step],
             self.p.on_level(level),
         )
+
+    def z_start(self, da):
+        for step in (2, 1, 3):
+            self.z_copy(da, step).start()
+
+    def z_total(self, da):
+        total = self.buf[pl.ds(self.level_rows(da, self.p.z), 48), pl.ds(self.mine, self.half)]
+        total = total.astype(jnp.float32)
+        for step in (1, 3, 2):
+            self.z_copy(da, step).wait_recv()
+            total += self.z_in[self.z_slot(da, step), :].astype(jnp.float32)
+        return total
 
     def end_copy(self):
         return remote(
@@ -640,21 +676,27 @@
         for da in (1, 0):
             self.b_copy(da).wait_recv()
             self.add(self.run_rows(da, 0), self.b_in, 4, da * 192)
-            if da == 1:
+            if self.z_first:
+                self.z_start(da)
+            elif da == 1:
                 self.a_copy().start()
 
     def joined(self):
-        self.a_copy().wait_recv()
-        self.add(self.run_rows(0, 0), self.a_in, 4)
-        for step in (2, 1, 3):
-            self.z_copy(step).start()
+        if self.z_first:
+            self.buf[pl.ds(self.level_rows(1, self.p.z), 48), pl.ds(self.mine, self.half)] = (
+                self.z_total(1).astype(jnp.bfloat16)
+            )
+            self.a_copy().start()
+        else:
+            self.a_copy().wait_recv()
+            self.add(self.run_rows(0, 0), self.a_in, 4)
+            self.z_start(0)
 
     def close(self):
-        total = self.buf[pl.ds(self.level_rows(0, self.p.z), 48), pl.ds(self.mine, self.half)]
-        total = total.astype(jnp.float32)
-        for step in (1, 3, 2):
-            self.z_copy(step).wait_recv()
-            total += self.z_in[(3 - step) * 48 : (4 - step) * 48, :].astype(jnp.float32)
+        total = self.z_total(0)
+        if self.z_first:
+            self.a_copy().wait_recv()
+            total += self.a_in[...].astype(jnp.float32)
         self.last[...] = total
         self.end_copy().start()
         self.share[:, pl.ds(self.mine, self.half)] = self.last[
@@ -669,8 +711,9 @@
         self.pair_copy().wait_send()
         for da in range(2):
             self.b_copy(da).wait_send()
-        for step in range(1, 4):
-            self.z_copy(step).wait_send()
+        for da in range(2 if self.z_first else 1):
+            for step in range(1, 4):
+                self.z_copy(da, step).wait_send()
 
 
 class Links:
@@ -690,10 +733,15 @@
         out += [(now, section.pairs_far), (now + 0.5, section.pairs_near)]
         now = self.use("flat", now + 0.5, 1.01 * size)
         out.append((now, section.blocks))
-        now = self.use("flat", now, 0.5 * size)
-        out.append((now, section.joined))
-        now = self.use("high", now, 1.01 * size)
-        out.append((now, section.close))
+        if section.z_first:
+            now = self.use("high", now, 2.02 * size)
+            out.append((now, section.joined))
+            now = self.use("flat", now, 0.13 * size)
+        else:
+            now = self.use("flat", now, 0.5 * size)
+            out.append((now, section.joined))
+            now = self.use("high", now, 1.01 * size)
+        out += [(now, section.close), (now + 4.0, section.finish)]
         return out
 
 
@@ -801,9 +849,9 @@
 
         lax.fori_loop(1, 32, start, 0)
 
-    def finish(self):
+    def finish(self, small):
+        scalars = jnp.sum(small[...].reshape(32, 8, 768), axis=0)[3:4]
         lane = lax.broadcasted_iota(jnp.int32, (1, 768), 1)
-        scalars = self.sums
         square = jnp.sum(jnp.where((lane == 1) | (lane == 2), scalars * scalars, 0.0))
         return scalars, jnp.sqrt(self.total() + square)
 
@@ -814,11 +862,11 @@
         return self.mine[...] + jnp.sum(self.everyone[...], axis=0)
 
 
-def small_tail(p, small, map_q, probe, share, spread, map_out_ref, map_q_ref):
+def small_tail(p, small, map_q, probe, map_out_ref, map_q_ref):
     everything = small[...]
     as_rows = everything.astype(jnp.bfloat16)
     sums = jnp.sum(everything.reshape(32, 8, 768), axis=0)
-    query, scalars = sums[2:3], sums[3:4]
+    query = sums[2:3]
     device = lax.broadcasted_iota(jnp.int32, (32, 256), 0) * 8
     row = lax.broadcasted_iota(jnp.int32, (32, 256), 1)
 
@@ -843,16 +891,16 @@
         + jnp.sum(map_q_share * map_q_share)
         + jnp.sum(probe_share * probe_share)
     )
-
+    map_out_ref[...], map_q_ref[...] = map_out, map_q_share
+    return probe_share, square
+
+
+def square_share(share, square, start, stop):
     def one(step, total):
         part = share[:, pl.ds(aligned(step * 256, 256), 256)]
         return total + jnp.sum(part * part)
 
-    square = lax.fori_loop(0, SCATTER_COLS // 256, one, square)
-    spread.begin(jnp.full((8, 128), square, jnp.float32))
-    spread.sums = scalars
-    map_out_ref[...], map_q_ref[...] = map_out, map_q_share
-    return probe_share
+    return lax.fori_loop(start, stop, one, square)
 
 
 COL_VECTORS = 2304
@@ -1240,21 +1288,10 @@
     map_q_copy.start()
     greet_all(p)
 
-    count = len(GATHER_SECTIONS)
-    gathers, swaps = [], []
-    pieces = (
-        (master, 0, 0, 3 * D),
-        (extra, 0, 3 * D, 256),
-        (master, 3 * D, COL_OUT, D + 2 * FF),
-        (master, map_q_at + D, COL_MAP_KV, 3 * D),
-    )
-    for number, (first, width) in enumerate(GATHER_SECTIONS):
-        swaps.append(
-            Swap(p, pieces, stage, 0, 24, first, width, first // 2, swap_sems.at[number])
-        )
-        swaps[-1].begin((extra, False))
-        gathers.append(Gather(p, t.w, CHIP_ROWS, first, width, [s.at[number] for s in gather_s]))
-    own_vectors = vectors[...].astype(jnp.bfloat16).astype(jnp.float32)
+    own_vectors = jnp.transpose(
+        jnp.concatenate([vectors[...], jnp.zeros((121, 24), jnp.float32)], axis=0)
+    )
+    own_vectors = own_vectors.astype(jnp.bfloat16).astype(jnp.float32)
     map_q_copy.wait()
     map_q[...] = map_q[...].astype(jnp.bfloat16).astype(jnp.float32)
     part = jnp.sum(own_vectors[:, 6:7] * map_q[...], axis=0, keepdims=True)
@@ -1264,18 +1301,42 @@
         extra[side : side + 1, 128:256] = high[:, lanes]
         extra[6 + side : 7 + side, 128:256] = (part - high)[:, lanes]
     extra[12:24, 128:256] = jnp.zeros((12, 128), jnp.float32)
-    extra[:, 0:128] = jnp.concatenate([own_vectors, jnp.zeros((24, 121), jnp.float32)], axis=1)
-    swaps[0].begin((extra, True))
+    extra[:, 0:128] = own_vectors
     each = captions.shape[0]
     caps[...] = jnp.concatenate(
         [unit_rows(captions[...].astype(jnp.float32)), jnp.zeros((64 - each, D), jnp.float32)], axis=0
     ).astype(jnp.bfloat16)
+    slot = lax.broadcasted_iota(jnp.int32, (8 * each, 512), 1)
+    within = (slot >> 7) * 16 + (slot & 15)
+    source = ((slot >> 5) & 3) * (2 * each) + ((slot >> 4) & 1) * each + within
+    label = lax.broadcasted_iota(jnp.int32, (8 * each, 512), 0)
+    pick = ((label == source) & (within < each)).astype(jnp.float32).astype(jnp.bfloat16)
+    row = 2.0 * labels[pl.ds(p.blk, 1), :].astype(jnp.float32) - 1.0
+    signs[...] = dot(jnp.broadcast_to(row, (16, 8 * each)).astype(jnp.bfloat16), pick)
+    all_greeted()
+
+    count = len(GATHER_SECTIONS)
+    gathers, swaps = [], []
+    pieces = (
+        (master, 0, 0, 3 * D),
+        (extra, 0, 3 * D, 256),
+        (master, 3 * D, COL_OUT, D + 2 * FF),
+        (master, map_q_at + D, COL_MAP_KV, 3 * D),
+    )
+    for number, (first, width, z_first) in enumerate(GATHER_SECTIONS):
+        swaps.append(
+            Swap(p, pieces, stage, 0, 24, first, width, first // 2, swap_sems.at[number])
+        )
+        swaps[-1].begin()
+        gathers.append(
+            Gather(p, t.w, CHIP_ROWS, first, width, z_first, [s.at[number] for s in gather_s])
+        )
     own_caps = caps.at[pl.ds(aligned(p.blk * 16, 16), 16), :]
     swaps.append(
         Swap(p, ((own_caps, 0, 0, D),), t.cap, p.chip * 32, 16, 0, D, None, swap_sems.at[count])
     )
     swaps[-1].begin()
-    gathers.append(Gather(p, t.cap, 32, 0, D, [s.at[count] for s in gather_s]))
+    gathers.append(Gather(p, t.cap, 32, 0, D, True, [s.at[count] for s in gather_s]))
     token_copies = []
     for step in range(1, 4):
         to = lax.rem(p.blk + step, 4)
@@ -1297,7 +1358,7 @@
     def ready(number):
         swaps[number].finish()
         if number < count:
-            first, width = GATHER_SECTIONS[number]
+            first, width, _ = GATHER_SECTIONS[number]
             t.w[
                 pl.ds(aligned(p.chip * 48, 48), 48), pl.ds(gathers[number].mine, width // 2)
             ] = stage[:, first // 2 : first // 2 + width // 2].astype(jnp.bfloat16)
@@ -1319,13 +1380,6 @@
 
     for entry in order[: ends[0] + 1]:
         entry[3]()
-    slot = lax.broadcasted_iota(jnp.int32, (8 * each, 512), 1)
-    within = (slot >> 7) * 16 + (slot & 15)
-    source = ((slot >> 5) & 3) * (2 * each) + ((slot >> 4) & 1) * each + within
-    label = lax.broadcasted_iota(jnp.int32, (8 * each, 512), 0)
-    pick = ((label == source) & (within < each)).astype(jnp.float32).astype(jnp.bfloat16)
-    row = 2.0 * labels[pl.ds(p.blk, 1), :].astype(jnp.float32) - 1.0
-    signs[...] = dot(jnp.broadcast_to(row, (16, 8 * each)).astype(jnp.bfloat16), pick)
     for step in range(3):
         source = lax.rem(p.blk + 3 - step, 4)
         landed = t.x.at[pl.ds(aligned(source * 144, 144), 144), :]
@@ -1354,15 +1408,12 @@
         p, ((t.small_own, 0, 0, D),), small, p.chip * 16, 8, 0, D, None, swap_sems.at[count + 1]
     )
     swap.begin()
-    small_gather = Gather(p, small, 16, 0, D, [s.at[count + 1] for s in gather_s])
+    small_gather = Gather(p, small, 16, 0, D, True, [s.at[count + 1] for s in gather_s])
     small_steps = small_gather.steps()
-    for gather in gathers:
-        gather.sent()
-    for copy in token_copies:
-        copy.wait_send()
+    gathers[3].sent()
 
     sections = []
-    for number, (first, width) in enumerate(SCATTER_SECTIONS):
+    for number, (first, width, z_first) in enumerate(SCATTER_SECTIONS):
         half = width // 2
         which, at = PAIR_PLACES[number]
         pair_in = (pair_a, pair_b)[which].at[:, at : at + half]
@@ -1372,12 +1423,12 @@
             here = slice(LATE_PLACES[number - 4], LATE_PLACES[number - 4] + half)
             others = (
                 t.g.at[0:384, here],
-                t.g.at[384:576, here],
-                t.gp.at[0:144, here],
+                t.g.at[384 : 432 if z_first else 576, here],
+                t.gp.at[0 : 288 if z_first else 144, here],
             )
         bufs = (pair_in, *others, last[number])
         sections.append(
-            Scatter(p, t.w, share, first, width, bufs, [s.at[number] for s in scatter_s])
+            Scatter(p, t.w, share, first, width, z_first, bufs, [s.at[number] for s in scatter_s])
         )
 
     def small_begin():
@@ -1421,12 +1472,14 @@
     plans = program.plans
     t.pool_back(None, sections[0].begin)
     t.turn(t.f)
+    gathers[2].sent()
     t.down_back(0, 6, plans["down_first"])
     sections[1].begin()
     t.down_back(6, 6, plans["down_second"])
     sections[2].begin()
     t.up_input(plans["up_input"])
     t.turn(t.h2)
+    gathers[1].sent()
     t.up_weight(0, 6, plans["up_first"])
     sections[3].begin()
     t.up_weight(6, 6, plans["up_second"])
@@ -1457,33 +1510,30 @@
         t.h.at[pl.ds(aligned(p.blk * 144, 144), 144), :], patch_out.at[p.blk], patch_sems.at[0, 3]
     )
     own_patch.start()
+    gathers[0].sent()
     t.project_weight(0, 5, plans["front"])
     sections[6].begin()
     t.project_weight(5, 4, plans["end"])
     t.vectors_back()
     sections[7].begin()
-    for step in program.tail:
-        step()
-    for section in sections:
-        section.finish()
+    small_gather.finish()
+    probe_share, square = small_tail(
+        p, small, map_q[...], own_vectors[:, 6:7], map_out, map_q_share
+    )
+    small_gather.sent()
+    gathers[4].sent()
+    for copy in token_copies:
+        copy.wait_send()
     outs = [
-        pltpu.make_async_copy(
-            share.at[:, source : source + width],
-            share_out.at[:, target : target + width],
-            own_sems.at[1 + number],
-        )
-        for number, (source, target, width) in enumerate(
-            (
-                (0, 0, 3 * D),
-                (COL_OUT, 3 * D, D + 2 * FF),
-                (COL_MAP_KV, map_q_at + D, 2 * D),
-            )
+        pltpu.make_async_copy(source, share_out.at[:, target : target + D], own_sems.at[4 + number])
+        for number, (source, target) in enumerate(
+            ((map_q_share, map_q_at), (map_out, map_q_at + 3 * D))
         )
     ]
     for out in outs:
         out.start()
-    small_gather.finish()
-    small_gather.sent()
+    for step in program.tail[:-2]:
+        step()
     for step, copy in enumerate(patch_copies):
         source = lax.rem(p.blk + 3 - step, 4)
         landed = patch_out.at[source]
@@ -1492,18 +1542,27 @@
         ).wait_recv()
         copy.wait_send()
     own_patch.wait()
+    square = square_share(share, square, COL_OUT // 256, SCATTER_COLS // 256)
+    for step in program.tail[-2:]:
+        step()
     spread = Spread(p, mine, everyone, send_sem, recv_sem)
-    tail = small_tail(p, small, map_q[...], own_vectors[:, 6:7], share, spread, map_out, map_q_share)
-    for number, (source, target) in enumerate(((map_q_share, map_q_at), (map_out, map_q_at + 3 * D))):
+    spread.begin(jnp.full((8, 128), square_share(share, square, 0, COL_OUT // 256), jnp.float32))
+    for number, (source, target, width) in enumerate(
+        ((0, 0, 3 * D), (COL_OUT, 3 * D, D + 2 * FF), (COL_MAP_KV, map_q_at + D, 2 * D))
+    ):
         outs.append(
             pltpu.make_async_copy(
-                source, share_out.at[:, target : target + D], own_sems.at[4 + number]
+                share.at[:, source : source + width],
+                share_out.at[:, target : target + width],
+                own_sems.at[1 + number],
             )
         )
         outs[-1].start()
     lane = lax.broadcasted_iota(jnp.int32, (24, 128), 1)
-    vector_out[...] = jnp.where(lane == 6, tail, share[:, COL_VECTORS : COL_VECTORS + 128])
-    sums, norm = spread.finish()
+    vector_out[...] = jnp.transpose(
+        jnp.where(lane == 6, probe_share, share[:, COL_VECTORS : COL_VECTORS + 128])
+    )[0:8]
+    sums, norm = spread.finish(small)
     facts[...] = jnp.concatenate([jnp.broadcast_to(sums[:, :128], (7, 128)), norm[:1]], axis=0)
     for out in outs:
         out.wait()
@@ -1524,7 +1583,7 @@
         layer_kernel,
         out_shape=(
             jax.ShapeDtypeStruct((24, 8 * D + 2 * FF), f32),
-            jax.ShapeDtypeStruct((24, 128), f32),
+            jax.ShapeDtypeStruct((8, 24), f32),
             jax.ShapeDtypeStruct((8, 128), f32),
             jax.ShapeDtypeStruct((4, 144, D), jnp.bfloat16),
         ),
@@ -1567,8 +1626,8 @@
             vm(D, 1920),
             vm(D, 1536),
             [vm(384, w) for w in widths[:4]],
-            [vm(144, w) for w in widths[:4]],
-            [vm(192, w) for w in widths[:4]],
+            [vm(288 if entry[2] else 144, entry[1] // 2) for entry in SCATTER_SECTIONS[:4]],
+            [vm(48 if entry[2] else 192, entry[1] // 2) for entry in SCATTER_SECTIONS[:4]],
             [vm(48, w, dt=f32) for w in widths],
             vm(8, 128, dt=f32),
             vm(31, 8, 128, dt=f32),
@@ -1590,7 +1649,7 @@
             dma((count, 2)),
             dma((count, 2, 2)),
             dma((count, 2)),
-            dma((count, 2, 3)),
+            dma((count, 2, 2, 3)),
             dma((count, 2)),
         ],
         compiler_params=pltpu.CompilerParams(
@@ -1615,9 +1674,9 @@
     scalar_second,
 ):
     weight_share, vector_share, facts, patch_grad = layer_call(
-        master_weights, patch_tokens, captions, master_vectors, pair_labels, loss_scalars
-    )
-    vector_share = vector_share[:, :7]
+        master_weights, patch_tokens, captions, master_vectors.T, pair_labels, loss_scalars
+    )
+    vector_share = vector_share[:7].T
     patch_grad = patch_grad.astype(jnp.float32)
     loss_total, scalar_total, grad_norm = facts[0, 0], facts[0, 1:3], facts[7, 0]
     factor = CLIP_AT / jnp.maximum(grad_norm, CLIP_AT)

time: 253 us -> 242 us (0.957)
  Pallas kernels: 237 us -> 231 us
  local copies, waits for them, and re-layouts: 5.5 us -> 1.31 us
    pallas_call x1, Pallas kernels: 237 us -> 231 us  [layer_call(): pl.pallas_call(layer_kernel, out_shape=(jax.ShapeDtypeStruct((24, 8 * D +...]
    unnamed x21 -> x16, local copies, waits for them, and re-layouts: 4.24 us -> 0.05 us
where the time goes in v5:
time: 242 us
  Pallas kernels  231 us (95%)
  other arithmetic  8.26 us (3%)
    pallas_call x1, Pallas kernels, layer_call(): pl.pallas_call(layer_kernel, out_shape=(jax.ShapeDtypeStruct((24, 8 * D +...  231 us
    convert_element_type x1, other arithmetic, local_kernel(): new_w.astype(jnp.bfloat16)  5 us

profile of v5, /device:TPU:0, one launch (start us, length us, event | category | flops | bytes accessed | tf_op | source)
XLA Modules:
  0.0 241.7 jit_solution(12601945927103535350)
XLA Ops:
  0.6 230.7 %layer_step.1 = (f32[24,12288]{1,0:T(8,128)}, f32[8,24]{1,0:T(8,128)}, f32[8,128]{1,0:T(8,128)}, bf16[4,144,768]{2,1,0:T(8,128)(2,1)}) custom-call(f32[24,12288]{1,0:T(8,128)} %master.1, bf16[4,144,768]{2,1,0:T(8,128)(2,1)} %tokens.1, bf16[50,768]{1,0:T(8,128)(2,1)} %captions.1, f32[7,24]{1,0:T(8,128)} %bitcast.17, s32[4,400]{1,0:T(4,128)} %labels.1, f32[2]{0:T(128)} %scalars.1), custom_call_target="tpu_custom_call" | custom-call | tf_op jit(solution)/shard_map/layer_step/pallas_call | solution.py:1582
  231.4 1.3 fusion.12
  233.3 0.0 copy-start.1
  233.3 0.0 copy-start.2
  233.3 0.0 copy-start.3
  233.4 0.0 copy-start.4
  233.4 0.0 copy-start.5
  233.4 0.0 copy-start.6
  233.4 0.0 copy-start.7
  233.4 0.0 copy-start
  233.4 5.0 %fusion.10 = (bf16[24,12288]{1,0:T(8,128)(2,1)}, f32[24,12288]{1,0:T(8,128)}, f32[24,12288]{1,0:T(8,128)}, f32[24,12288]{1,0:T(8,128)}) fusion(f32[24,12288]{1,0:T(8,128)} %master.1, f32[24,12288]{1,0:T(8,128)} %get-tuple-element.20, f32[]{:T(128)S(6)} %div.42, f32[24,12288]{1,0:T(8,128)} %param.16, f32[24,12288]{1,0:T(8,128)} %param.17), kind=kLoop, calls=%fused_computation.17 | loop fusion | flops 5013504 | bytes 8847364 | tf_op jit(solution)/shard_map/convert_element_type | solution.py:1699
  238.4 0.0 copy-done.1
  238.4 0.0 copy-done.2
  238.4 0.0 copy-done.3
  238.4 0.0 copy-done.4
  238.4 0.6 fusion.7
  239.1 0.0 copy-done.5
  239.1 0.0 copy-done.6
  239.1 0.0 copy-done.7
  239.1 1.3 multiply_subtract_fusion.2
  240.3 0.0 copy-done
  240.3 1.4 convert_element_type.9
Async XLA Ops:
  233.3 5.1 %copy-start.1 = (f32[24,7]{0,1:T(8,128)S(1)}, f32[24,7]{0,1:T(8,128)}, u32[]{:S(2)}) copy-start(f32[24,7]{0,1:T(8,128)} %param.18) | copy-start | bytes 2020
  233.3 5.1 %copy-start.2 = (f32[24,7]{0,1:T(8,128)S(1)}, f32[24,7]{0,1:T(8,128)}, u32[]{:S(2)}) copy-start(f32[24,7]{0,1:T(8,128)} %param.19) | copy-start | bytes 2020
  233.3 5.1 %copy-start.3 = (f32[24,7]{0,1:T(8,128)S(1)}, f32[24,7]{0,1:T(8,128)}, u32[]{:S(2)}) copy-start(f32[24,7]{0,1:T(8,128)} %param.20) | copy-start | bytes 2020
  233.4 5.1 %copy-start.4 = (f32[8,24]{1,0:T(8,128)S(1)}, f32[8,24]{1,0:T(8,128)}, u32[]{:S(2)}) copy-start(f32[8,24]{1,0:T(8,128)} %get-tuple-element.21) | copy-start | bytes 2308
  233.4 5.7 %copy-start.5 = (f32[2]{0:T(128)S(1)}, f32[2]{0:T(128)}, u32[]{:S(2)}) copy-start(f32[2]{0:T(128)} %scalars.1) | copy-start | bytes 28
  233.4 5.7 %copy-start.6 = (f32[2]{0:T(128)S(1)}, f32[2]{0:T(128)}, u32[]{:S(2)}) copy-start(f32[2]{0:T(128)} %param.22) | copy-start | bytes 28
  233.4 5.7 %copy-start.7 = (f32[2]{0:T(128)S(1)}, f32[2]{0:T(128)}, u32[]{:S(2)}) copy-start(f32[2]{0:T(128)} %param.23) | copy-start | bytes 28
  233.4 7.0 %copy-start = (bf16[4,144,768]{2,1,0:T(8,128)(2,1)S(1)}, bf16[4,144,768]{2,1,0:T(8,128)(2,1)}, u32[]{:S(2)}) copy-start(bf16[4,144,768]{2,1,0:T(8,128)(2,1)} %get-tuple-element.19) | copy-start | bytes 2654212

commit v6 on v5

--- a/solution.py
+++ b/solution.py
@@ -349,7 +349,7 @@
     )
 
 
-LINK_SPEED = (1.1, 3.0)
+LINK_SPEED = (1.1, 4.0)
 
 
 def gather_key(number, at):

time: 242 us -> 240 us (level)
  no operation moved by 1% of the time
where the time goes in v6:
time: 240 us
  Pallas kernels  229 us (95%)
  other arithmetic  8.26 us (3%)
    pallas_call x1, Pallas kernels, layer_call(): pl.pallas_call(layer_kernel, out_shape=(jax.ShapeDtypeStruct((24, 8 * D +...  229 us
    convert_element_type x1, other arithmetic, local_kernel(): new_w.astype(jnp.bfloat16)  5 us

profile of v6, /device:TPU:0, one launch (start us, length us, event | category | flops | bytes accessed | tf_op | source)
XLA Modules:
  0.0 239.5 jit_solution(12962931229370514470)
XLA Ops:
  0.6 228.5 %layer_step.1 = (f32[24,12288]{1,0:T(8,128)}, f32[8,24]{1,0:T(8,128)}, f32[8,128]{1,0:T(8,128)}, bf16[4,144,768]{2,1,0:T(8,128)(2,1)}) custom-call(f32[24,12288]{1,0:T(8,128)} %master.1, bf16[4,144,768]{2,1,0:T(8,128)(2,1)} %tokens.1, bf16[50,768]{1,0:T(8,128)(2,1)} %captions.1, f32[7,24]{1,0:T(8,128)} %bitcast.17, s32[4,400]{1,0:T(4,128)} %labels.1, f32[2]{0:T(128)} %scalars.1), custom_call_target="tpu_custom_call" | custom-call | tf_op jit(solution)/shard_map/layer_step/pallas_call | solution.py:1582
  229.2 1.3 fusion.12
  231.2 0.0 copy-start.1
  231.2 0.0 copy-start.2
  231.2 0.0 copy-start.3
  231.2 0.0 copy-start.4
  231.2 0.0 copy-start.5
  231.2 0.0 copy-start.6
  231.2 0.0 copy-start.7
  231.2 0.0 copy-start
  231.2 5.0 %fusion.10 = (bf16[24,12288]{1,0:T(8,128)(2,1)}, f32[24,12288]{1,0:T(8,128)}, f32[24,12288]{1,0:T(8,128)}, f32[24,12288]{1,0:T(8,128)}) fusion(f32[24,12288]{1,0:T(8,128)} %master.1, f32[24,12288]{1,0:T(8,128)} %get-tuple-element.20, f32[]{:T(128)S(6)} %div.42, f32[24,12288]{1,0:T(8,128)} %param.16, f32[24,12288]{1,0:T(8,128)} %param.17), kind=kLoop, calls=%fused_computation.17 | loop fusion | flops 5013504 | bytes 8847364 | tf_op jit(solution)/shard_map/convert_element_type | solution.py:1699
  236.2 0.0 copy-done.1
  236.2 0.0 copy-done.2
  236.2 0.0 copy-done.3
  236.3 0.0 copy-done.4
  236.3 0.6 fusion.7
  236.9 0.0 copy-done.5
  236.9 0.0 copy-done.6
  236.9 0.0 copy-done.7
  236.9 1.3 multiply_subtract_fusion.2
  238.2 0.0 copy-done
  238.2 1.4 convert_element_type.9
Async XLA Ops:
  231.2 5.1 %copy-start.1 = (f32[24,7]{0,1:T(8,128)S(1)}, f32[24,7]{0,1:T(8,128)}, u32[]{:S(2)}) copy-start(f32[24,7]{0,1:T(8,128)} %param.18) | copy-start | bytes 2020
  231.2 5.1 %copy-start.2 = (f32[24,7]{0,1:T(8,128)S(1)}, f32[24,7]{0,1:T(8,128)}, u32[]{:S(2)}) copy-start(f32[24,7]{0,1:T(8,128)} %param.19) | copy-start | bytes 2020
  231.2 5.1 %copy-start.3 = (f32[24,7]{0,1:T(8,128)S(1)}, f32[24,7]{0,1:T(8,128)}, u32[]{:S(2)}) copy-start(f32[24,7]{0,1:T(8,128)} %param.20) | copy-start | bytes 2020
  231.2 5.1 %copy-start.4 = (f32[8,24]{1,0:T(8,128)S(1)}, f32[8,24]{1,0:T(8,128)}, u32[]{:S(2)}) copy-start(f32[8,24]{1,0:T(8,128)} %get-tuple-element.21) | copy-start | bytes 2308
  231.2 5.7 %copy-start.5 = (f32[2]{0:T(128)S(1)}, f32[2]{0:T(128)}, u32[]{:S(2)}) copy-start(f32[2]{0:T(128)} %scalars.1) | copy-start | bytes 28
  231.2 5.7 %copy-start.6 = (f32[2]{0:T(128)S(1)}, f32[2]{0:T(128)}, u32[]{:S(2)}) copy-start(f32[2]{0:T(128)} %param.22) | copy-start | bytes 28
  231.2 5.7 %copy-start.7 = (f32[2]{0:T(128)S(1)}, f32[2]{0:T(128)}, u32[]{:S(2)}) copy-start(f32[2]{0:T(128)} %param.23) | copy-start | bytes 28
  231.2 7.0 %copy-start = (bf16[4,144,768]{2,1,0:T(8,128)(2,1)S(1)}, bf16[4,144,768]{2,1,0:T(8,128)(2,1)}, u32[]{:S(2)}) copy-start(bf16[4,144,768]{2,1,0:T(8,128)(2,1)} %get-tuple-element.19) | copy-start | bytes 2654212

commit v7 on v6

--- a/solution.py
+++ b/solution.py
@@ -349,7 +349,7 @@
     )
 
 
-LINK_SPEED = (1.1, 4.0)
+LINK_SPEED = (1.1, 5.0)
 
 
 def gather_key(number, at):

time: 240 us -> 242 us (level)
  no operation moved by 1% of the time
where the time goes in v7:
time: 242 us
  Pallas kernels  231 us (95%)
  other arithmetic  8.26 us (3%)
    pallas_call x1, Pallas kernels, layer_call(): pl.pallas_call(layer_kernel, out_shape=(jax.ShapeDtypeStruct((24, 8 * D +...  231 us
    convert_element_type x1, other arithmetic, local_kernel(): new_w.astype(jnp.bfloat16)  5 us

profile of v7, /device:TPU:0, one launch (start us, length us, event | category | flops | bytes accessed | tf_op | source)
XLA Modules:
  0.0 242.0 jit_solution(4783700700317169785)
XLA Ops:
  0.6 231.0 %layer_step.1 = (f32[24,12288]{1,0:T(8,128)}, f32[8,24]{1,0:T(8,128)}, f32[8,128]{1,0:T(8,128)}, bf16[4,144,768]{2,1,0:T(8,128)(2,1)}) custom-call(f32[24,12288]{1,0:T(8,128)} %master.1, bf16[4,144,768]{2,1,0:T(8,128)(2,1)} %tokens.1, bf16[50,768]{1,0:T(8,128)(2,1)} %captions.1, f32[7,24]{1,0:T(8,128)} %bitcast.17, s32[4,400]{1,0:T(4,128)} %labels.1, f32[2]{0:T(128)} %scalars.1), custom_call_target="tpu_custom_call" | custom-call | tf_op jit(solution)/shard_map/layer_step/pallas_call | solution.py:1582
  231.6 1.3 fusion.12
  233.6 0.0 copy-start.1
  233.6 0.0 copy-start.2
  233.6 0.0 copy-start.3
  233.6 0.0 copy-start.4
  233.6 0.0 copy-start.5
  233.6 0.0 copy-start.6
  233.6 0.0 copy-start.7
  233.7 0.0 copy-start
  233.7 5.0 %fusion.10 = (bf16[24,12288]{1,0:T(8,128)(2,1)}, f32[24,12288]{1,0:T(8,128)}, f32[24,12288]{1,0:T(8,128)}, f32[24,12288]{1,0:T(8,128)}) fusion(f32[24,12288]{1,0:T(8,128)} %master.1, f32[24,12288]{1,0:T(8,128)} %get-tuple-element.20, f32[]{:T(128)S(6)} %div.42, f32[24,12288]{1,0:T(8,128)} %param.16, f32[24,12288]{1,0:T(8,128)} %param.17), kind=kLoop, calls=%fused_computation.17 | loop fusion | flops 5013504 | bytes 8847364 | tf_op jit(solution)/shard_map/convert_element_type | solution.py:1699
  238.7 0.0 copy-done.1
  238.7 0.0 copy-done.2
  238.7 0.0 copy-done.3
  238.7 0.0 copy-done.4
  238.7 0.6 fusion.7
  239.3 0.0 copy-done.5
  239.3 0.0 copy-done.6
  239.3 0.0 copy-done.7
  239.3 1.3 multiply_subtract_fusion.2
  240.6 0.0 copy-done
  240.6 1.4 convert_element_type.9
Async XLA Ops:
  233.6 5.1 %copy-start.1 = (f32[24,7]{0,1:T(8,128)S(1)}, f32[24,7]{0,1:T(8,128)}, u32[]{:S(2)}) copy-start(f32[24,7]{0,1:T(8,128)} %param.18) | copy-start | bytes 2020
  233.6 5.1 %copy-start.2 = (f32[24,7]{0,1:T(8,128)S(1)}, f32[24,7]{0,1:T(8,128)}, u32[]{:S(2)}) copy-start(f32[24,7]{0,1:T(8,128)} %param.19) | copy-start | bytes 2020
  233.6 5.1 %copy-start.3 = (f32[24,7]{0,1:T(8,128)S(1)}, f32[24,7]{0,1:T(8,128)}, u32[]{:S(2)}) copy-start(f32[24,7]{0,1:T(8,128)} %param.20) | copy-start | bytes 2020
  233.6 5.1 %copy-start.4 = (f32[8,24]{1,0:T(8,128)S(1)}, f32[8,24]{1,0:T(8,128)}, u32[]{:S(2)}) copy-start(f32[8,24]{1,0:T(8,128)} %get-tuple-element.21) | copy-start | bytes 2308
  233.6 5.7 %copy-start.5 = (f32[2]{0:T(128)S(1)}, f32[2]{0:T(128)}, u32[]{:S(2)}) copy-start(f32[2]{0:T(128)} %scalars.1) | copy-start | bytes 28
  233.6 5.7 %copy-start.6 = (f32[2]{0:T(128)S(1)}, f32[2]{0:T(128)}, u32[]{:S(2)}) copy-start(f32[2]{0:T(128)} %param.22) | copy-start | bytes 28
  233.6 5.7 %copy-start.7 = (f32[2]{0:T(128)S(1)}, f32[2]{0:T(128)}, u32[]{:S(2)}) copy-start(f32[2]{0:T(128)} %param.23) | copy-start | bytes 28
  233.7 7.0 %copy-start = (bf16[4,144,768]{2,1,0:T(8,128)(2,1)S(1)}, bf16[4,144,768]{2,1,0:T(8,128)(2,1)}, u32[]{:S(2)}) copy-start(bf16[4,144,768]{2,1,0:T(8,128)(2,1)} %get-tuple-element.19) | copy-start | bytes 2654212
